TPU v7x, 256 devices: a whole 4x4x8 slice. The times are simulated.
256 devices in a mesh: blk: 32 (over z, x_lo, core), group: 8 (over y, x_hi).
Axes of the slice: x: 4 (x_hi: 2, x_lo: 2; x = x_hi * 2 + x_lo), y: 4, z: 8, core: 2. Of those that a mesh axis runs over, the one named last changes fastest.
Arguments:
- image: float32 [16384, 1024], P('blk'), may hold values from -8 to 8
- text: float32 [16384, 1024], P(('blk', 'group')), may hold values from -8 to 8
Outputs:
- grad_image: float32 [16384, 1024], P('blk')
- grad_text: float32 [16384, 1024], P(('blk', 'group'))
All inputs are finite; a program needn't handle non-finite values.
Results may differ from a plain program's by a relative error of at most 0.0003.
Values sent between devices are 32-bit elements; how exact they have to be, the bound alone decides.
No kernel may reach another device: no remote copies, remote signals or barrier semaphores. Data moves between devices by JAX's collectives and lax.ppermute only.
A program may use at most 64 MiB of HBM per device.

v0:
```python
import jax
import jax.numpy as jnp
from jax import lax
from jax.sharding import PartitionSpec as P

PRECISE = lax.Precision.HIGHEST


def similarity(piece, image):
    return jnp.einsum(
        "td,id->ti", piece, image, precision=PRECISE, preferred_element_type=jnp.float32
    )


def stats_from(carry, scores):
    row_high, row_sums, column_high, column_sums = carry
    new_high = jnp.max(scores, axis=0)
    row_sums = row_sums * jnp.exp(row_high - new_high) + jnp.sum(
        jnp.exp(scores - new_high[None, :]), axis=0
    )
    piece_high = jnp.max(scores, axis=1)
    piece_sums = jnp.sum(jnp.exp(scores - piece_high[:, None]), axis=1)
    column_high = piece_high
    column_sums = piece_sums
    return (new_high, row_sums, column_high, column_sums)


def local(image, text):
    text_rows = text.shape[0]
    image_rows, width = image.shape
    columns = text_rows * lax.axis_size("blk")
    my_blk = lax.axis_index("blk")
    my_group = lax.axis_index("group")
    start_stats = (
        jnp.full((image_rows,), -jnp.inf, jnp.float32),
        jnp.zeros((image_rows,), jnp.float32),
        jnp.full((columns,), -jnp.inf, jnp.float32),
        jnp.zeros((columns,), jnp.float32),
    )
    row_high, row_sums, column_high, column_sums = stats_from(
        start_stats, similarity(lax.all_gather(text, "blk", axis=0, tiled=True), image)
    )
    row_top = lax.pmax(row_high, "group")
    row_sums = lax.psum(row_sums * jnp.exp(row_high - row_top), "group")
    column_top = lax.pmax(column_high, "blk")
    column_sums = lax.psum(column_sums * jnp.exp(column_high - column_top), "blk")
    row_high = row_top
    column_high = column_top
    row_level = row_high + jnp.log(row_sums)
    column_level = column_high + jnp.log(column_sums)
    image_index = jnp.arange(image_rows, dtype=jnp.int32)
    piece = lax.all_gather(text, "blk", axis=0, tiled=True)
    scores = similarity(piece, image)
    number = scores.shape[0]
    position = jnp.arange(number, dtype=jnp.int32)
    owner_match = position // text_rows == my_blk
    partner = my_group * text_rows + position % text_rows
    same_pair = owner_match[:, None] & (partner[:, None] == image_index[None, :])
    factors = (
        0.5 * jnp.exp(scores - row_level[None, :])
        + 0.5 * jnp.exp(scores - column_level[:, None])
        - same_pair.astype(jnp.float32)
    )
    grad_sum = jnp.einsum(
        "ti,td->id", factors, piece, precision=PRECISE, preferred_element_type=jnp.float32
    )
    product = jnp.einsum(
        "ti,id->td", factors, image, precision=PRECISE, preferred_element_type=jnp.float32
    )
    text_sums = product
    grad_local, text_sums = (grad_sum, text_sums)
    grad_text = lax.psum_scatter(text_sums, "blk", scatter_dimension=0, tiled=True)
    grad_image = lax.psum(grad_local, "group")
    return (grad_image, grad_text)


def solution(mesh):
    placed = (P("blk", None), P(("blk", "group"), None))
    return jax.shard_map(
        local,
        mesh=mesh,
        in_specs=placed,
        out_specs=(P("blk", None), P(("blk", "group"), None)),
        check_vma=False,
    )
```

profile of v0, /device:TPU:2, one launch (start us, length us, event | category | flops | bytes accessed | tf_op | source)
XLA Modules:
  0.0 526.1 jit_solution(7916439804410938649)
XLA Ops:
  7.2 0.0 copy-start
  7.2 0.0 all-gather.2.cloned.1.call-start
  7.2 0.7 all-gather.2.cloned.1.call-update
  7.9 0.0 all-reduce.2.cloned.1.call-start
  8.0 77.1 %all-gather.2.cloned.1.call-done = f32[2048,1024]{1,0:T(8,128)} async-done(((f32[64,1024]{1,0:T(8,128)}), f32[2048,1024]{1,0:T(8,128)}) %all-gather.2.cloned.1.call-update) | async-done | bytes 8388624 | tf_op jit(solution)/shard_map/all_gather | solution.py:52
  85.1 0.0 copy-done
  85.1 17.0 %fusion.12 = (f32[512]{0:T(512)S(1)}, f32[2048]{0:T(1024)S(1)}, f32[2048,512]{1,0:T(8,128)}) fusion(f32[2048,1024]{1,0:T(8,128)} %all-gather.2.cloned.1.call-done, f32[512,1024]{1,0:T(8,128)S(1)} %copy-done), kind=kOutput, calls=%fused_computation.24 | convolution fusion | flops 12886996992 | bytes 14690304 | tf_op jit(solution)/shard_map/td,id->ti/dot_general | solution.py:10
  102.1 23.3 %pmax.14 = f32[512]{0:T(512)S(1)} all-reduce(f32[512]{0:T(512)S(1)} %get-tuple-element.4), channel_id=1, replica_groups=mesh['blk'=32,'group'=8] {'group'}, use_global_device_ids=true, to_apply=%region_1.0 | all-reduce | flops 512 | bytes 4096 | tf_op jit(solution)/shard_map/pmax | solution.py:43
  125.4 51.1 %pmax.15 = f32[2048]{0:T(1024)S(1)} all-reduce(f32[2048]{0:T(1024)S(1)} %get-tuple-element.5), channel_id=1, replica_groups=mesh['blk'=32,'group'=8] {'blk'}, use_global_device_ids=true, to_apply=%region_5.0 | all-reduce | flops 2048 | bytes 16384 | tf_op jit(solution)/shard_map/pmax | solution.py:45
  176.5 3.2 exponential_reduce_fusion.1
  179.7 19.0 %psum.21 = f32[512]{0:T(512)S(1)} all-reduce(f32[512]{0:T(512)S(1)} %exponential_multiply_fusion.1), channel_id=1, replica_groups=mesh['blk'=32,'group'=8] {'group'}, use_global_device_ids=true, to_apply=%region_3.0 | all-reduce | flops 512 | bytes 4096 | tf_op jit(solution)/shard_map/psum | solution.py:44
  198.7 54.2 %psum.22 = f32[2048]{0:T(1024)S(1)} all-reduce(f32[2048]{0:T(1024)S(1)} %exponential_multiply_fusion), channel_id=1, replica_groups=mesh['blk'=32,'group'=8] {'blk'}, use_global_device_ids=true, to_apply=%region_7.0 | all-reduce | flops 2048 | bytes 16384 | tf_op jit(solution)/shard_map/psum | solution.py:46
  252.9 21.0 %fusion.11 = f32[512,1024]{1,0:T(8,128)} fusion(f32[2048,1024]{1,0:T(8,128)} %all-gather.2.cloned.1.call-done, f32[2048,512]{1,0:T(8,128)} %get-tuple-element.6, s32[2048]{0:T(1024)S(1)} %fusion.8, f32[2048]{0:T(1024)S(1)} %log_add_fusion, f32[512]{0:T(512)S(1)} %log_add_fusion.1, pred[2048]{0:T(1024)(128)(4,1)S(1)} %fusion.7), kind=kOutput, calls=%fused_computation.23 | convolution fusion | flops 12893290496 | bytes 14700544 | tf_op jit(solution)/shard_map/ti,td->id/dot_general | solution.py:64
  273.9 0.0 all-reduce.2.cloned.1.call-update
  273.9 0.0 reduce-scatter.2.cloned.1.call-start
  274.0 18.8 %fusion.10 = f32[2048,1024]{1,0:T(8,128)} fusion(f32[512,1024]{1,0:T(8,128)S(1)} %copy-done, f32[2048,512]{1,0:T(8,128)} %get-tuple-element.6, s32[2048]{0:T(1024)S(1)} %fusion.8, f32[2048]{0:T(1024)S(1)} %log_add_fusion, f32[512]{0:T(512)S(1)} %log_add_fusion.1, pred[2048]{0:T(1024)(128)(4,1)S(1)} %fusion.7), kind=kOutput, calls=%fused_computation.22 | convolution fusion | flops 12893290496 | bytes 14700544 | tf_op jit(solution)/shard_map/ti,id->td/dot_general | solution.py:67
  292.8 0.0 reduce-scatter.2.cloned.1.call-update
  292.8 94.1 %all-reduce.2.cloned.1.call-done = f32[512,1024]{1,0:T(8,128)} async-done(((f32[512,1024]{1,0:T(8,128)}), f32[512,1024]{1,0:T(8,128)}) %all-reduce.2.cloned.1.call-update) | async-done | bytes 2097168 | tf_op jit(solution)/shard_map/psum | solution.py:73
  386.9 129.5 %reduce-scatter.2.cloned.1.call-done = f32[64,1024]{1,0:T(8,128)} async-done(((f32[2048,1024]{1,0:T(8,128)}), f32[64,1024]{1,0:T(8,128)}) %reduce-scatter.2.cloned.1.call-update) | async-done | bytes 262160 | tf_op jit(solution)/shard_map/reduce_scatter | solution.py:72
  516.4 3.2 copy.5
  (6 shorter events, 0.1 us)
Async XLA Ops:
  7.2 78.0 %copy-start = (f32[512,1024]{1,0:T(8,128)S(1)}, f32[512,1024]{1,0:T(8,128)}, u32[]{:S(2)}) copy-start(f32[512,1024]{1,0:T(8,128)} %param.2) | copy-start | bytes 6291460
  7.2 77.9 %all-gather.2.cloned.1.call-start = ((), (), s32[]{:S(2)}) async-start(), calls=%async_computation.1 | async-start | bytes 8650752 | tf_op jit(solution)/shard_map/all_gather | solution.py:52
  7.9 379.0 %all-reduce.2.cloned.1.call-start = ((), (), s32[]{:S(2)}) async-start(), calls=%async_computation.2 | async-start | bytes 4194304 | tf_op jit(solution)/shard_map/psum | solution.py:73
  273.9 242.4 %reduce-scatter.2.cloned.1.call-start = ((), (), s32[]{:S(2)}) async-start(), calls=%async_computation.3 | async-start | bytes 8650752 | tf_op jit(solution)/shard_map/reduce_scatter | solution.py:72
Sparse Core Ops, SparseCore 0:
  9.9 75.1 all-gather.1
  274.1 112.7 all-reduce.1
  390.0 126.3 reduce-scatter.1
where the time goes:
time: 530 us; the launch traced here: 526 us
  waiting for transfers between devices  301 us (57%)
  blocking collectives  148 us (28%)
  matrix products  56.8 us (11%)
  between operations  13.8 us (3%)
    reduce_scatter x1, waiting for transfers between devices, local(): lax.psum_scatter(text_sums, 'blk', scatter_dimension=0, tiled=True)  129 us
    psum x1, waiting for transfers between devices, local(): grad_image = lax.psum(grad_local, 'group')  94.1 us
    all_gather x1, waiting for transfers between devices, local(): piece = lax.all_gather(text, 'blk', axis=0, tiled=True)  77.1 us
    psum x1, blocking collectives, local(): lax.psum(column_sums * jnp.exp(column_high - column_top), 'blk')  54.2 us
    pmax x1, blocking collectives, local(): column_top = lax.pmax(column_high, 'blk')  51.1 us
    pmax x1, blocking collectives, local(): row_top = lax.pmax(row_high, 'group')  23.3 us
    dot_general x1, matrix products, local(): jnp.einsum('ti,td->id', factors, piece, precision=PRECISE, preferred_elem...  21 us
    psum x1, blocking collectives, local(): row_sums = lax.psum(row_sums * jnp.exp(row_high - row_top), 'group')  19 us
  transfers between devices with their start and end apart: 3, of which 3 were waited for; matrix products, arithmetic and copies ran while one was open for 4% of the time, Pallas kernels for 0%

commit v1 on v0

v1 whole, which is shorter than its diff:
```python
import jax
import jax.numpy as jnp
from jax import lax
from jax.sharding import Mesh, PartitionSpec as P

FULL = lax.Precision.HIGHEST
THREE = lax.Precision.HIGH
ORDER = (0, 1, 7, 2, 6, 3, 5, 4)
PLACE = tuple(ORDER.index(k) for k in range(8))


def x_other():
    pairs = []
    for x in range(4):
        t = (x - 1) % 4 if x % 2 == 0 else (x + 1) % 4
        pairs.append(((x % 2) * 2 + x // 2, (t % 2) * 2 + t // 2))
    return pairs


def join_levels(levels):
    top = jnp.max(levels, axis=0)
    return top + jnp.log(jnp.sum(jnp.exp(levels - top[None]), axis=0))


def swap_core(a):
    return lax.ppermute(a, "core", [(0, 1), (1, 0)])


def swap_x(near, far):
    return (
        lax.ppermute(near, "xl", [(0, 1), (1, 0)]),
        lax.ppermute(far, ("xl", "xh"), x_other()),
    )


def local(image, text):
    rows, width = image.shape
    part = text.shape[0]
    z, xl, core = (lax.axis_index(a) for a in ("z", "xl", "core"))
    group = lax.axis_index("y") * 2 + lax.axis_index("xh")
    half = rows // 2

    chunks = {0: text}
    for k in (1, 7, 2, 6, 3, 5, 4):
        chunks[k] = lax.ppermute(text, "z", [(i, (i + k) % 8) for i in range(8)])
    near, far = swap_x(image[:half], image[half:])
    both = jnp.concatenate([image, near, far], axis=0)

    texts, scores = [], []
    for b in range(2):
        mine = jnp.concatenate([chunks[k] for k in ORDER[4 * b : 4 * b + 4]], axis=0)
        texts.append(jnp.concatenate([mine, swap_core(mine)], axis=0))
        scores.append(
            jnp.einsum("id,td->it", both, texts[b], precision=FULL, preferred_element_type=jnp.float32)
        )
    scores = jnp.concatenate(scores, axis=1)
    piece = jnp.concatenate(texts, axis=0)

    row_top = jnp.max(scores, axis=1)
    row_part = row_top + jnp.log(jnp.sum(jnp.exp(scores - row_top[:, None]), axis=1))
    col_top = jnp.max(scores, axis=0)
    col_part = col_top + jnp.log(jnp.sum(jnp.exp(scores - col_top[None, :]), axis=0))

    r = row_part.reshape(2, rows)
    r = jnp.where(xl == 0, r, r[::-1])
    r = jnp.broadcast_to(r.reshape(1, -1), (16, 2 * rows))
    r = join_levels(lax.all_to_all(r, ("xl", "y", "xh"), 0, 0, tiled=True)).reshape(2, rows)
    row_level = jnp.where(xl == 0, r, r[::-1]).reshape(-1)

    c = col_part.reshape(2, 2, 4, part).transpose(1, 0, 2, 3).reshape(2, 8, part)
    c = jnp.where(core == 0, c, c[::-1])[:, jnp.array(PLACE), :]
    turn = (z - jnp.arange(8)) % 8
    c = jnp.take(c, turn, axis=1)
    c = jnp.broadcast_to(c.reshape(1, -1), (16, 16 * part))
    c = join_levels(lax.all_to_all(c, ("z", "core"), 0, 0, tiled=True)).reshape(2, 8, part)
    c = jnp.take(c, turn, axis=1)[:, jnp.array(ORDER), :]
    c = jnp.where(core == 0, c, c[::-1])
    col_level = c.reshape(2, 2, 4, part).transpose(1, 0, 2, 3).reshape(-1)

    i = jnp.arange(2 * rows)[:, None]
    j = jnp.arange(16 * part)[None, :]
    same = (j < part) & (i == group * part + j)
    weights = (
        0.5 * jnp.exp(scores - row_level[:, None])
        + 0.5 * jnp.exp(scores - col_level[None, :])
        - same.astype(jnp.float32)
    )

    def times_text(w):
        return jnp.einsum("it,td->id", w, piece, precision=THREE, preferred_element_type=jnp.float32)

    away = times_text(weights[rows:])
    got = swap_x(away[:half], away[half:])
    g_text = jnp.einsum("it,id->td", weights, both, precision=THREE, preferred_element_type=jnp.float32)
    home = times_text(weights[:rows])

    g_text = g_text.reshape(2, 2, 4 * part, width)
    g_text = g_text[:, 0] + swap_core(g_text[:, 1])
    g_text = g_text.reshape(8, part, width)
    g_text = jnp.concatenate(
        [
            lax.dynamic_index_in_dim(g_text, jnp.array(PLACE)[(z - zz) % 8], 0)
            for zz in range(8)
        ],
        axis=0,
    ).reshape(8 * part, width)
    grad_text = lax.psum_scatter(g_text, "z", scatter_dimension=0, tiled=True)

    home = home + jnp.concatenate(got, axis=0)
    home = lax.all_to_all(home.reshape(8, part, width), ("y", "xh"), 0, 0, tiled=True)
    mine = jnp.sum(home.reshape(8, part, width), axis=0)
    out = jnp.broadcast_to(mine[None], (8, part, width))
    out = lax.all_to_all(out, ("y", "xh"), 0, 0, tiled=True)
    return out.reshape(rows, width), grad_text


def solution(mesh):
    fine = Mesh(mesh.devices.reshape(8, 2, 2, 4, 2), ("z", "xl", "core", "y", "xh"))
    blk = ("z", "xl", "core")
    placed = (P(blk, None), P(blk + ("y", "xh"), None))
    return jax.shard_map(local, mesh=fine, in_specs=placed, out_specs=placed, check_vma=False)
```

time: 530 us -> 266 us (0.50)
  waiting for transfers between devices: 301 us -> 57.2 us
  blocking collectives: 148 us -> 60.1 us
  starting transfers between devices: 0.12 us -> 41.4 us
  local copies, waits for them, and re-layouts: 3.17 us -> 22.6 us
  between operations: 13.8 us -> 29.7 us
  matrix products: 56.8 us -> 45.4 us
  other arithmetic: 3.22 us -> 9.34 us
    reduce_scatter x1, waiting for transfers between devices: 129 us -> 0.01 us  [local(): grad_text = lax.psum_scatter(g_text, 'z', scatter_dimension=0, tiled=True)]
    psum x1 -> x0, waiting for transfers between devices: 94.1 us -> none  [local(): grad_image = lax.psum(grad_local, 'group')]
    all_gather x1 -> x0, waiting for transfers between devices: 77.1 us -> none  [local(): piece = lax.all_gather(text, 'blk', axis=0, tiled=True)]
    pmax x2 -> x0, blocking collectives: 74.3 us -> none  [the longest x1 51.1 us: local(): column_top = lax.pmax(column_high, 'blk')]
    psum x2 -> x0, blocking collectives: 73.2 us -> none  [the longest x1 54.2 us: local(): lax.psum(column_sums * jnp.exp(column_high - column_top), 'blk')]
    all_to_all x0 -> x2, blocking collectives: none -> 60.1 us  [the longest x1 31 us: local(): lax.all_to_all(home.reshape(8, part, width), ('y', 'xh'), 0, 0, tiled=True)]
    ppermute x0 -> x14, waiting for transfers between devices: none -> 44.6 us  [the longest x7 22 us: local(): chunks[k] = lax.ppermute(text, 'z', [(i, (i + k) % 8) for i in range(8)])]
    ppermute x0 -> x14, starting transfers between devices: none -> 25.9 us  [the longest x7 20.9 us: local(): chunks[k] = lax.ppermute(text, 'z', [(i, (i + k) % 8) for i in range(8)])]
  transfers between devices with their start and end apart: 3 -> 17, of which waited for: 3 -> 8; matrix products, arithmetic and copies ran while one was open for 4% -> 11% of each run, Pallas kernels for 0% -> 0%
where the time goes in v1:
time: 266 us
  blocking collectives  60.1 us (23%)
  waiting for transfers between devices  57.2 us (22%)
  matrix products  45.4 us (17%)
  starting transfers between devices  41.4 us (16%)
  between operations  29.7 us (11%)
  local copies, waits for them, and re-layouts  22.6 us (8%)
  other arithmetic  9.34 us (4%)
    all_to_all x1, blocking collectives, local(): lax.all_to_all(home.reshape(8, part, width), ('y', 'xh'), 0, 0, tiled=True)  31 us
    all_to_all x1, blocking collectives, local(): out = lax.all_to_all(out, ('y', 'xh'), 0, 0, tiled=True)  29.2 us
    dot_general x2, matrix products, local(): jnp.einsum('id,td->it', both, texts[b], precision=FULL, preferred_element...  25.8 us
    ppermute x7, waiting for transfers between devices, local(): chunks[k] = lax.ppermute(text, 'z', [(i, (i + k) % 8) for i in range(8)])  22 us
    ppermute x2, waiting for transfers between devices, swap_x(): lax.ppermute(near, 'xl', [(0, 1), (1, 0)])  21.2 us
    ppermute x7, starting transfers between devices, local(): chunks[k] = lax.ppermute(text, 'z', [(i, (i + k) % 8) for i in range(8)])  20.9 us
    dot_general x2, matrix products, times_text(): jnp.einsum('it,td->id', w, piece, precision=THREE, preferred_element_type...  12.8 us
    unnamed x52, local copies, waits for them, and re-layouts  10.3 us
  transfers between devices with their start and end apart: 17, of which 8 were waited for; matrix products, arithmetic and copies ran while one was open for 11% of the time, Pallas kernels for 0%

profile of v1, /device:TPU:2, one launch (start us, length us, event | category | flops | bytes accessed | tf_op | source)
XLA Modules:
  0.0 265.7 jit_solution(15889987438268447013)
XLA Ops:
  7.2 2.0 collective-permute-start.2
  9.2 4.0 %collective-permute-start.3 = (f32[64,1024]{1,0:T(8,128)}, f32[64,1024]{1,0:T(8,128)}, u32[]{:S(2)}, u32[]{:S(2)}) collective-permute-start(f32[64,1024]{1,0:T(8,128)} %param.15), channel_id=1, source_target_pairs={{0,224},{32,0},{64,32},{96,64},{128,96},{160,128},{192,160},{224,1... | collective-permute-start | bytes 786440 | tf_op jit(solution)/shard_map/ppermute | solution.py:45
  13.2 4.1 %collective-permute-start.6 = (f32[64,1024]{1,0:T(8,128)}, f32[64,1024]{1,0:T(8,128)}, u32[]{:S(2)}, u32[]{:S(2)}) collective-permute-start(f32[64,1024]{1,0:T(8,128)} %param.15), channel_id=1, source_target_pairs={{0,192},{32,224},{64,0},{96,32},{128,64},{160,96},{192,128},{224,1... | collective-permute-start | bytes 786440 | tf_op jit(solution)/shard_map/ppermute | solution.py:45
  17.3 0.6 collective-permute-start.7
  17.9 3.2 %fusion.15 = (f32[256,1024]{1,0:T(8,128)}, f32[256,1024]{1,0:T(8,128)}) fusion(f32[512,1024]{1,0:T(8,128)} %param.14), kind=kLoop, calls=%fused_computation.81 | loop fusion | bytes 4194304 | tf_op jit(solution)/shard_map/slice | solution.py:46
  21.1 0.8 constant_dynamic-update-slice_fusion.7
  22.0 0.7 copy-done.12
  22.7 0.5 collective-permute-start
  23.3 1.5 collective-permute-done.3
  24.8 6.3 %collective-permute-start.8 = (f32[64,1024]{1,0:T(8,128)S(1)}, f32[64,1024]{1,0:T(8,128)S(1)}, u32[]{:S(2)}, u32[]{:S(2)}) collective-permute-start(f32[64,1024]{1,0:T(8,128)S(1)} %copy-done.11), channel_id=1, source_target_pairs={{0,160},{32,192},{64,224},{96,0},{128,32},{160,64},{192,96},{224,1... | collective-permute-start | bytes 786440 | tf_op jit(solution)/shard_map/ppermute | solution.py:45
  31.0 3.7 %collective-permute-done.4 = f32[64,1024]{1,0:T(8,128)} collective-permute-done((f32[64,1024]{1,0:T(8,128)}, f32[64,1024]{1,0:T(8,128)}, u32[]{:S(2)}, u32[]{:S(2)}) %collective-permute-start.4) | collective-permute-done | bytes 262176 | tf_op jit(solution)/shard_map/ppermute | solution.py:45
  34.8 1.5 collective-permute-start.1
  36.3 1.2 pad_maximum_fusion.1
  37.5 3.9 %collective-permute-start.9 = (f32[64,1024]{1,0:T(8,128)S(1)}, f32[64,1024]{1,0:T(8,128)S(1)}, u32[]{:S(2)}, u32[]{:S(2)}) collective-permute-start(f32[64,1024]{1,0:T(8,128)S(1)} %copy-done.11), channel_id=1, source_target_pairs={{0,128},{32,160},{64,192},{96,224},{128,0},{160,32},{192,64},{224,... | collective-permute-start | bytes 786440 | tf_op jit(solution)/shard_map/ppermute | solution.py:45
  41.4 12.3 %collective-permute-done.7 = f32[64,1024]{1,0:T(8,128)} collective-permute-done((f32[64,1024]{1,0:T(8,128)}, f32[64,1024]{1,0:T(8,128)}, u32[]{:S(2)}, u32[]{:S(2)}) %collective-permute-start.7) | collective-permute-done | bytes 262176 | tf_op jit(solution)/shard_map/ppermute | solution.py:45
  53.8 0.1 constant_dynamic-update-slice_fusion.2
  53.9 4.4 %collective-permute-done.8 = f32[64,1024]{1,0:T(8,128)S(1)} collective-permute-done((f32[64,1024]{1,0:T(8,128)S(1)}, f32[64,1024]{1,0:T(8,128)S(1)}, u32[]{:S(2)}, u32[]{:S(2)}) %collective-permute-start.8) | collective-permute-done | bytes 262176 | tf_op jit(solution)/shard_map/ppermute | solution.py:45
  58.3 1.1 pad_maximum_fusion.2
  59.4 0.3 collective-permute-start.10
  59.9 1.0 constant_dynamic-update-slice_fusion.5
  60.9 1.0 constant_dynamic-update-slice_fusion.4
  62.0 0.1 constant_dynamic-update-slice_fusion
  62.1 0.2 constant_dynamic-update-slice_fusion.3
  62.4 1.2 constant_dynamic-update-slice_fusion.12
  63.6 1.0 constant_dynamic-update-slice_fusion.11
  64.7 0.2 constant_dynamic-update-slice_fusion.8
  65.0 6.8 %fusion.18 = (f32[1024]{0:T(1024)S(1)}, f32[1024,512]{0,1:T(8,128)S(1)}) fusion(f32[1024,1024]{1,0:T(8,128)S(1)} %constant_dynamic-update-slice_fusion, f32[512,1024]{1,0:T(8,128)S(1)} %get-tuple-element.9), kind=kOutput, calls=%fused_computation.84 | convolution fusion | flops 6442974208 | bytes 8392704 | tf_op jit(solution)/shard_map/id,td->it/dot_general | solution.py:54
  71.8 18.9 %fusion.17 = (f32[1024]{0:T(1024)S(1)}, f32[1024,512]{0,1:T(8,128)S(1)}) fusion(f32[1024,1024]{1,0:T(8,128)S(1)} %constant_dynamic-update-slice_fusion, f32[512,1024]{1,0:T(8,128)S(1)} %get-tuple-element.11), kind=kOutput, calls=%fused_computation.83 | convolution fusion | flops 6442974208 | bytes 8392704 | tf_op jit(solution)/shard_map/id,td->it/dot_general | solution.py:54
  90.8 0.8 exponential_reduce_fusion.1
  91.6 0.5 copy-done
  92.1 1.0 exponential_reduce_fusion
  93.2 0.1 rev.12
  93.3 0.7 broadcast_in_dim.42
  94.0 7.5 %all-to-all-start = ((f32[16,1,1024]{2,1,0:T(1,128)}), f32[16,1,1024]{2,1,0:T(1,128)S(1)}, u32[]{:S(2)}, u32[]{:S(2)}) async-start(f32[16,1,1024]{2,1,0:T(1,128)} %broadcast_in_dim.42), calls=%async_computation | async-start | bytes 131072 | tf_op jit(solution)/shard_map/all_to_all | solution.py:67
  101.6 0.6 gather_fusion
  102.2 0.6 gather_fusion.2
  102.9 5.0 %all-to-all-done = f32[16,1,1024]{2,1,0:T(1,128)S(1)} async-done(((f32[16,1,1024]{2,1,0:T(1,128)}), f32[16,1,1024]{2,1,0:T(1,128)S(1)}, u32[]{:S(2)}, u32[]{:S(2)}) %all-to-all-start) | async-done | bytes 65568 | tf_op jit(solution)/shard_map/all_to_all | solution.py:67
  107.9 0.7 broadcast_in_dim.45
  108.6 8.0 %all-to-all-start.1 = ((f32[16,1,1024]{2,1,0:T(1,128)}), f32[16,1,1024]{2,1,0:T(1,128)S(1)}, u32[]{:S(2)}, u32[]{:S(2)}) async-start(f32[16,1,1024]{2,1,0:T(1,128)} %broadcast_in_dim.45), calls=%async_computation.1 | async-start | bytes 131072 | tf_op jit(solution)/shard_map/all_to_all | solution.py:75
  116.7 0.1 rev.13
  116.9 7.5 %all-to-all-done.1 = f32[16,1,1024]{2,1,0:T(1,128)S(1)} async-done(((f32[16,1,1024]{2,1,0:T(1,128)}), f32[16,1,1024]{2,1,0:T(1,128)S(1)}, u32[]{:S(2)}, u32[]{:S(2)}) %all-to-all-start.1) | async-done | bytes 65568 | tf_op jit(solution)/shard_map/all_to_all | solution.py:75
  124.6 0.6 gather_fusion.3
  125.3 0.6 gather_fusion.1
  125.9 0.1 sub.95
  126.0 4.3 %convert_subtract_fusion = f32[1024,1024]{0,1:T(8,128)S(1)} fusion(s32[1024]{0:T(1024)S(1)} %iota_add_fusion, f32[1024]{0:T(1024)S(1)} %sub.95, f32[1024]{0:T(1024)S(1)} %bitcast.80, pred[1024]{0:T(1024)(128)(4,1)S(1)} %iota_compare_fusion.1, f32[1024,512]{0,1:T(8,128)S(1)} %get-tuple-element.40, f32[1024,512]{0,1:T(8,128)} %copy-done), kind=kLoop, calls=%fused_computation.5 | loop fusion | flops 9437184 | bytes 8401920 | tf_op jit(solution)/shard_map/sub | solution.py:84
  130.3 6.7 %fusion.19 = f32[1024,1024]{1,0:T(8,128)S(1)} fusion(f32[1024,1024]{0,1:T(8,128)S(1)} %convert_subtract_fusion, f32[1024,1024]{1,0:T(8,128)S(1)} %copy-done.2), kind=kOutput, calls=%fused_computation.85 | convolution fusion | flops 6442450944 | bytes 12582912 | tf_op jit(solution)/shard_map/it,id->td/dot_general | solution.py:94
  137.1 1.8 slice_bitcast_fusion
  138.9 0.8 copy-done.7
  139.7 0.3 collective-permute-start.13
  140.0 0.7 fusion.16
  155.6 6.2 %fusion.2 = f32[512,1024]{1,0:T(8,128)S(1)} fusion(f32[1024,1024]{1,0:T(8,128)} %copy-done.4, f32[1024,1024]{0,1:T(8,128)} %copy-done.5), kind=kOutput, calls=%fused_computation.13 | convolution fusion | flops 3221225472 | bytes 8388608 | tf_op jit(solution)/shard_map/it,td->id/dot_general | solution.py:90
  161.8 1.4 fusion.14
  163.2 1.5 collective-permute-start.11
  164.7 0.8 collective-permute-start.12
  165.5 0.4 fusion.1
  166.2 1.3 copy-done.9
  167.5 21.1 %collective-permute-done.11 = f32[256,1024]{1,0:T(8,128)S(1)} collective-permute-done((f32[256,1024]{1,0:T(8,128)}, f32[256,1024]{1,0:T(8,128)S(1)}, u32[]{:S(2)}, u32[]{:S(2)}) %collective-permute-start.11) | collective-permute-done | bytes 1048608 | tf_op jit(solution)/shard_map/ppermute | solution.py:31
  188.7 1.5 collective-permute-done.12
  190.1 6.7 %maximum_add_fusion = f32[512,1024]{1,0:T(8,128)S(1)} fusion(f32[256,1024]{1,0:T(8,128)} %collective-permute-done.12, f32[256,1024]{1,0:T(8,128)S(1)} %collective-permute-done.11, f32[1024,1024]{1,0:T(8,128)} %copy-done.4, f32[1024,1024]{0,1:T(8,128)} %copy-done.5), kind=kOutput, calls=%fused_computation.17 | convolution fusion | flops 3222274048 | bytes 10485760 | tf_op jit(solution)/shard_map/it,td->id/dot_general | solution.py:90
  196.8 31.0 %all_to_all.28 = f32[8,64,1024]{2,1,0:T(8,128)S(1)} all-to-all(f32[8,64,1024]{2,1,0:T(8,128)S(1)} %bitcast.69), channel_id=1, replica_groups=mesh['z'=8,'xl'=2,'core'=2,'y'=4,'xh'=2] {'y','xh'}, dimensions={0} | all-to-all | bytes 4194304 | tf_op jit(solution)/shard_map/all_to_all | solution.py:110
  227.8 0.1 reduce_sum.49
  227.9 0.2 broadcast_in_dim.47
  228.2 29.2 %all_to_all.29 = f32[8,64,1024]{2,1,0:T(8,128)S(1)} all-to-all(f32[8,64,1024]{2,1,0:T(8,128)S(1)} %broadcast_in_dim.47), channel_id=1, replica_groups=mesh['z'=8,'xl'=2,'core'=2,'y'=4,'xh'=2] {'y','xh'}, dimensions={0} | all-to-all | bytes 4194304 | tf_op jit(solution)/shard_map/all_to_all | solution.py:113
  257.4 1.3 copy.73
  (86 shorter events, 1.3 us)
Async XLA Ops:
  7.2 14.8 %collective-permute-start.2 = (f32[64,1024]{1,0:T(8,128)}, f32[64,1024]{1,0:T(8,128)S(1)}, u32[]{:S(2)}, u32[]{:S(2)}) collective-permute-start(f32[64,1024]{1,0:T(8,128)} %param.15), channel_id=1, source_target_pairs={{0,32},{32,64},{64,96},{96,128},{128,160},{160,192},{192,224},{224... | collective-permute-start | bytes 786440 | tf_op jit(solution)/shard_map/ppermute | solution.py:45
  9.2 15.6 %collective-permute-start.3 = (f32[64,1024]{1,0:T(8,128)}, f32[64,1024]{1,0:T(8,128)}, u32[]{:S(2)}, u32[]{:S(2)}) collective-permute-start(f32[64,1024]{1,0:T(8,128)} %param.15), channel_id=1, source_target_pairs={{0,224},{32,0},{64,32},{96,64},{128,96},{160,128},{192,160},{224,1... | collective-permute-start | bytes 786440 | tf_op jit(solution)/shard_map/ppermute | solution.py:45
  13.2 21.6 %collective-permute-start.4 = (f32[64,1024]{1,0:T(8,128)}, f32[64,1024]{1,0:T(8,128)}, u32[]{:S(2)}, u32[]{:S(2)}) collective-permute-start(f32[64,1024]{1,0:T(8,128)} %param.15), channel_id=1, source_target_pairs={{0,64},{32,96},{64,128},{96,160},{128,192},{160,224},{192,0},{224,... | collective-permute-start | bytes 786440 | tf_op jit(solution)/shard_map/ppermute | solution.py:45
  13.2 24.3 %collective-permute-start.6 = (f32[64,1024]{1,0:T(8,128)}, f32[64,1024]{1,0:T(8,128)}, u32[]{:S(2)}, u32[]{:S(2)}) collective-permute-start(f32[64,1024]{1,0:T(8,128)} %param.15), channel_id=1, source_target_pairs={{0,192},{32,224},{64,0},{96,32},{128,64},{160,96},{192,128},{224,1... | collective-permute-start | bytes 786440 | tf_op jit(solution)/shard_map/ppermute | solution.py:45
  17.3 36.4 %collective-permute-start.7 = (f32[64,1024]{1,0:T(8,128)}, f32[64,1024]{1,0:T(8,128)}, u32[]{:S(2)}, u32[]{:S(2)}) collective-permute-start(f32[64,1024]{1,0:T(8,128)} %param.15), channel_id=1, source_target_pairs={{0,96},{32,128},{64,160},{96,192},{128,224},{160,0},{192,32},{224,... | collective-permute-start | bytes 786440 | tf_op jit(solution)/shard_map/ppermute | solution.py:45
  17.9 3.2 %copy-start.14 = (s32[8]{0:T(128)S(1)}, s32[8]{0:T(128)}, u32[]{:S(2)}) copy-start(s32[8]{0:T(128)} %constant.135.clone) | copy-start | bytes 100
  17.9 3.2 %copy-start.11 = (f32[64,1024]{1,0:T(8,128)S(1)}, f32[64,1024]{1,0:T(8,128)}, u32[]{:S(2)}) copy-start(f32[64,1024]{1,0:T(8,128)} %param.15) | copy-start | bytes 786436
  17.9 5.3 %copy-start.15 = (s32[8]{0:T(128)S(1)}, s32[8]{0:T(128)}, u32[]{:S(2)}) copy-start(s32[8]{0:T(128)} %constant.147) | copy-start | bytes 100
  21.1 32.6 %copy-start.6 = (f32[512,1024]{1,0:T(8,128)S(1)}, f32[512,1024]{1,0:T(8,128)}, u32[]{:S(2)}) copy-start(f32[512,1024]{1,0:T(8,128)} %param.14) | copy-start | bytes 6291460
  22.0 0.7 copy-start.12
  22.7 39.2 %collective-permute-start = (f32[256,1024]{1,0:T(8,128)}, f32[256,1024]{1,0:T(8,128)S(1)}, u32[]{:S(2)}, u32[]{:S(2)}) collective-permute-start(f32[256,1024]{1,0:T(8,128)} %get-tuple-element.8), channel_id=1, source_target_pairs={{0,16},{16,0},{1,17},{17,1},{2,18},{18,2},{3,19},{19,3},{4,20},{20... | collective-permute-start | bytes 3145736 | tf_op jit(solution)/shard_map/ppermute | solution.py:31
  24.8 33.6 %collective-permute-start.8 = (f32[64,1024]{1,0:T(8,128)S(1)}, f32[64,1024]{1,0:T(8,128)S(1)}, u32[]{:S(2)}, u32[]{:S(2)}) collective-permute-start(f32[64,1024]{1,0:T(8,128)S(1)} %copy-done.11), channel_id=1, source_target_pairs={{0,160},{32,192},{64,224},{96,0},{128,32},{160,64},{192,96},{224,1... | collective-permute-start | bytes 786440 | tf_op jit(solution)/shard_map/ppermute | solution.py:45
  34.8 27.2 %collective-permute-start.1 = (f32[256,1024]{1,0:T(8,128)}, f32[256,1024]{1,0:T(8,128)S(1)}, u32[]{:S(2)}, u32[]{:S(2)}) collective-permute-start(f32[256,1024]{1,0:T(8,128)} %get-tuple-element.7), channel_id=1, source_target_pairs={{0,17},{16,1},{1,16},{17,0},{2,19},{18,3},{3,18},{19,2},{4,21},{20... | collective-permute-start | bytes 3145736 | tf_op jit(solution)/shard_map/ppermute | solution.py:32
  36.3 23.5 %copy-start.13 = (f32[64,1024]{1,0:T(8,128)S(1)}, f32[64,1024]{1,0:T(8,128)}, u32[]{:S(2)}) copy-start(f32[64,1024]{1,0:T(8,128)} %copy-done.12) | copy-start | bytes 786436
  37.5 20.8 %collective-permute-start.9 = (f32[64,1024]{1,0:T(8,128)S(1)}, f32[64,1024]{1,0:T(8,128)S(1)}, u32[]{:S(2)}, u32[]{:S(2)}) collective-permute-start(f32[64,1024]{1,0:T(8,128)S(1)} %copy-done.11), channel_id=1, source_target_pairs={{0,128},{32,160},{64,192},{96,224},{128,0},{160,32},{192,64},{224,... | collective-permute-start | bytes 786440 | tf_op jit(solution)/shard_map/ppermute | solution.py:45
  53.7 8.4 %collective-permute-start.5 = (f32[256,1024]{1,0:T(8,128)S(1)}, f32[256,1024]{1,0:T(8,128)S(1)}, u32[]{:S(2)}, u32[]{:S(2)}) collective-permute-start(f32[256,1024]{1,0:T(8,128)S(1)} %pad_maximum_fusion.1), channel_id=1, source_target_pairs={{0,8},{8,0},{1,9},{9,1},{2,10},{10,2},{3,11},{11,3},{4,12},{12,4},... | collective-permute-start | bytes 3145736 | tf_op jit(solution)/shard_map/ppermute | solution.py:26
  53.8 6.1 %copy-start.3 = (f32[1024,1024]{1,0:T(8,128)S(1)}, f32[1024,1024]{1,0:T(8,128)}, u32[]{:S(2)}) copy-start(f32[1024,1024]{1,0:T(8,128)} %get-tuple-element.28) | copy-start | bytes 12582916
  53.9 5.9 %copy-start.10 = (f32[512,1024]{1,0:T(8,128)S(1)}, f32[512,1024]{1,0:T(8,128)}, u32[]{:S(2)}) copy-start(f32[512,1024]{1,0:T(8,128)} %get-tuple-element.27) | copy-start | bytes 6291460
  59.4 5.3 %collective-permute-start.10 = (f32[256,1024]{1,0:T(8,128)S(1)}, f32[256,1024]{1,0:T(8,128)S(1)}, u32[]{:S(2)}, u32[]{:S(2)}) collective-permute-start(f32[256,1024]{1,0:T(8,128)S(1)} %pad_maximum_fusion.2), channel_id=1, source_target_pairs={{0,8},{8,0},{1,9},{9,1},{2,10},{10,2},{3,11},{11,3},{4,12},{12,4},... | collective-permute-start | bytes 3145736 | tf_op jit(solution)/shard_map/ppermute | solution.py:26
  62.1 9.7 %copy-start.1 = (f32[1024,1024]{1,0:T(8,128)}, f32[1024,1024]{1,0:T(8,128)S(1)}, u32[]{:S(2)}) copy-start(f32[1024,1024]{1,0:T(8,128)S(1)} %constant_dynamic-update-slice_fusion) | copy-start | bytes 12582916
  65.0 6.9 %copy-start.4 = (f32[1024,1024]{1,0:T(8,128)}, f32[1024,1024]{1,0:T(8,128)S(1)}, u32[]{:S(2)}) copy-start(f32[1024,1024]{1,0:T(8,128)S(1)} %get-tuple-element.10) | copy-start | bytes 12582916
  90.8 1.3 copy-start
  94.0 14.0 %all-to-all-start = ((f32[16,1,1024]{2,1,0:T(1,128)}), f32[16,1,1024]{2,1,0:T(1,128)S(1)}, u32[]{:S(2)}, u32[]{:S(2)}) async-start(f32[16,1,1024]{2,1,0:T(1,128)} %broadcast_in_dim.42), calls=%async_computation | async-start | bytes 131072 | tf_op jit(solution)/shard_map/all_to_all | solution.py:67
  108.6 15.8 %all-to-all-start.1 = ((f32[16,1,1024]{2,1,0:T(1,128)}), f32[16,1,1024]{2,1,0:T(1,128)S(1)}, u32[]{:S(2)}, u32[]{:S(2)}) async-start(f32[16,1,1024]{2,1,0:T(1,128)} %broadcast_in_dim.45), calls=%async_computation.1 | async-start | bytes 131072 | tf_op jit(solution)/shard_map/all_to_all | solution.py:75
  116.6 140.8 %reduce-scatter.2.cloned.1.call-start = ((), (), s32[]{:S(2)}) async-start(), calls=%async_computation.5 | async-start | bytes 2359296 | tf_op jit(solution)/shard_map/reduce_scatter | solution.py:107
  126.0 4.3 %copy-start.2 = (f32[1024,1024]{1,0:T(8,128)S(1)}, f32[1024,1024]{1,0:T(8,128)}, u32[]{:S(2)}) copy-start(f32[1024,1024]{1,0:T(8,128)} %copy-done.1) | copy-start | bytes 12582916
  130.3 6.8 %copy-start.5 = (f32[1024,1024]{0,1:T(8,128)}, f32[1024,1024]{0,1:T(8,128)S(1)}, u32[]{:S(2)}) copy-start(f32[1024,1024]{0,1:T(8,128)S(1)} %convert_subtract_fusion) | copy-start | bytes 12582916
  137.1 2.6 copy-start.7
  139.7 25.8 %collective-permute-start.13 = (f32[2,256,1024]{2,1,0:T(8,128)}, f32[2,256,1024]{2,1,0:T(8,128)S(1)}, u32[]{:S(2)}, u32[]{:S(2)}) collective-permute-start(f32[2,256,1024]{2,1,0:T(8,128)} %slice_bitcast_fusion), channel_id=1, source_target_pairs={{0,8},{8,0},{1,9},{9,1},{2,10},{10,2},{3,11},{11,3},{4,12},{12,4},... | collective-permute-start | bytes 6291464 | tf_op jit(solution)/shard_map/ppermute | solution.py:26
  161.8 3.7 %copy-start.8 = (f32[1024,1024]{1,0:T(8,128)S(1)}, f32[1024,1024]{1,0:T(8,128)}, u32[]{:S(2)}) copy-start(f32[1024,1024]{1,0:T(8,128)} %copy-done.7) | copy-start | bytes 12582916
  163.2 25.4 %collective-permute-start.11 = (f32[256,1024]{1,0:T(8,128)}, f32[256,1024]{1,0:T(8,128)S(1)}, u32[]{:S(2)}, u32[]{:S(2)}) collective-permute-start(f32[256,1024]{1,0:T(8,128)} %get-tuple-element.5), channel_id=1, source_target_pairs={{0,16},{16,0},{1,17},{17,1},{2,18},{18,2},{3,19},{19,3},{4,20},{20... | collective-permute-start | bytes 3145736 | tf_op jit(solution)/shard_map/ppermute | solution.py:31
  164.7 25.5 %collective-permute-start.12 = (f32[256,1024]{1,0:T(8,128)}, f32[256,1024]{1,0:T(8,128)}, u32[]{:S(2)}, u32[]{:S(2)}) collective-permute-start(f32[256,1024]{1,0:T(8,128)} %get-tuple-element.6), channel_id=1, source_target_pairs={{0,17},{16,1},{1,16},{17,0},{2,19},{18,3},{3,18},{19,2},{4,21},{20... | collective-permute-start | bytes 3145736 | tf_op jit(solution)/shard_map/ppermute | solution.py:32
  166.2 1.3 copy-start.9
Sparse Core Ops, SparseCore 0:
  167.6 36.4 reduce-scatter.1

commit v2 on v1

v2 whole, which is shorter than its diff:
```python
import functools

import jax
import jax.numpy as jnp
from jax import lax
from jax.experimental import pallas as pl
from jax.experimental.pallas import tpu as pltpu
from jax.sharding import Mesh, PartitionSpec as P

Z, Y = 8, 4
STEP = 256
CUTS = 8
PARTS = 2
PICK = 100_000_000
F32, BF16 = jnp.float32, jnp.bfloat16
VMEM = pl.BlockSpec(memory_space=pltpu.VMEM)
SMEM = pl.BlockSpec(memory_space=pltpu.SMEM)


def call(kernel, name, outs, n_in, scalars=False, scratch=(), cost=1000):
    in_specs = [VMEM] * n_in
    if scalars:
        in_specs = [SMEM] + in_specs
    return pl.pallas_call(
        kernel,
        out_shape=tuple(jax.ShapeDtypeStruct(s, t) for s, t in outs),
        in_specs=in_specs,
        out_specs=(VMEM,) * len(outs),
        scratch_shapes=scratch,
        compiler_params=pltpu.CompilerParams(vmem_limit_bytes=24 * 1024 * 1024),
        cost_estimate=pl.CostEstimate(flops=1000, bytes_accessed=cost, transcendentals=0),
        name=name,
    )


def grid_call(kernel, name, steps, ins, outs, scratch=(), cost=1000):
    run = pl.pallas_call(
        kernel,
        grid=(steps,),
        out_shape=tuple(pltpu.HBM(s, t) for s, t, _ in outs),
        in_specs=list(ins),
        out_specs=tuple(spec for _, _, spec in outs),
        scratch_shapes=scratch,
        compiler_params=pltpu.CompilerParams(
            vmem_limit_bytes=40 * 1024 * 1024, dimension_semantics=("arbitrary",)
        ),
        cost_estimate=pl.CostEstimate(flops=1000, bytes_accessed=cost, transcendentals=0),
        name=name,
    )

    def apply(*args):
        return run(
            *[
                a if spec is SMEM else pltpu.with_memory_space_constraint(a, pltpu.HBM)
                for a, spec in zip(args, ins)
            ]
        )

    return apply


def rows_at(block, start=0):
    return pl.BlockSpec(block, lambda i: (i + start, 0))


def whole(block):
    return pl.BlockSpec(block, lambda i: (0,) * len(block))


def ring(n, step):
    return [(i, (i + step) % n) for i in range(n)]


def flip(a, axis, size, bit):
    return lax.ppermute(a, axis, [(i, i ^ bit) for i in range(size)])


def x_other():
    pairs = []
    for x in range(4):
        t = (x - 1) % 4 if x % 2 == 0 else (x + 1) % 4
        pairs.append(((x % 2) * 2 + x // 2, (t % 2) * 2 + t // 2))
    return pairs


def swap_x(near, far):
    return flip(near, "xl", 2, 1), lax.ppermute(far, ("xl", "xh"), x_other())


def join(a, b):
    top = jnp.maximum(a, b)
    return top + jnp.log(1.0 + jnp.exp(jnp.minimum(a, b) - top))


def split2(a):
    high = a.astype(BF16)
    return high, (a - high.astype(F32)).astype(BF16)


def split3(a):
    high = a.astype(BF16)
    rest = a - high.astype(F32)
    mid = rest.astype(BF16)
    return high, mid, (rest - mid.astype(F32)).astype(BF16)


def dot(a, b, dims=((1,), (0,))):
    return lax.dot_general(a, b, (dims, ((), ())), preferred_element_type=F32)


def scores_kernel(first, place, *refs):
    i = pl.program_id(0)
    if first:
        image_ref, near_ref, far_ref, text_ref = refs[:4]
        s_ref, th_ref, tm_ref, r_ref, c_ref, ih_ref, im_ref, il_ref = refs[4:12]
    else:
        ih_ref, im_ref, il_ref, r_in, c_in, text_ref = refs[:6]
        s_ref, th_ref, tm_ref, r_ref, c_ref = refs[6:11]
    h_t, m_t, l_t, top, total = refs[-5:]

    @pl.when(i == 0)
    def _():
        text = text_ref[...]
        th_ref[...], tm_ref[...] = split2(text)
        h_t[...], m_t[...], l_t[...] = split3(text.T)
        top[...] = jnp.full(top.shape, -jnp.inf, F32)
        total[...] = jnp.zeros(total.shape, F32)
        if first:
            c_ref[...] = jnp.zeros(c_ref.shape, F32)
        else:
            c_ref[...] = c_in[...]

    if first:
        a = jnp.where(i < 2, image_ref[...], jnp.where(i == 2, near_ref[...], far_ref[...]))
        ih_ref[...], im_ref[...], il_ref[...] = split3(a)
    ih, im, il = ih_ref[...], im_ref[...], il_ref[...]
    th, tm, tl = h_t[...], m_t[...], l_t[...]
    small = dot(ih, tl) + dot(il, th) + dot(im, tm)
    s = dot(ih, th) + (dot(ih, tm) + dot(im, th) + small)
    s_ref[...] = s
    high = jnp.max(s, axis=1, keepdims=True)
    row = high + jnp.log(jnp.sum(jnp.exp(s - high), axis=1, keepdims=True))
    row = jnp.broadcast_to(row, (row.shape[0], 128)).T[:1, :]
    slot = pl.ds((i + 2 * place[0]) % 4, 1)
    r_ref[slot, :] = row if first else join(row, r_in[slot, :])
    high = jnp.maximum(jnp.max(s, axis=0, keepdims=True), top[...])
    total[...] = total[...] * jnp.exp(top[...] - high) + jnp.sum(jnp.exp(s - high), axis=0, keepdims=True)
    top[...] = high

    @pl.when(i == pl.num_programs(0) - 1)
    def _():
        core = place[1] if first else 1 - place[1]
        c_ref[pl.ds(core, 1), :] = top[...] + jnp.log(total[...])


def weights(s, row, col):
    return 0.5 * jnp.exp(s - row) + 0.5 * jnp.exp(s - col)


def rows_kernel(away, place, s1, s2, r_ref, c_ref, th1, tm1, th2, tm2, *refs):
    i = pl.program_id(0)
    if away:
        near, far = refs[:2]
    kept = refs[2 if away else 1 :]
    part = c_ref.shape[1] // Z

    c1, c2 = (c_ref[pl.ds(a, 1), :] for a in (place[1], 1 - place[1]))
    row = r_ref[pl.ds((i + 2 * away + 2 * place[0]) % 4, 1), :]
    row = jnp.broadcast_to(row, (128, row.shape[1])).T[:, :1]
    total = None
    for b, (s, c, th, tm) in enumerate(((s1, c1, th1, tm1), (s2, c2, th2, tm2))):
        w = weights(s[...], row, c)
        if b == 0 and not away:
            x = lax.broadcasted_iota(jnp.int32, w.shape, 0) + (i * w.shape[0] - place[3])
            y = lax.broadcasted_iota(jnp.int32, w.shape, 1) - place[2] * part
            w = jnp.where((x == y) & (y >= 0) & (y < part), w - 1.0, w)
        wh, wl = split2(w)
        kept[2 * b][...], kept[2 * b + 1][...] = wh, wl
        term = dot(wh, th[...]) + (dot(wh, tm[...]) + dot(wl, th[...]))
        total = term if total is None else total + term
    if not away:
        refs[0][...] = total
    else:

        @pl.when(i == 0)
        def _():
            near[...] = total

        @pl.when(i == 1)
        def _():
            far[...] = total


def text_kernel(home_h, home_l, away_h, away_l, ih, im, *outs):
    tn = ((0,), (0,))
    rows = home_h.shape[0]
    total = None
    for h, l, k in ((home_h, home_l, 0), (away_h, away_l, rows)):
        high, mid = ih[k : k + rows, :], im[k : k + rows, :]
        wh, wl = h[...], l[...]
        term = dot(wh, high, tn) + (dot(wh, mid, tn) + dot(wl, high, tn))
        total = term if total is None else total + term
    if len(outs) == 1:
        outs[0][...] = total
        return
    n = outs[0].shape[0]
    each = total.shape[0] // n
    for k, out in enumerate(outs):

        @pl.when(pl.program_id(0) == k // each)
        def _():
            out[...] = total[k % each * n : (k % each + 1) * n]


def collect_kernel(own, *refs):
    got, out = refs[:-1], refs[-1]
    n = out.shape[0] // len(got)
    for k, ref in enumerate(got):
        at = slice(k * n, (k + 1) * n)
        out[at, :] = own[at, :] + ref[...]


def pick_kernel(place, home_ref, near_ref, far_ref, *outs):
    size, each = outs[0].shape
    for k in range(Y):
        at = (place[4] + k) % Y
        got = pl.ds((at % 2) * size, size)
        total = home_ref[pl.ds(at * size, size), :] + jnp.where(at < 2, near_ref[got, :], far_ref[got, :])
        for p in range(PARTS):
            outs[p * Y + k][...] = total[:, p * each : (p + 1) * each]


def assemble_kernel(place, *refs):
    pieces, out = refs[:-1], refs[-1]
    size, each = pieces[0].shape
    for p in range(PARTS):
        for k in range(Y):
            at = (place[4] + Y - k) % Y
            out[pl.ds(at * size, size), p * each : (p + 1) * each] = pieces[p * Y + k][...]


def local(image, text):
    rows, width = image.shape
    part = text.shape[0]
    z, xl, core, y = (lax.axis_index(a) for a in ("z", "xl", "core", "y"))
    group = y * 2 + lax.axis_index("xh")
    half = rows // 2
    place = jnp.stack([xl, core, z, group * part, y]).astype(jnp.int32)
    tall, steps = (STEP, width), rows // STEP
    table = [((2 * steps, STEP), F32, whole((2 * steps, STEP))), ((2, Z * part), F32, whole((2, Z * part)))]

    near, far = swap_x(image[:half], image[half:])
    line = lax.all_gather(text, "z", axis=0, tiled=True)
    line, near, far = lax.optimization_barrier((line, near, far))
    columns = Z * part
    full = (columns, width)

    s, th, tm = [], [], []
    for b, texts in enumerate((line, flip(line, "core", 2, 1))):
        outs = [
            ((2 * rows, columns), F32, rows_at((STEP, columns))),
            (full, BF16, whole(full)),
            (full, BF16, whole(full)),
        ] + table
        if b == 0:
            ins = [pl.BlockSpec(tall, lambda i: (jnp.minimum(i, 1), 0)), whole(tall), whole(tall)]
            outs += [((2 * rows, width), BF16, rows_at(tall))] * 3
            args = (image, near, far)
        else:
            ins = [rows_at(tall)] * 3 + [spec for _, _, spec in table]
            args = (ih, im, il, r, c)
        out = grid_call(
            functools.partial(scores_kernel, b == 0),
            "scores",
            2 * steps,
            [SMEM] + ins + [whole(full)],
            outs,
            scratch=[pltpu.VMEM((width, columns), BF16)] * 3 + [pltpu.VMEM((1, columns), F32)] * 2,
        )(place, *args, texts)
        s.append(out[0])
        th.append(out[1])
        tm.append(out[2])
        r, c = out[3:5]
        if b == 0:
            ih, im, il = out[5:]

    c = c.reshape(2, Z, part)
    rounds = zip(
        (("y", 4, 1), ("y", 4, 2), ("xl", 2, 1), ("xh", 2, 1)),
        (("core", 2, 1), ("z", 8, 1), ("z", 8, 2), ("z", 8, 4)),
    )
    for row_round, col_round in rounds:
        r, c = join(r, flip(r, *row_round)), join(c, flip(c, *col_round))

    c = c.reshape(2, columns)
    args = (s[0], s[1], r, c, th[0], tm[0], th[1], tm[1])
    sizes = [a.shape[1] for a in s]
    kept = [((rows, n), BF16, rows_at((STEP, n))) for n in sizes for _ in range(2)]
    fixed = [spec for _, _, spec in table] + [whole((n, width)) for n in sizes for _ in range(2)]
    away = grid_call(
        functools.partial(rows_kernel, 1),
        "away",
        steps,
        [SMEM] + [rows_at((STEP, n), steps) for n in sizes] + fixed,
        [((half, width), F32, whole((half, width)))] * 2 + kept,
    )(place, *args)
    got = swap_x(*away[:2])
    kept_away = away[2:]
    late, _ = lax.optimization_barrier((args, away[0]))
    home = grid_call(
        functools.partial(rows_kernel, 0),
        "home",
        steps,
        [SMEM] + [rows_at((STEP, n)) for n in sizes] + fixed,
        [((rows, width), F32, rows_at(tall))] + kept,
    )(place, *late)
    home, kept_home = home[0], home[1:]

    def make_text(b, name, outs):
        wide = pl.BlockSpec((rows, STEP), lambda i: (0, i))
        return grid_call(
            text_kernel,
            name,
            columns // STEP,
            [wide] * 4 + [whole((2 * rows, width))] * 2,
            outs,
        )(*kept_home[2 * b : 2 * b + 2], *kept_away[2 * b : 2 * b + 2], ih, im)

    piece = (columns // CUTS, width)
    other = make_text(1, "text_other", [(piece, F32, whole(piece))] * CUTS)
    (own,) = make_text(0, "text_own", [(full, F32, rows_at(tall))])
    pieces = [flip(a, "core", 2, 1) for a in other]
    (g_text,) = call(collect_kernel, "collect", [(full, F32)], 1 + len(pieces))(own, *pieces)
    g_text, *got = lax.optimization_barrier((g_text, *got))
    grad_text = lax.psum_scatter(g_text, "z", scatter_dimension=0, tiled=True)

    quarter = rows // Y
    mine = call(
        pick_kernel, "pick", [((quarter, width // PARTS), F32)] * (PARTS * Y), 3, scalars=True, cost=PICK
    )(place, home, *got)
    pieces = []
    for p in range(PARTS):
        own = mine[p * Y] + sum(lax.ppermute(mine[p * Y + k], "y", ring(Y, k)) for k in (1, 3, 2))
        own = own + flip(own, "xh", 2, 1)
        pieces += [own] + [lax.ppermute(own, "y", ring(Y, k)) for k in (1, 2, 3)]
    (out,) = call(assemble_kernel, "assemble", [((rows, width), F32)], PARTS * Y, scalars=True)(place, *pieces)
    return out, grad_text


def solution(mesh):
    fine = Mesh(mesh.devices.reshape(Z, 2, 2, Y, 2), ("z", "xl", "core", "y", "xh"))
    blk = ("z", "xl", "core")
    placed = (P(blk, None), P(blk + ("y", "xh"), None))
    return jax.shard_map(local, mesh=fine, in_specs=placed, out_specs=placed, check_vma=False)
```

time: 266 us -> 217 us (0.82)
  Pallas kernels: 0 us -> 63.7 us
  blocking collectives: 60.1 us -> 0 us
  matrix products: 45.4 us -> 0 us
  waiting for transfers between devices: 57.2 us -> 90.9 us
  between operations: 29.7 us -> 14.2 us
  local copies, waits for them, and re-layouts: 22.6 us -> 7.69 us
  other arithmetic: 9.34 us -> 1.64 us
  starting transfers between devices: 41.4 us -> 36.5 us
    pallas_call x0 -> x9, Pallas kernels: none -> 63.7 us  [the longest x6 58.6 us: apply(): run(*[a if spec is SMEM else pltpu.with_memory_space_constraint(a, pltpu....]
    all_to_all x2 -> x0, blocking collectives: 60.1 us -> none  [the longest x1 31 us: local(): lax.all_to_all(home.reshape(8, part, width), ('y', 'xh'), 0, 0, tiled=True)]
    dot_general x5 -> x0, matrix products: 45.4 us -> none  [the longest x2 25.8 us: local(): jnp.einsum('id,td->it', both, texts[b], precision=FULL, preferred_element...]
    ppermute x14 -> x35, waiting for transfers between devices: 44.6 us -> 72.1 us  [the longest x2 21.6 us: swap_x(): return (flip(near, 'xl', 2, 1), lax.ppermute(far, ('xl', 'xh'), x_other()))]
    all_gather x0 -> x1, waiting for transfers between devices: none -> 18.1 us  [local(): line = lax.all_gather(text, 'z', axis=0, tiled=True)]
    all_to_all x2 -> x0, starting transfers between devices: 15.4 us -> none  [the longest x1 7.96 us: local(): lax.all_to_all(c, ('z', 'core'), 0, 0, tiled=True)]
    all_to_all x2 -> x0, waiting for transfers between devices: 12.6 us -> none  [the longest x1 7.54 us: local(): lax.all_to_all(c, ('z', 'core'), 0, 0, tiled=True)]
    ppermute x14 -> x35, starting transfers between devices: 25.9 us -> 36.4 us  [the longest x21 18.9 us: flip(): return lax.ppermute(a, axis, [(i, i ^ bit) for i in range(size)])]
  transfers between devices with their start and end apart: 17 -> 37, of which waited for: 8 -> 20; matrix products, arithmetic and copies ran while one was open for 11% -> 2% of each run, Pallas kernels for 0% -> 20%
where the time goes in v2:
time: 217 us; the launch traced here: 215 us
  waiting for transfers between devices  90.9 us (42%)
  Pallas kernels  63.7 us (29%)
  starting transfers between devices  36.5 us (17%)
  between operations  14.2 us (7%)
  local copies, waits for them, and re-layouts  7.69 us (4%)
    pallas_call x6, Pallas kernels, apply(): run(*[a if spec is SMEM else pltpu.with_memory_space_constraint(a, pltpu....  58.6 us
    ppermute x2, waiting for transfers between devices, swap_x(): return (flip(near, 'xl', 2, 1), lax.ppermute(far, ('xl', 'xh'), x_other()))  21.6 us
    ppermute x6, waiting for transfers between devices, local(): lax.ppermute(mine[p * Y + k], 'y', ring(Y, k))  19.7 us
    ppermute x21, starting transfers between devices, flip(): return lax.ppermute(a, axis, [(i, i ^ bit) for i in range(size)])  18.9 us
    all_gather x1, waiting for transfers between devices, local(): line = lax.all_gather(text, 'z', axis=0, tiled=True)  18.1 us
    ppermute x6, waiting for transfers between devices, local(): pieces += [own] + [lax.ppermute(own, 'y', ring(Y, k)) for k in (1, 2, 3)]  16 us
    ppermute x21, waiting for transfers between devices, flip(): return lax.ppermute(a, axis, [(i, i ^ bit) for i in range(size)])  14.8 us
    ppermute x6, starting transfers between devices, local(): pieces += [own] + [lax.ppermute(own, 'y', ring(Y, k)) for k in (1, 2, 3)]  7.79 us
  transfers between devices with their start and end apart: 37, of which 20 were waited for; matrix products, arithmetic and copies ran while one was open for 2% of the time, Pallas kernels for 20%

profile of v2, /device:TPU:2, one launch (start us, length us, event | category | flops | bytes accessed | tf_op | source)
XLA Modules:
  0.0 214.6 jit_solution(3102237110835617317)
XLA Ops:
  7.2 0.7 all-gather.2.cloned.1.call-update
  7.9 1.7 fusion
  9.6 1.6 collective-permute-start.1
  11.2 1.8 collective-permute-start
  13.0 21.6 %collective-permute-done.1.refs_2_ = f32[256,1024]{1,0:T(8,128)S(1)} collective-permute-done((f32[256,1024]{1,0:T(8,128)S(1)}, f32[256,1024]{1,0:T(8,128)S(1)}, u32[]{:S(2)}, u32[]{:S(2)}) %collective-permute-start.1) | collective-permute-done | bytes 1048608 | tf_op jit(solution)/shard_map/ppermute | solution.py:87
  34.6 1.4 collective-permute-done.refs_1_
  36.0 18.1 %all-gather.2.cloned.1.call-done.refs_3_ = f32[512,1024]{1,0:T(8,128)} async-done(((f32[64,1024]{1,0:T(8,128)}), f32[512,1024]{1,0:T(8,128)}) %all-gather.2.cloned.1.call-update) | async-done | bytes 2097168 | tf_op jit(solution)/shard_map/all_gather | solution.py:253
  54.2 14.1 %scores.2 = (f32[1024,512]{1,0:T(8,128)}, bf16[512,1024]{1,0:T(8,128)(2,1)}, bf16[512,1024]{1,0:T(8,128)(2,1)}, f32[4,256]{1,0:T(4,128)}, f32[2,512]{1,0:T(2,128...) custom-call(s32[5]{0:T(128)S(1)} %stack.23.place, f32[512,1024]{1,0:T(8,128)} %refs_0_.1, ...), custom_call_target="tpu_custom_call" | custom-call | flops 1000 | bytes 1000 | tf_op jit(solution)/shard_map/scores/pallas_call | solution.py:52
  68.2 1.3 copy-done.2
  69.6 13.1 %scores.3 = (f32[1024,512]{1,0:T(8,128)}, bf16[512,1024]{1,0:T(8,128)(2,1)}, bf16[512,1024]{1,0:T(8,128)(2,1)}, f32[4,256]{1,0:T(4,128)}, f32[2,512]{1,0:T(2,128)}) custom-call(s32[5]{0:T(128)S(1)} %stack.23.place, bf16[1024,1024]{1,0:T(8,128)(2,1)} %get-tuple-element.60.refs_0_.ih, bf16[1024,1024]{1,0:T(8,128)(2,1)} %get-tuple-element.61.refs_1_.im, ...), custom_call_target="tpu_custom_call" | custom-call | flops 1000 | bytes 1000 | tf_op jit(solution)/shard_map/scores/pallas_call | solution.py:52
  82.7 0.8 reshape.10
  83.4 0.5 collective-permute-start.7
  83.9 1.5 collective-permute-start.3
  85.4 1.1 collective-permute-start.8
  86.6 1.2 collective-permute-done.3
  87.8 0.7 log_add_fusion.7
  88.5 3.1 %collective-permute-start.4 = (f32[4,256]{1,0:T(4,128)S(1)}, f32[4,256]{1,0:T(4,128)S(1)}, u32[]{:S(2)}, u32[]{:S(2)}) collective-permute-start(f32[4,256]{1,0:T(4,128)S(1)} %log_add_fusion.7), channel_id=1, source_target_pairs={{0,4},{2,6},{4,0},{6,2},{1,5},{3,7},{5,1},{7,3},{8,12},{10,14},{12... | collective-permute-start | bytes 12296 | tf_op jit(solution)/shard_map/ppermute | solution.py:75
  91.6 1.1 collective-permute-start.9
  92.7 0.9 collective-permute-done.4
  93.7 0.7 collective-permute-start.5
  94.3 1.9 collective-permute-done.9
  96.2 2.9 %collective-permute-start.10 = (f32[2,8,64]{2,1,0:T(8,128)S(1)}, f32[2,8,64]{2,1,0:T(8,128)S(1)}, u32[]{:S(2)}, u32[]{:S(2)}) collective-permute-start(f32[2,8,64]{2,1,0:T(8,128)S(1)} %log_add_fusion.1), channel_id=1, source_target_pairs={{0,128},{32,160},{64,192},{96,224},{128,0},{160,32},{192,64},{224,... | collective-permute-start | bytes 12296 | tf_op jit(solution)/shard_map/ppermute | solution.py:75
  99.1 2.5 %collective-permute-start.6 = (f32[4,256]{1,0:T(4,128)S(1)}, f32[4,256]{1,0:T(4,128)S(1)}, u32[]{:S(2)}, u32[]{:S(2)}) collective-permute-start(f32[4,256]{1,0:T(4,128)S(1)} %log_add_fusion.5), channel_id=1, source_target_pairs={{0,1},{1,0},{2,3},{3,2},{4,5},{5,4},{6,7},{7,6},{8,9},{9,8},{10,11... | collective-permute-start | bytes 12296 | tf_op jit(solution)/shard_map/ppermute | solution.py:75
  101.6 2.2 %collective-permute-done.10 = f32[2,8,64]{2,1,0:T(8,128)S(1)} collective-permute-done((f32[2,8,64]{2,1,0:T(8,128)S(1)}, f32[2,8,64]{2,1,0:T(8,128)S(1)}, u32[]{:S(2)}, u32[]{:S(2)}) %collective-permute-start.10) | collective-permute-done | bytes 4128 | tf_op jit(solution)/shard_map/ppermute | solution.py:75
  103.9 0.7 reshape.11.c_ref
  104.6 0.6 log_add_fusion.4.r_ref
  105.2 8.6 %away.1 = (f32[256,1024]{1,0:T(8,128)}, f32[256,1024]{1,0:T(8,128)}, bf16[512,512]{1,0:T(8,128)(2,1)}, bf16[512,512]{1,0:T(8,128)(2,1)}, bf16[512,512]{1,0:T(8,128)(2,1)}, /*index=5*/bf16[512,512]{1,0:T(8,128)(2,1)}) custom-call(s32[5]{0:T(128)S(1)} %stack.23.place, f32[1024,512]{1,0:T(8,128)} %get-tuple-element.73.s1, f32[1024,512]{1,0:T(8,128)} %get-tuple-element.74.s2, ...), custom_call_target="tpu_custom_call" | custom-call | flops 1000 | bytes 1000 | tf_op jit(solution)/shard_map/away/pallas_call | solution.py:52
  113.8 1.6 collective-permute-start.20
  115.3 1.9 collective-permute-start.19
  117.2 7.8 %home.1 = (f32[512,1024]{1,0:T(8,128)}, bf16[512,512]{1,0:T(8,128)(2,1)}, bf16[512,512]{1,0:T(8,128)(2,1)}, bf16[512,512]{1,0:T(8,128)(2,1)}, bf16[512,512]{1,0:T(8,128)(2,1)}) custom-call(s32[5]{0:T(128)S(1)} %stack.23.place, f32[1024,512]{1,0:T(8,128)} %get-tuple-element.73.s1, f32[1024,512]{1,0:T(8,128)} %get-tuple-element.74.s2, ...), custom_call_target="tpu_custom_call" | custom-call | flops 1000 | bytes 1000 | tf_op jit(solution)/shard_map/home/pallas_call | solution.py:52
  125.0 7.7 %text_other.1 = (f32[64,1024]{1,0:T(8,128)}, f32[64,1024]{1,0:T(8,128)}, f32[64,1024]{1,0:T(8,128)}, f32[64,1024]{1,0:T(8,128)}, f32[64,1024]{1,0:T(8,128)}, /*i...) custom-call(bf16[512,512]{1,0:T(8,128)(2,1)} %get-tuple-element.86.home_h, ...), custom_call_target="tpu_custom_call" | custom-call | flops 1000 | bytes 1000 | tf_op jit(solution)/shard_map/text_other/pallas_call | solution.py:52
  132.8 0.5 collective-permute-start.12
  133.4 1.1 collective-permute-done.11.refs_0_
  134.7 0.2 collective-permute-done.12.refs_1_
  134.9 0.1 collective-permute-start.15
  135.0 0.2 collective-permute-done.13.refs_2_
  135.3 0.1 collective-permute-start.16
  135.4 0.9 collective-permute-done.14.refs_3_
  136.4 0.2 collective-permute-done.15.refs_4_
  136.6 0.1 collective-permute-start.18
  136.8 7.3 %text_own.1.own = f32[512,1024]{1,0:T(8,128)} custom-call(bf16[512,512]{1,0:T(8,128)(2,1)} %get-tuple-element.82.home_h, bf16[512,512]{1,0:T(8,128)(2,1)} %get-tuple-element.83.home_l, bf16[512,512]{1,0:T(8,128)(2,1)} %get-tuple-element.84.away_h, bf16[512,512]{1,0:T(8,128)(2,1)} %get-tuple-element.85.away_l, ...), custom_call_target="tpu_custom_call" | custom-call | flops 1000 | bytes 1000 | tf_op jit(solution)/shard_map/text_own/pallas_call | solution.py:52
  144.1 1.6 copy-done
  145.7 1.5 collect.1
  147.2 1.6 copy-done.1
  148.8 1.5 pick.1
  150.4 0.7 collective-permute-start.21
  151.0 2.6 %collective-permute-start.22 = (f32[128,512]{1,0:T(8,128)S(1)}, f32[128,512]{1,0:T(8,128)S(1)}, u32[]{:S(2)}, u32[]{:S(2)}) collective-permute-start(f32[128,512]{1,0:T(8,128)S(1)} %get-tuple-element.103), channel_id=1, source_target_pairs={{0,6},{2,0},{4,2},{6,4},{1,7},{3,1},{5,3},{7,5},{8,14},{10,8},{12,... | collective-permute-start | bytes 786440 | tf_op jit(solution)/shard_map/ppermute | solution.py:343
  153.8 0.8 collective-permute-start.28
  154.5 2.5 %collective-permute-start.29 = (f32[128,512]{1,0:T(8,128)S(1)}, f32[128,512]{1,0:T(8,128)S(1)}, u32[]{:S(2)}, u32[]{:S(2)}) collective-permute-start(f32[128,512]{1,0:T(8,128)S(1)} %get-tuple-element.107), channel_id=1, source_target_pairs={{0,6},{2,0},{4,2},{6,4},{1,7},{3,1},{5,3},{7,5},{8,14},{10,8},{12,... | collective-permute-start | bytes 786440 | tf_op jit(solution)/shard_map/ppermute | solution.py:343
  157.0 9.4 %collective-permute-done.21 = f32[128,512]{1,0:T(8,128)S(1)} collective-permute-done((f32[128,512]{1,0:T(8,128)S(1)}, f32[128,512]{1,0:T(8,128)S(1)}, u32[]{:S(2)}, u32[]{:S(2)}) %collective-permute-start.21) | collective-permute-done | bytes 262176 | tf_op jit(solution)/shard_map/ppermute | solution.py:343
  166.5 0.2 collective-permute-start.24
  166.7 10.3 %collective-permute-done.28 = f32[128,512]{1,0:T(8,128)S(1)} collective-permute-done((f32[128,512]{1,0:T(8,128)S(1)}, f32[128,512]{1,0:T(8,128)S(1)}, u32[]{:S(2)}, u32[]{:S(2)}) %collective-permute-start.28) | collective-permute-done | bytes 262176 | tf_op jit(solution)/shard_map/ppermute | solution.py:343
  177.2 0.2 collective-permute-start.31
  177.4 3.0 %collective-permute-start.27 = (f32[128,512]{1,0:T(8,128)S(1)}, f32[128,512]{1,0:T(8,128)S(1)}, u32[]{:S(2)}, u32[]{:S(2)}) collective-permute-start(f32[128,512]{1,0:T(8,128)S(1)} %add.97.refs_0_), channel_id=1, source_target_pairs={{0,6},{2,0},{4,2},{6,4},{1,7},{3,1},{5,3},{7,5},{8,14},{10,8},{12,... | collective-permute-start | bytes 786440 | tf_op jit(solution)/shard_map/ppermute | solution.py:345
  180.5 0.9 collective-permute-start.25
  181.4 4.5 %collective-permute-done.31 = f32[128,512]{1,0:T(8,128)S(1)} collective-permute-done((f32[128,512]{1,0:T(8,128)S(1)}, f32[128,512]{1,0:T(8,128)S(1)}, u32[]{:S(2)}, u32[]{:S(2)}) %collective-permute-start.31) | collective-permute-done | bytes 262176 | tf_op jit(solution)/shard_map/ppermute | solution.py:75
  185.9 3.5 %collective-permute-start.34 = (f32[128,512]{1,0:T(8,128)S(1)}, f32[128,512]{1,0:T(8,128)S(1)}, u32[]{:S(2)}, u32[]{:S(2)}) collective-permute-start(f32[128,512]{1,0:T(8,128)S(1)} %add.101.refs_4_), channel_id=1, source_target_pairs={{0,6},{2,0},{4,2},{6,4},{1,7},{3,1},{5,3},{7,5},{8,14},{10,8},{12,... | collective-permute-start | bytes 786440 | tf_op jit(solution)/shard_map/ppermute | solution.py:345
  189.4 0.3 collective-permute-start.33
  189.7 2.5 %collective-permute-done.27.refs_3_ = f32[128,512]{1,0:T(8,128)S(1)} collective-permute-done((f32[128,512]{1,0:T(8,128)S(1)}, f32[128,512]{1,0:T(8,128)S(1)}, u32[]{:S(2)}, u32[]{:S(2)}) %collective-permute-start.27) | collective-permute-done | bytes 262176 | tf_op jit(solution)/shard_map/ppermute | solution.py:345
  192.2 4.7 %collective-permute-done.25.refs_1_ = f32[128,512]{1,0:T(8,128)S(1)} collective-permute-done((f32[128,512]{1,0:T(8,128)S(1)}, f32[128,512]{1,0:T(8,128)S(1)}, u32[]{:S(2)}, u32[]{:S(2)}) %collective-permute-start.25) | collective-permute-done | bytes 262176 | tf_op jit(solution)/shard_map/ppermute | solution.py:345
  196.9 5.4 %collective-permute-done.34.refs_7_ = f32[128,512]{1,0:T(8,128)S(1)} collective-permute-done((f32[128,512]{1,0:T(8,128)S(1)}, f32[128,512]{1,0:T(8,128)S(1)}, u32[]{:S(2)}, u32[]{:S(2)}) %collective-permute-start.34) | collective-permute-done | bytes 262176 | tf_op jit(solution)/shard_map/ppermute | solution.py:345
  202.3 0.2 collective-permute-done.33.refs_6_
  202.5 3.2 %collective-permute-done.32.refs_5_ = f32[128,512]{1,0:T(8,128)S(1)} collective-permute-done((f32[128,512]{1,0:T(8,128)S(1)}, f32[128,512]{1,0:T(8,128)S(1)}, u32[]{:S(2)}, u32[]{:S(2)}) %collective-permute-start.32) | collective-permute-done | bytes 262176 | tf_op jit(solution)/shard_map/ppermute | solution.py:345
  205.8 2.0 assemble.1
  (45 shorter events, 1.1 us)
Async XLA Ops:
  7.2 46.9 %all-gather.2.cloned.1.call-start = ((), (), s32[]{:S(2)}) async-start(), calls=%async_computation.1 | async-start | bytes 2359296 | tf_op jit(solution)/shard_map/all_gather | solution.py:253
  7.9 199.9 %reduce-scatter.2.cloned.1.call-start = ((), (), s32[]{:S(2)}) async-start(), calls=%async_computation.2 | async-start | bytes 2359296 | tf_op jit(solution)/shard_map/reduce_scatter | solution.py:335
  9.6 25.0 %collective-permute-start.1 = (f32[256,1024]{1,0:T(8,128)S(1)}, f32[256,1024]{1,0:T(8,128)S(1)}, u32[]{:S(2)}, u32[]{:S(2)}) collective-permute-start(f32[256,1024]{1,0:T(8,128)S(1)} %get-tuple-element.110), channel_id=1, source_target_pairs={{0,17},{16,1},{1,16},{17,0},{2,19},{18,3},{3,18},{19,2},{4,21},{20... | collective-permute-start | bytes 3145736 | tf_op jit(solution)/shard_map/ppermute | solution.py:87
  11.2 24.8 %collective-permute-start = (f32[256,1024]{1,0:T(8,128)S(1)}, f32[256,1024]{1,0:T(8,128)}, u32[]{:S(2)}, u32[]{:S(2)}) collective-permute-start(f32[256,1024]{1,0:T(8,128)S(1)} %get-tuple-element.111), channel_id=1, source_target_pairs={{0,16},{16,0},{1,17},{17,1},{2,18},{18,2},{3,19},{19,3},{4,20},{20... | collective-permute-start | bytes 3145736 | tf_op jit(solution)/shard_map/ppermute | solution.py:75
  34.6 19.6 %copy-start.3 = (f32[256,1024]{1,0:T(8,128)}, f32[256,1024]{1,0:T(8,128)S(1)}, u32[]{:S(2)}) copy-start(f32[256,1024]{1,0:T(8,128)S(1)} %collective-permute-done.1.refs_2_) | copy-start | bytes 3145732
  54.1 14.1 %collective-permute-start.2 = (f32[512,1024]{1,0:T(8,128)}, f32[512,1024]{1,0:T(8,128)S(1)}, u32[]{:S(2)}, u32[]{:S(2)}) collective-permute-start(f32[512,1024]{1,0:T(8,128)} %all-gather.2.cloned.1.call-done.refs_3_), channel_id=1, source_target_pairs={{0,8},{8,0},{1,9},{9,1},{2,10},{10,2},{3,11},{11,3},{4,12},{12,4},... | collective-permute-start | bytes 6291464 | tf_op jit(solution)/shard_map/ppermute | solution.py:75
  68.2 1.4 copy-start.2
  83.4 2.0 collective-permute-start.7
  83.9 3.8 %collective-permute-start.3 = (f32[4,256]{1,0:T(4,128)}, f32[4,256]{1,0:T(4,128)S(1)}, u32[]{:S(2)}, u32[]{:S(2)}) collective-permute-start(f32[4,256]{1,0:T(4,128)} %get-tuple-element.66), channel_id=1, source_target_pairs={{0,2},{2,0},{4,6},{6,4},{1,3},{3,1},{5,7},{7,5},{8,10},{10,8},{12,... | collective-permute-start | bytes 12296 | tf_op jit(solution)/shard_map/ppermute | solution.py:75
  85.4 6.1 %collective-permute-start.8 = (f32[2,8,64]{2,1,0:T(8,128)S(1)}, f32[2,8,64]{2,1,0:T(8,128)S(1)}, u32[]{:S(2)}, u32[]{:S(2)}) collective-permute-start(f32[2,8,64]{2,1,0:T(8,128)S(1)} %log_add_fusion.3), channel_id=1, source_target_pairs={{0,32},{32,0},{64,96},{96,64},{128,160},{160,128},{192,224},{224,1... | collective-permute-start | bytes 12296 | tf_op jit(solution)/shard_map/ppermute | solution.py:75
  88.5 5.2 %collective-permute-start.4 = (f32[4,256]{1,0:T(4,128)S(1)}, f32[4,256]{1,0:T(4,128)S(1)}, u32[]{:S(2)}, u32[]{:S(2)}) collective-permute-start(f32[4,256]{1,0:T(4,128)S(1)} %log_add_fusion.7), channel_id=1, source_target_pairs={{0,4},{2,6},{4,0},{6,2},{1,5},{3,7},{5,1},{7,3},{8,12},{10,14},{12... | collective-permute-start | bytes 12296 | tf_op jit(solution)/shard_map/ppermute | solution.py:75
  91.6 4.6 %collective-permute-start.9 = (f32[2,8,64]{2,1,0:T(8,128)S(1)}, f32[2,8,64]{2,1,0:T(8,128)S(1)}, u32[]{:S(2)}, u32[]{:S(2)}) collective-permute-start(f32[2,8,64]{2,1,0:T(8,128)S(1)} %log_add_fusion.2), channel_id=1, source_target_pairs={{0,64},{32,96},{64,0},{96,32},{128,192},{160,224},{192,128},{224,1... | collective-permute-start | bytes 12296 | tf_op jit(solution)/shard_map/ppermute | solution.py:75
  93.7 5.4 %collective-permute-start.5 = (f32[4,256]{1,0:T(4,128)S(1)}, f32[4,256]{1,0:T(4,128)S(1)}, u32[]{:S(2)}, u32[]{:S(2)}) collective-permute-start(f32[4,256]{1,0:T(4,128)S(1)} %log_add_fusion.6), channel_id=1, source_target_pairs={{0,16},{16,0},{1,17},{17,1},{2,18},{18,2},{3,19},{19,3},{4,20},{20... | collective-permute-start | bytes 12296 | tf_op jit(solution)/shard_map/ppermute | solution.py:75
  96.2 7.6 %collective-permute-start.10 = (f32[2,8,64]{2,1,0:T(8,128)S(1)}, f32[2,8,64]{2,1,0:T(8,128)S(1)}, u32[]{:S(2)}, u32[]{:S(2)}) collective-permute-start(f32[2,8,64]{2,1,0:T(8,128)S(1)} %log_add_fusion.1), channel_id=1, source_target_pairs={{0,128},{32,160},{64,192},{96,224},{128,0},{160,32},{192,64},{224,... | collective-permute-start | bytes 12296 | tf_op jit(solution)/shard_map/ppermute | solution.py:75
  99.1 5.4 %collective-permute-start.6 = (f32[4,256]{1,0:T(4,128)S(1)}, f32[4,256]{1,0:T(4,128)S(1)}, u32[]{:S(2)}, u32[]{:S(2)}) collective-permute-start(f32[4,256]{1,0:T(4,128)S(1)} %log_add_fusion.5), channel_id=1, source_target_pairs={{0,1},{1,0},{2,3},{3,2},{4,5},{5,4},{6,7},{7,6},{8,9},{9,8},{10,11... | collective-permute-start | bytes 12296 | tf_op jit(solution)/shard_map/ppermute | solution.py:75
  113.8 33.5 %collective-permute-start.20 = (f32[256,1024]{1,0:T(8,128)}, f32[256,1024]{1,0:T(8,128)S(1)}, u32[]{:S(2)}, u32[]{:S(2)}) collective-permute-start(f32[256,1024]{1,0:T(8,128)} %get-tuple-element.98), channel_id=1, source_target_pairs={{0,17},{16,1},{1,16},{17,0},{2,19},{18,3},{3,18},{19,2},{4,21},{20... | collective-permute-start | bytes 3145736 | tf_op jit(solution)/shard_map/ppermute | solution.py:87
  115.3 31.9 %collective-permute-start.19 = (f32[256,1024]{1,0:T(8,128)}, f32[256,1024]{1,0:T(8,128)}, u32[]{:S(2)}, u32[]{:S(2)}) collective-permute-start(f32[256,1024]{1,0:T(8,128)} %get-tuple-element.72), channel_id=1, source_target_pairs={{0,16},{16,0},{1,17},{17,1},{2,18},{18,2},{3,19},{19,3},{4,20},{20... | collective-permute-start | bytes 3145736 | tf_op jit(solution)/shard_map/ppermute | solution.py:75
  132.8 1.7 collective-permute-start.11
  132.8 2.1 collective-permute-start.12
  133.3 2.0 collective-permute-start.13
  134.5 1.7 collective-permute-start.14
  134.9 1.7 collective-permute-start.15
  135.3 8.8 %collective-permute-start.16 = (f32[64,1024]{1,0:T(8,128)}, f32[64,1024]{1,0:T(8,128)S(1)}, u32[]{:S(2)}, u32[]{:S(2)}) collective-permute-start(f32[64,1024]{1,0:T(8,128)} %get-tuple-element.95), channel_id=1, source_target_pairs={{0,8},{8,0},{1,9},{9,1},{2,10},{10,2},{3,11},{11,3},{4,12},{12,4},... | collective-permute-start | bytes 786440 | tf_op jit(solution)/shard_map/ppermute | solution.py:75
  136.3 7.8 %collective-permute-start.17 = (f32[64,1024]{1,0:T(8,128)}, f32[64,1024]{1,0:T(8,128)S(1)}, u32[]{:S(2)}, u32[]{:S(2)}) collective-permute-start(f32[64,1024]{1,0:T(8,128)} %get-tuple-element.96), channel_id=1, source_target_pairs={{0,8},{8,0},{1,9},{9,1},{2,10},{10,2},{3,11},{11,3},{4,12},{12,4},... | collective-permute-start | bytes 786440 | tf_op jit(solution)/shard_map/ppermute | solution.py:75
  136.6 7.4 %collective-permute-start.18 = (f32[64,1024]{1,0:T(8,128)}, f32[64,1024]{1,0:T(8,128)S(1)}, u32[]{:S(2)}, u32[]{:S(2)}) collective-permute-start(f32[64,1024]{1,0:T(8,128)} %get-tuple-element.97), channel_id=1, source_target_pairs={{0,8},{8,0},{1,9},{9,1},{2,10},{10,2},{3,11},{11,3},{4,12},{12,4},... | collective-permute-start | bytes 786440 | tf_op jit(solution)/shard_map/ppermute | solution.py:75
  144.1 1.6 copy-start
  147.2 1.6 copy-start.1
  150.4 16.0 %collective-permute-start.21 = (f32[128,512]{1,0:T(8,128)S(1)}, f32[128,512]{1,0:T(8,128)S(1)}, u32[]{:S(2)}, u32[]{:S(2)}) collective-permute-start(f32[128,512]{1,0:T(8,128)S(1)} %get-tuple-element.102), channel_id=1, source_target_pairs={{0,2},{2,4},{4,6},{6,0},{1,3},{3,5},{5,7},{7,1},{8,10},{10,12},{12... | collective-permute-start | bytes 786440 | tf_op jit(solution)/shard_map/ppermute | solution.py:343
  151.0 15.4 %collective-permute-start.22 = (f32[128,512]{1,0:T(8,128)S(1)}, f32[128,512]{1,0:T(8,128)S(1)}, u32[]{:S(2)}, u32[]{:S(2)}) collective-permute-start(f32[128,512]{1,0:T(8,128)S(1)} %get-tuple-element.103), channel_id=1, source_target_pairs={{0,6},{2,0},{4,2},{6,4},{1,7},{3,1},{5,3},{7,5},{8,14},{10,8},{12,... | collective-permute-start | bytes 786440 | tf_op jit(solution)/shard_map/ppermute | solution.py:343
  153.7 12.7 %collective-permute-start.23 = (f32[128,512]{1,0:T(8,128)S(1)}, f32[128,512]{1,0:T(8,128)S(1)}, u32[]{:S(2)}, u32[]{:S(2)}) collective-permute-start(f32[128,512]{1,0:T(8,128)S(1)} %get-tuple-element.104), channel_id=1, source_target_pairs={{0,4},{2,6},{4,0},{6,2},{1,5},{3,7},{5,1},{7,3},{8,12},{10,14},{12... | collective-permute-start | bytes 786440 | tf_op jit(solution)/shard_map/ppermute | solution.py:343
  153.8 23.3 %collective-permute-start.28 = (f32[128,512]{1,0:T(8,128)S(1)}, f32[128,512]{1,0:T(8,128)S(1)}, u32[]{:S(2)}, u32[]{:S(2)}) collective-permute-start(f32[128,512]{1,0:T(8,128)S(1)} %get-tuple-element.106), channel_id=1, source_target_pairs={{0,2},{2,4},{4,6},{6,0},{1,3},{3,5},{5,7},{7,1},{8,10},{10,12},{12... | collective-permute-start | bytes 786440 | tf_op jit(solution)/shard_map/ppermute | solution.py:343
  154.5 22.5 %collective-permute-start.29 = (f32[128,512]{1,0:T(8,128)S(1)}, f32[128,512]{1,0:T(8,128)S(1)}, u32[]{:S(2)}, u32[]{:S(2)}) collective-permute-start(f32[128,512]{1,0:T(8,128)S(1)} %get-tuple-element.107), channel_id=1, source_target_pairs={{0,6},{2,0},{4,2},{6,4},{1,7},{3,1},{5,3},{7,5},{8,14},{10,8},{12,... | collective-permute-start | bytes 786440 | tf_op jit(solution)/shard_map/ppermute | solution.py:343
  166.4 10.7 %collective-permute-start.30 = (f32[128,512]{1,0:T(8,128)S(1)}, f32[128,512]{1,0:T(8,128)S(1)}, u32[]{:S(2)}, u32[]{:S(2)}) collective-permute-start(f32[128,512]{1,0:T(8,128)S(1)} %get-tuple-element.108), channel_id=1, source_target_pairs={{0,4},{2,6},{4,0},{6,2},{1,5},{3,7},{5,1},{7,3},{8,12},{10,14},{12... | collective-permute-start | bytes 786440 | tf_op jit(solution)/shard_map/ppermute | solution.py:343
  166.5 10.9 %collective-permute-start.24 = (f32[128,512]{1,0:T(8,128)S(1)}, f32[128,512]{1,0:T(8,128)S(1)}, u32[]{:S(2)}, u32[]{:S(2)}) collective-permute-start(f32[128,512]{1,0:T(8,128)S(1)} %add_add_fusion.1), channel_id=1, source_target_pairs={{0,1},{1,0},{2,3},{3,2},{4,5},{5,4},{6,7},{7,6},{8,9},{9,8},{10,11... | collective-permute-start | bytes 786440 | tf_op jit(solution)/shard_map/ppermute | solution.py:75
  177.2 8.7 %collective-permute-start.31 = (f32[128,512]{1,0:T(8,128)S(1)}, f32[128,512]{1,0:T(8,128)S(1)}, u32[]{:S(2)}, u32[]{:S(2)}) collective-permute-start(f32[128,512]{1,0:T(8,128)S(1)} %add_add_fusion), channel_id=1, source_target_pairs={{0,1},{1,0},{2,3},{3,2},{4,5},{5,4},{6,7},{7,6},{8,9},{9,8},{10,11... | collective-permute-start | bytes 786440 | tf_op jit(solution)/shard_map/ppermute | solution.py:75
  177.4 14.8 %collective-permute-start.27 = (f32[128,512]{1,0:T(8,128)S(1)}, f32[128,512]{1,0:T(8,128)S(1)}, u32[]{:S(2)}, u32[]{:S(2)}) collective-permute-start(f32[128,512]{1,0:T(8,128)S(1)} %add.97.refs_0_), channel_id=1, source_target_pairs={{0,6},{2,0},{4,2},{6,4},{1,7},{3,1},{5,3},{7,5},{8,14},{10,8},{12,... | collective-permute-start | bytes 786440 | tf_op jit(solution)/shard_map/ppermute | solution.py:345
  180.5 11.8 %collective-permute-start.26 = (f32[128,512]{1,0:T(8,128)S(1)}, f32[128,512]{1,0:T(8,128)S(1)}, u32[]{:S(2)}, u32[]{:S(2)}) collective-permute-start(f32[128,512]{1,0:T(8,128)S(1)} %add.97.refs_0_), channel_id=1, source_target_pairs={{0,4},{2,6},{4,0},{6,2},{1,5},{3,7},{5,1},{7,3},{8,12},{10,14},{12... | collective-permute-start | bytes 786440 | tf_op jit(solution)/shard_map/ppermute | solution.py:345
  180.5 16.4 %collective-permute-start.25 = (f32[128,512]{1,0:T(8,128)S(1)}, f32[128,512]{1,0:T(8,128)S(1)}, u32[]{:S(2)}, u32[]{:S(2)}) collective-permute-start(f32[128,512]{1,0:T(8,128)S(1)} %add.97.refs_0_), channel_id=1, source_target_pairs={{0,2},{2,4},{4,6},{6,0},{1,3},{3,5},{5,7},{7,1},{8,10},{10,12},{12... | collective-permute-start | bytes 786440 | tf_op jit(solution)/shard_map/ppermute | solution.py:345
  185.9 16.4 %collective-permute-start.34 = (f32[128,512]{1,0:T(8,128)S(1)}, f32[128,512]{1,0:T(8,128)S(1)}, u32[]{:S(2)}, u32[]{:S(2)}) collective-permute-start(f32[128,512]{1,0:T(8,128)S(1)} %add.101.refs_4_), channel_id=1, source_target_pairs={{0,6},{2,0},{4,2},{6,4},{1,7},{3,1},{5,3},{7,5},{8,14},{10,8},{12,... | collective-permute-start | bytes 786440 | tf_op jit(solution)/shard_map/ppermute | solution.py:345
  189.4 13.1 %collective-permute-start.33 = (f32[128,512]{1,0:T(8,128)S(1)}, f32[128,512]{1,0:T(8,128)S(1)}, u32[]{:S(2)}, u32[]{:S(2)}) collective-permute-start(f32[128,512]{1,0:T(8,128)S(1)} %add.101.refs_4_), channel_id=1, source_target_pairs={{0,4},{2,6},{4,0},{6,2},{1,5},{3,7},{5,1},{7,3},{8,12},{10,14},{12... | collective-permute-start | bytes 786440 | tf_op jit(solution)/shard_map/ppermute | solution.py:345
  192.2 13.5 %collective-permute-start.32 = (f32[128,512]{1,0:T(8,128)S(1)}, f32[128,512]{1,0:T(8,128)S(1)}, u32[]{:S(2)}, u32[]{:S(2)}) collective-permute-start(f32[128,512]{1,0:T(8,128)S(1)} %add.101.refs_4_), channel_id=1, source_target_pairs={{0,2},{2,4},{4,6},{6,0},{1,3},{3,5},{5,7},{7,1},{8,10},{10,12},{12... | collective-permute-start | bytes 786440 | tf_op jit(solution)/shard_map/ppermute | solution.py:345
Sparse Core Ops, SparseCore 0:
  9.8 44.2 all-gather.1
  147.4 38.0 reduce-scatter.1

commit v3 on v2

--- a/solution.py
+++ b/solution.py
@@ -10,7 +10,7 @@
 Z, Y = 8, 4
 STEP = 256
 CUTS = 8
-PARTS = 2
+WIDE = 512
 PICK = 100_000_000
 F32, BF16 = jnp.float32, jnp.bfloat16
 VMEM = pl.BlockSpec(memory_space=pltpu.VMEM)
@@ -33,11 +33,13 @@
     )
 
 
-def grid_call(kernel, name, steps, ins, outs, scratch=(), cost=1000):
+def grid_call(kernel, name, steps, ins, outs, scratch=(), cost=1000, free_in=(), free_out=()):
     run = pl.pallas_call(
         kernel,
         grid=(steps,),
-        out_shape=tuple(pltpu.HBM(s, t) for s, t, _ in outs),
+        out_shape=tuple(
+            jax.ShapeDtypeStruct(s, t) if k in free_out else pltpu.HBM(s, t) for k, (s, t, _) in enumerate(outs)
+        ),
         in_specs=list(ins),
         out_specs=tuple(spec for _, _, spec in outs),
         scratch_shapes=scratch,
@@ -51,8 +53,8 @@
     def apply(*args):
         return run(
             *[
-                a if spec is SMEM else pltpu.with_memory_space_constraint(a, pltpu.HBM)
-                for a, spec in zip(args, ins)
+                a if k == 0 and ins[0] is SMEM or k in free_in else pltpu.with_memory_space_constraint(a, pltpu.HBM)
+                for k, a in enumerate(args)
             ]
         )
 
@@ -225,18 +227,36 @@
     for k in range(Y):
         at = (place[4] + k) % Y
         got = pl.ds((at % 2) * size, size)
-        total = home_ref[pl.ds(at * size, size), :] + jnp.where(at < 2, near_ref[got, :], far_ref[got, :])
-        for p in range(PARTS):
-            outs[p * Y + k][...] = total[:, p * each : (p + 1) * each]
+        outs[k][...] = home_ref[pl.ds(at * size, size), :each] + jnp.where(
+            at < 2, near_ref[got, :each], far_ref[got, :each]
+        )
+    half = near_ref.shape[0]
+    for out, at in ((outs[Y], place[5]), (outs[Y + 1], 1 - place[5])):
+        out[...] = home_ref[pl.ds(at * half, half), each:] + jnp.where(at == 0, near_ref[:, each:], far_ref[:, each:])
+
+
+def turn_kernel(place, kept, got, *outs):
+    size = outs[0].shape[0]
+    for k in range(Y):
+        at = pl.ds((place[4] + k) % Y * size, size)
+        outs[k][...] = kept[at, :] + got[at, :]
+
+
+def gather_kernel(place, *refs):
+    pieces, out = refs[:-1], refs[-1]
+    size = pieces[0].shape[0]
+    for k in range(Y):
+        out[pl.ds((place[4] + Y - k) % Y * size, size), :] = pieces[k][...]
 
 
 def assemble_kernel(place, *refs):
-    pieces, out = refs[:-1], refs[-1]
+    pieces, halves, out = refs[:Y], refs[Y:-1], refs[-1]
     size, each = pieces[0].shape
-    for p in range(PARTS):
-        for k in range(Y):
-            at = (place[4] + Y - k) % Y
-            out[pl.ds(at * size, size), p * each : (p + 1) * each] = pieces[p * Y + k][...]
+    for k in range(Y):
+        out[pl.ds((place[4] + Y - k) % Y * size, size), :each] = pieces[k][...]
+    size = halves[0].shape[0]
+    for half, at in ((halves[0], place[5]), (halves[1], 1 - place[5])):
+        out[pl.ds(at * size, size), each:] = half[...]
 
 
 def local(image, text):
@@ -245,7 +265,7 @@
     z, xl, core, y = (lax.axis_index(a) for a in ("z", "xl", "core", "y"))
     group = y * 2 + lax.axis_index("xh")
     half = rows // 2
-    place = jnp.stack([xl, core, z, group * part, y]).astype(jnp.int32)
+    place = jnp.stack([xl, core, z, group * part, y, lax.axis_index("xh")]).astype(jnp.int32)
     tall, steps = (STEP, width), rows // STEP
     table = [((2 * steps, STEP), F32, whole((2 * steps, STEP))), ((2, Z * part), F32, whole((2, Z * part)))]
 
@@ -276,6 +296,7 @@
             [SMEM] + ins + [whole(full)],
             outs,
             scratch=[pltpu.VMEM((width, columns), BF16)] * 3 + [pltpu.VMEM((1, columns), F32)] * 2,
+            free_in=(6,) if b else (2, 3),
         )(place, *args, texts)
         s.append(out[0])
         th.append(out[1])
@@ -313,6 +334,7 @@
         steps,
         [SMEM] + [rows_at((STEP, n)) for n in sizes] + fixed,
         [((rows, width), F32, rows_at(tall))] + kept,
+        free_out=(0,),
     )(place, *late)
     home, kept_home = home[0], home[1:]
 
@@ -324,6 +346,7 @@
             columns // STEP,
             [wide] * 4 + [whole((2 * rows, width))] * 2,
             outs,
+            free_out=(0,) if len(outs) == 1 else (),
         )(*kept_home[2 * b : 2 * b + 2], *kept_away[2 * b : 2 * b + 2], ih, im)
 
     piece = (columns // CUTS, width)
@@ -334,16 +357,24 @@
     g_text, *got = lax.optimization_barrier((g_text, *got))
     grad_text = lax.psum_scatter(g_text, "z", scatter_dimension=0, tiled=True)
 
-    quarter = rows // Y
-    mine = call(
-        pick_kernel, "pick", [((quarter, width // PARTS), F32)] * (PARTS * Y), 3, scalars=True, cost=PICK
+    def over_y(pieces):
+        return pieces[0] + sum(lax.ppermute(pieces[k], "y", ring(Y, k)) for k in (1, 3, 2))
+
+    def to_y(own):
+        return [own] + [lax.ppermute(own, "y", ring(Y, k)) for k in (1, 2, 3)]
+
+    each = width - WIDE
+    picked = call(
+        pick_kernel, "pick", [((rows // Y, each), F32)] * Y + [((half, WIDE), F32)] * 2, 3, scalars=True, cost=PICK
     )(place, home, *got)
-    pieces = []
-    for p in range(PARTS):
-        own = mine[p * Y] + sum(lax.ppermute(mine[p * Y + k], "y", ring(Y, k)) for k in (1, 3, 2))
-        own = own + flip(own, "xh", 2, 1)
-        pieces += [own] + [lax.ppermute(own, "y", ring(Y, k)) for k in (1, 2, 3)]
-    (out,) = call(assemble_kernel, "assemble", [((rows, width), F32)], PARTS * Y, scalars=True)(place, *pieces)
+    got, first = lax.optimization_barrier((flip(picked[Y + 1], "xh", 2, 1), over_y(picked[:Y])))
+    terms = call(turn_kernel, "turn", [((half // Y, WIDE), F32)] * Y, 2, scalars=True)(place, picked[Y], got)
+    second, first = lax.optimization_barrier((over_y(terms), first + flip(first, "xh", 2, 1)))
+    second = to_y(second)
+    (second,) = call(gather_kernel, "gather", [((half, WIDE), F32)], Y, scalars=True)(place, *second)
+    (out,) = call(assemble_kernel, "assemble", [((rows, width), F32)], Y + 2, scalars=True)(
+        place, *to_y(first), second, flip(second, "xh", 2, 1)
+    )
     return out, grad_text
 
 

time: 217 us -> 207 us (0.954); the launches traced: 215 us -> 207 us
  waiting for transfers between devices: 90.9 us -> 80.9 us
  starting transfers between devices: 36.5 us -> 43 us
  local copies, waits for them, and re-layouts: 7.69 us -> 5.43 us
    ppermute x12, waiting for transfers between devices: 35.7 us -> 28.4 us  [the longest x6 14.5 us: over_y(): lax.ppermute(pieces[k], 'y', ring(Y, k))]
    ppermute x21 -> x22, starting transfers between devices: 18.9 us -> 24.7 us  [flip(): return lax.ppermute(a, axis, [(i, i ^ bit) for i in range(size)])]
    unnamed x8 -> x4, local copies, waits for them, and re-layouts: 4.5 us -> 2.2 us
    pallas_call x8 -> x10, Pallas kernels: 62.1 us -> 60.3 us  [the longest x6 55.4 us: apply(): run(*[a if k == 0 and ins[0] is SMEM or k in free_in else pltpu.with_memo...]
    ppermute x21 -> x22, waiting for transfers between devices: 14.8 us -> 13 us  [flip(): return lax.ppermute(a, axis, [(i, i ^ bit) for i in range(size)])]
  transfers between devices with their start and end apart: 37 -> 38, of which waited for: 20 -> 23; matrix products, arithmetic and copies ran while one was open for 2% -> 2% of each run, Pallas kernels for 20% -> 20%
where the time goes in v3:
time: 207 us
  waiting for transfers between devices  80.9 us (39%)
  Pallas kernels  61.8 us (30%)
  starting transfers between devices  43 us (21%)
  between operations  14.2 us (7%)
  local copies, waits for them, and re-layouts  5.43 us (3%)
    pallas_call x6, Pallas kernels, apply(): run(*[a if k == 0 and ins[0] is SMEM or k in free_in else pltpu.with_memo...  55.4 us
    ppermute x22, starting transfers between devices, flip(): return lax.ppermute(a, axis, [(i, i ^ bit) for i in range(size)])  24.7 us
    ppermute x2, waiting for transfers between devices, swap_x(): return (flip(near, 'xl', 2, 1), lax.ppermute(far, ('xl', 'xh'), x_other()))  21.6 us
    all_gather x1, waiting for transfers between devices, local(): line = lax.all_gather(text, 'z', axis=0, tiled=True)  17.2 us
    ppermute x6, waiting for transfers between devices, over_y(): lax.ppermute(pieces[k], 'y', ring(Y, k))  14.5 us
    ppermute x6, waiting for transfers between devices, to_y(): return [own] + [lax.ppermute(own, 'y', ring(Y, k)) for k in (1, 2, 3)]  13.9 us
    ppermute x22, waiting for transfers between devices, flip(): return lax.ppermute(a, axis, [(i, i ^ bit) for i in range(size)])  13 us
    ppermute x6, starting transfers between devices, over_y(): lax.ppermute(pieces[k], 'y', ring(Y, k))  7.76 us
  transfers between devices with their start and end apart: 38, of which 23 were waited for; matrix products, arithmetic and copies ran while one was open for 2% of the time, Pallas kernels for 20%

profile of v3, /device:TPU:2, one launch (start us, length us, event | category | flops | bytes accessed | tf_op | source)
XLA Modules:
  0.0 206.9 jit_solution(1809186370210919539)
XLA Ops:
  7.2 0.7 all-gather.2.cloned.1.call-update
  7.9 1.7 fusion
  9.7 1.6 collective-permute-start.1
  11.3 1.8 collective-permute-start
  13.1 21.6 %collective-permute-done.1.refs_2_ = f32[256,1024]{1,0:T(8,128)S(1)} collective-permute-done((f32[256,1024]{1,0:T(8,128)S(1)}, f32[256,1024]{1,0:T(8,128)S(1)}, u32[]{:S(2)}, u32[]{:S(2)}) %collective-permute-start.1) | collective-permute-done | bytes 1048608 | tf_op jit(solution)/shard_map/ppermute | solution.py:89
  34.7 1.3 collective-permute-done.refs_1_
  35.9 1.0 copy-done
  36.9 17.2 %all-gather.2.cloned.1.call-done.refs_3_ = f32[512,1024]{1,0:T(8,128)} async-done(((f32[64,1024]{1,0:T(8,128)}), f32[512,1024]{1,0:T(8,128)}) %all-gather.2.cloned.1.call-update) | async-done | bytes 2097168 | tf_op jit(solution)/shard_map/all_gather | solution.py:273
  54.2 1.2 copy-done.1
  55.4 13.7 %scores.2 = (f32[1024,512]{1,0:T(8,128)}, bf16[512,1024]{1,0:T(8,128)(2,1)}, bf16[512,1024]{1,0:T(8,128)(2,1)}, f32[4,256]{1,0:T(4,128)}, f32[2,512]{1,0:T(2,128...) custom-call(s32[6]{0:T(128)S(1)} %stack.27.place, f32[512,1024]{1,0:T(8,128)} %refs_0_.1, ...), custom_call_target="tpu_custom_call" | custom-call | flops 1000 | bytes 1000 | tf_op jit(solution)/shard_map/scores/pallas_call | solution.py:54
  69.1 12.2 %scores.3 = (f32[1024,512]{1,0:T(8,128)}, bf16[512,1024]{1,0:T(8,128)(2,1)}, bf16[512,1024]{1,0:T(8,128)(2,1)}, f32[4,256]{1,0:T(4,128)}, f32[2,512]{1,0:T(2,128)}) custom-call(s32[6]{0:T(128)S(1)} %stack.27.place, bf16[1024,1024]{1,0:T(8,128)(2,1)} %get-tuple-element.66.refs_0_.ih, bf16[1024,1024]{1,0:T(8,128)(2,1)} %get-tuple-element.67.refs_1_.im, ...), custom_call_target="tpu_custom_call" | custom-call | flops 1000 | bytes 1000 | tf_op jit(solution)/shard_map/scores/pallas_call | solution.py:54
  81.3 0.7 reshape.10
  82.1 0.5 collective-permute-start.7
  82.6 1.5 collective-permute-start.3
  84.1 1.1 collective-permute-start.8
  85.2 1.2 collective-permute-done.3
  86.4 0.7 log_add_fusion.7
  87.1 3.1 %collective-permute-start.4 = (f32[4,256]{1,0:T(4,128)S(1)}, f32[4,256]{1,0:T(4,128)S(1)}, u32[]{:S(2)}, u32[]{:S(2)}) collective-permute-start(f32[4,256]{1,0:T(4,128)S(1)} %log_add_fusion.7), channel_id=1, source_target_pairs={{0,4},{2,6},{4,0},{6,2},{1,5},{3,7},{5,1},{7,3},{8,12},{10,14},{12... | collective-permute-start | bytes 12296 | tf_op jit(solution)/shard_map/ppermute | solution.py:77
  90.2 1.1 collective-permute-start.9
  91.3 1.0 collective-permute-done.4
  92.3 0.6 collective-permute-start.5
  93.0 1.9 collective-permute-done.9
  94.9 2.8 %collective-permute-start.10 = (f32[2,8,64]{2,1,0:T(8,128)S(1)}, f32[2,8,64]{2,1,0:T(8,128)S(1)}, u32[]{:S(2)}, u32[]{:S(2)}) collective-permute-start(f32[2,8,64]{2,1,0:T(8,128)S(1)} %log_add_fusion.1), channel_id=1, source_target_pairs={{0,128},{32,160},{64,192},{96,224},{128,0},{160,32},{192,64},{224,... | collective-permute-start | bytes 12296 | tf_op jit(solution)/shard_map/ppermute | solution.py:77
  97.7 2.5 %collective-permute-start.6 = (f32[4,256]{1,0:T(4,128)S(1)}, f32[4,256]{1,0:T(4,128)S(1)}, u32[]{:S(2)}, u32[]{:S(2)}) collective-permute-start(f32[4,256]{1,0:T(4,128)S(1)} %log_add_fusion.5), channel_id=1, source_target_pairs={{0,1},{1,0},{2,3},{3,2},{4,5},{5,4},{6,7},{7,6},{8,9},{9,8},{10,11... | collective-permute-start | bytes 12296 | tf_op jit(solution)/shard_map/ppermute | solution.py:77
  100.2 2.3 %collective-permute-done.10 = f32[2,8,64]{2,1,0:T(8,128)S(1)} collective-permute-done((f32[2,8,64]{2,1,0:T(8,128)S(1)}, f32[2,8,64]{2,1,0:T(8,128)S(1)}, u32[]{:S(2)}, u32[]{:S(2)}) %collective-permute-start.10) | collective-permute-done | bytes 4128 | tf_op jit(solution)/shard_map/ppermute | solution.py:77
  102.5 0.7 reshape.11.c_ref
  103.2 0.6 log_add_fusion.4.r_ref
  103.8 8.6 %away.1 = (f32[256,1024]{1,0:T(8,128)}, f32[256,1024]{1,0:T(8,128)}, bf16[512,512]{1,0:T(8,128)(2,1)}, bf16[512,512]{1,0:T(8,128)(2,1)}, bf16[512,512]{1,0:T(8,128)(2,1)}, /*index=5*/bf16[512,512]{1,0:T(8,128)(2,1)}) custom-call(s32[6]{0:T(128)S(1)} %stack.27.place, f32[1024,512]{1,0:T(8,128)} %get-tuple-element.79.s1, f32[1024,512]{1,0:T(8,128)} %get-tuple-element.80.s2, ...), custom_call_target="tpu_custom_call" | custom-call | flops 1000 | bytes 1000 | tf_op jit(solution)/shard_map/away/pallas_call | solution.py:54
  112.4 1.5 collective-permute-start.20
  113.9 1.9 collective-permute-start.19
  115.8 6.9 %home.1 = (f32[512,1024]{1,0:T(8,128)S(1)}, bf16[512,512]{1,0:T(8,128)(2,1)}, bf16[512,512]{1,0:T(8,128)(2,1)}, bf16[512,512]{1,0:T(8,128)(2,1)}, bf16[512,512]{1,0:T(8,128)(2,1)}) custom-call(s32[6]{0:T(128)S(1)} %stack.27.place, f32[1024,512]{1,0:T(8,128)} %get-tuple-element.79.s1, f32[1024,512]{1,0:T(8,128)} %get-tuple-element.80.s2, ...), custom_call_target="tpu_custom_call" | custom-call | flops 1000 | bytes 1000 | tf_op jit(solution)/shard_map/home/pallas_call | solution.py:54
  122.7 7.8 %text_other.1 = (f32[64,1024]{1,0:T(8,128)}, f32[64,1024]{1,0:T(8,128)}, f32[64,1024]{1,0:T(8,128)}, f32[64,1024]{1,0:T(8,128)}, f32[64,1024]{1,0:T(8,128)}, /*i...) custom-call(bf16[512,512]{1,0:T(8,128)(2,1)} %get-tuple-element.92.home_h, ...), custom_call_target="tpu_custom_call" | custom-call | flops 1000 | bytes 1000 | tf_op jit(solution)/shard_map/text_other/pallas_call | solution.py:54
  130.5 0.5 collective-permute-start.12
  131.1 1.1 collective-permute-done.11.refs_0_
  133.1 0.9 collective-permute-done.14.refs_3_
  134.5 6.3 %text_own.1.own = f32[512,1024]{1,0:T(8,128)S(1)} custom-call(bf16[512,512]{1,0:T(8,128)(2,1)} %get-tuple-element.88.home_h, bf16[512,512]{1,0:T(8,128)(2,1)} %get-tuple-element.89.home_l, bf16[512,512]{1,0:T(8,128)(2,1)} %get-tuple-element.90.away_h, bf16[512,512]{1,0:T(8,128)(2,1)} %get-tuple-element.91.away_l, ...), custom_call_target="tpu_custom_call" | custom-call | flops 1000 | bytes 1000 | tf_op jit(solution)/shard_map/text_own/pallas_call | solution.py:54
  140.8 1.5 collect.1
  142.4 1.7 pick.1
  144.1 0.3 collective-permute-start.21
  144.4 0.6 collective-permute-start.22
  144.9 2.7 %collective-permute-start.23 = (f32[128,512]{1,0:T(8,128)S(1)}, f32[128,512]{1,0:T(8,128)S(1)}, u32[]{:S(2)}, u32[]{:S(2)}) collective-permute-start(f32[128,512]{1,0:T(8,128)S(1)} %get-tuple-element.111), channel_id=1, source_target_pairs={{0,6},{2,0},{4,2},{6,4},{1,7},{3,1},{5,3},{7,5},{8,14},{10,8},{12,... | collective-permute-start | bytes 786440 | tf_op jit(solution)/shard_map/ppermute | solution.py:361
  147.7 11.9 %collective-permute-done.22 = f32[128,512]{1,0:T(8,128)S(1)} collective-permute-done((f32[128,512]{1,0:T(8,128)S(1)}, f32[128,512]{1,0:T(8,128)S(1)}, u32[]{:S(2)}, u32[]{:S(2)}) %collective-permute-start.22) | collective-permute-done | bytes 262176 | tf_op jit(solution)/shard_map/ppermute | solution.py:361
  159.9 0.6 turn.1
  160.5 0.8 collective-permute-start.25
  161.3 2.5 %collective-permute-start.26 = (f32[64,512]{1,0:T(8,128)S(1)}, f32[64,512]{1,0:T(8,128)S(1)}, u32[]{:S(2)}, u32[]{:S(2)}) collective-permute-start(f32[64,512]{1,0:T(8,128)S(1)} %get-tuple-element.116), channel_id=1, source_target_pairs={{0,6},{2,0},{4,2},{6,4},{1,7},{3,1},{5,3},{7,5},{8,14},{10,8},{12,... | collective-permute-start | bytes 393224 | tf_op jit(solution)/shard_map/ppermute | solution.py:361
  163.8 1.1 collective-permute-start.27
  164.9 3.2 %collective-permute-start.28 = (f32[128,512]{1,0:T(8,128)S(1)}, f32[128,512]{1,0:T(8,128)S(1)}, u32[]{:S(2)}, u32[]{:S(2)}) collective-permute-start(f32[128,512]{1,0:T(8,128)S(1)} %add_add_fusion), channel_id=1, source_target_pairs={{0,1},{1,0},{2,3},{3,2},{4,5},{5,4},{6,7},{7,6},{8,9},{9,8},{10,11... | collective-permute-start | bytes 786440 | tf_op jit(solution)/shard_map/ppermute | solution.py:77
  168.0 0.9 collective-permute-done.26
  168.9 1.7 collective-permute-done.27
  170.7 2.5 %collective-permute-done.28 = f32[128,512]{1,0:T(8,128)S(1)} collective-permute-done((f32[128,512]{1,0:T(8,128)S(1)}, f32[128,512]{1,0:T(8,128)S(1)}, u32[]{:S(2)}, u32[]{:S(2)}) %collective-permute-start.28) | collective-permute-done | bytes 262176 | tf_op jit(solution)/shard_map/ppermute | solution.py:77
  173.3 1.3 collective-permute-start.34
  174.6 2.0 collective-permute-start.33
  176.5 0.9 collective-permute-start.32
  177.4 1.1 collective-permute-done.34.refs_3_
  178.5 2.5 %collective-permute-done.33.refs_2_ = f32[64,512]{1,0:T(8,128)S(1)} collective-permute-done((f32[64,512]{1,0:T(8,128)S(1)}, f32[64,512]{1,0:T(8,128)S(1)}, u32[]{:S(2)}, u32[]{:S(2)}) %collective-permute-start.33) | collective-permute-done | bytes 131104 | tf_op jit(solution)/shard_map/ppermute | solution.py:364
  181.0 1.7 collective-permute-done.32.refs_1_
  182.7 0.6 gather.1.refs_4_
  183.3 3.1 %collective-permute-start.35 = (f32[256,512]{1,0:T(8,128)S(1)}, f32[256,512]{1,0:T(8,128)S(1)}, u32[]{:S(2)}, u32[]{:S(2)}) collective-permute-start(f32[256,512]{1,0:T(8,128)S(1)} %gather.1.refs_4_), channel_id=1, source_target_pairs={{0,1},{1,0},{2,3},{3,2},{4,5},{5,4},{6,7},{7,6},{8,9},{9,8},{10,11... | collective-permute-start | bytes 1572872 | tf_op jit(solution)/shard_map/ppermute | solution.py:77
  186.6 2.0 collective-permute-start.30
  188.6 0.9 collective-permute-start.29
  189.5 3.6 %collective-permute-done.31.refs_3_ = f32[128,512]{1,0:T(8,128)S(1)} collective-permute-done((f32[128,512]{1,0:T(8,128)S(1)}, f32[128,512]{1,0:T(8,128)S(1)}, u32[]{:S(2)}, u32[]{:S(2)}) %collective-permute-start.31) | collective-permute-done | bytes 262176 | tf_op jit(solution)/shard_map/ppermute | solution.py:364
  193.1 2.2 %collective-permute-done.30.refs_2_ = f32[128,512]{1,0:T(8,128)S(1)} collective-permute-done((f32[128,512]{1,0:T(8,128)S(1)}, f32[128,512]{1,0:T(8,128)S(1)}, u32[]{:S(2)}, u32[]{:S(2)}) %collective-permute-start.30) | collective-permute-done | bytes 262176 | tf_op jit(solution)/shard_map/ppermute | solution.py:364
  195.3 2.7 %collective-permute-done.29.refs_1_ = f32[128,512]{1,0:T(8,128)S(1)} collective-permute-done((f32[128,512]{1,0:T(8,128)S(1)}, f32[128,512]{1,0:T(8,128)S(1)}, u32[]{:S(2)}, u32[]{:S(2)}) %collective-permute-start.29) | collective-permute-done | bytes 262176 | tf_op jit(solution)/shard_map/ppermute | solution.py:364
  198.1 2.0 assemble.1
  (44 shorter events, 2.4 us)
Async XLA Ops:
  7.2 47.0 %all-gather.2.cloned.1.call-start = ((), (), s32[]{:S(2)}) async-start(), calls=%async_computation.1 | async-start | bytes 2359296 | tf_op jit(solution)/shard_map/all_gather | solution.py:273
  7.9 192.2 %reduce-scatter.2.cloned.1.call-start = ((), (), s32[]{:S(2)}) async-start(), calls=%async_computation.2 | async-start | bytes 2359296 | tf_op jit(solution)/shard_map/reduce_scatter | solution.py:358
  9.7 25.0 %collective-permute-start.1 = (f32[256,1024]{1,0:T(8,128)S(1)}, f32[256,1024]{1,0:T(8,128)S(1)}, u32[]{:S(2)}, u32[]{:S(2)}) collective-permute-start(f32[256,1024]{1,0:T(8,128)S(1)} %get-tuple-element.122), channel_id=1, source_target_pairs={{0,17},{16,1},{1,16},{17,0},{2,19},{18,3},{3,18},{19,2},{4,21},{20... | collective-permute-start | bytes 3145736 | tf_op jit(solution)/shard_map/ppermute | solution.py:89
  11.3 24.7 %collective-permute-start = (f32[256,1024]{1,0:T(8,128)S(1)}, f32[256,1024]{1,0:T(8,128)S(1)}, u32[]{:S(2)}, u32[]{:S(2)}) collective-permute-start(f32[256,1024]{1,0:T(8,128)S(1)} %get-tuple-element.123), channel_id=1, source_target_pairs={{0,16},{16,0},{1,17},{17,1},{2,18},{18,2},{3,19},{19,3},{4,20},{20... | collective-permute-start | bytes 3145736 | tf_op jit(solution)/shard_map/ppermute | solution.py:77
  35.9 1.0 copy-start
  54.1 15.0 %collective-permute-start.2 = (f32[512,1024]{1,0:T(8,128)}, f32[512,1024]{1,0:T(8,128)S(1)}, u32[]{:S(2)}, u32[]{:S(2)}) collective-permute-start(f32[512,1024]{1,0:T(8,128)} %all-gather.2.cloned.1.call-done.refs_3_), channel_id=1, source_target_pairs={{0,8},{8,0},{1,9},{9,1},{2,10},{10,2},{3,11},{11,3},{4,12},{12,4},... | collective-permute-start | bytes 6291464 | tf_op jit(solution)/shard_map/ppermute | solution.py:77
  54.2 1.2 copy-start.1
  82.1 2.0 collective-permute-start.7
  82.6 3.8 %collective-permute-start.3 = (f32[4,256]{1,0:T(4,128)}, f32[4,256]{1,0:T(4,128)S(1)}, u32[]{:S(2)}, u32[]{:S(2)}) collective-permute-start(f32[4,256]{1,0:T(4,128)} %get-tuple-element.72), channel_id=1, source_target_pairs={{0,2},{2,0},{4,6},{6,4},{1,3},{3,1},{5,7},{7,5},{8,10},{10,8},{12,... | collective-permute-start | bytes 12296 | tf_op jit(solution)/shard_map/ppermute | solution.py:77
  84.1 6.1 %collective-permute-start.8 = (f32[2,8,64]{2,1,0:T(8,128)S(1)}, f32[2,8,64]{2,1,0:T(8,128)S(1)}, u32[]{:S(2)}, u32[]{:S(2)}) collective-permute-start(f32[2,8,64]{2,1,0:T(8,128)S(1)} %log_add_fusion.3), channel_id=1, source_target_pairs={{0,32},{32,0},{64,96},{96,64},{128,160},{160,128},{192,224},{224,1... | collective-permute-start | bytes 12296 | tf_op jit(solution)/shard_map/ppermute | solution.py:77
  87.1 5.2 %collective-permute-start.4 = (f32[4,256]{1,0:T(4,128)S(1)}, f32[4,256]{1,0:T(4,128)S(1)}, u32[]{:S(2)}, u32[]{:S(2)}) collective-permute-start(f32[4,256]{1,0:T(4,128)S(1)} %log_add_fusion.7), channel_id=1, source_target_pairs={{0,4},{2,6},{4,0},{6,2},{1,5},{3,7},{5,1},{7,3},{8,12},{10,14},{12... | collective-permute-start | bytes 12296 | tf_op jit(solution)/shard_map/ppermute | solution.py:77
  90.2 4.6 %collective-permute-start.9 = (f32[2,8,64]{2,1,0:T(8,128)S(1)}, f32[2,8,64]{2,1,0:T(8,128)S(1)}, u32[]{:S(2)}, u32[]{:S(2)}) collective-permute-start(f32[2,8,64]{2,1,0:T(8,128)S(1)} %log_add_fusion.2), channel_id=1, source_target_pairs={{0,64},{32,96},{64,0},{96,32},{128,192},{160,224},{192,128},{224,1... | collective-permute-start | bytes 12296 | tf_op jit(solution)/shard_map/ppermute | solution.py:77
  92.3 5.4 %collective-permute-start.5 = (f32[4,256]{1,0:T(4,128)S(1)}, f32[4,256]{1,0:T(4,128)S(1)}, u32[]{:S(2)}, u32[]{:S(2)}) collective-permute-start(f32[4,256]{1,0:T(4,128)S(1)} %log_add_fusion.6), channel_id=1, source_target_pairs={{0,16},{16,0},{1,17},{17,1},{2,18},{18,2},{3,19},{19,3},{4,20},{20... | collective-permute-start | bytes 12296 | tf_op jit(solution)/shard_map/ppermute | solution.py:77
  94.9 7.6 %collective-permute-start.10 = (f32[2,8,64]{2,1,0:T(8,128)S(1)}, f32[2,8,64]{2,1,0:T(8,128)S(1)}, u32[]{:S(2)}, u32[]{:S(2)}) collective-permute-start(f32[2,8,64]{2,1,0:T(8,128)S(1)} %log_add_fusion.1), channel_id=1, source_target_pairs={{0,128},{32,160},{64,192},{96,224},{128,0},{160,32},{192,64},{224,... | collective-permute-start | bytes 12296 | tf_op jit(solution)/shard_map/ppermute | solution.py:77
  97.7 5.5 %collective-permute-start.6 = (f32[4,256]{1,0:T(4,128)S(1)}, f32[4,256]{1,0:T(4,128)S(1)}, u32[]{:S(2)}, u32[]{:S(2)}) collective-permute-start(f32[4,256]{1,0:T(4,128)S(1)} %log_add_fusion.5), channel_id=1, source_target_pairs={{0,1},{1,0},{2,3},{3,2},{4,5},{5,4},{6,7},{7,6},{8,9},{9,8},{10,11... | collective-permute-start | bytes 12296 | tf_op jit(solution)/shard_map/ppermute | solution.py:77
  112.4 30.0 %collective-permute-start.20 = (f32[256,1024]{1,0:T(8,128)}, f32[256,1024]{1,0:T(8,128)S(1)}, u32[]{:S(2)}, u32[]{:S(2)}) collective-permute-start(f32[256,1024]{1,0:T(8,128)} %get-tuple-element.104), channel_id=1, source_target_pairs={{0,17},{16,1},{1,16},{17,0},{2,19},{18,3},{3,18},{19,2},{4,21},{20... | collective-permute-start | bytes 3145736 | tf_op jit(solution)/shard_map/ppermute | solution.py:89
  113.9 28.4 %collective-permute-start.19 = (f32[256,1024]{1,0:T(8,128)}, f32[256,1024]{1,0:T(8,128)}, u32[]{:S(2)}, u32[]{:S(2)}) collective-permute-start(f32[256,1024]{1,0:T(8,128)} %get-tuple-element.78), channel_id=1, source_target_pairs={{0,16},{16,0},{1,17},{17,1},{2,18},{18,2},{3,19},{19,3},{4,20},{20... | collective-permute-start | bytes 3145736 | tf_op jit(solution)/shard_map/ppermute | solution.py:77
  130.5 1.7 collective-permute-start.11
  130.5 2.1 %collective-permute-start.12 = (f32[64,1024]{1,0:T(8,128)}, f32[64,1024]{1,0:T(8,128)S(1)}, u32[]{:S(2)}, u32[]{:S(2)}) collective-permute-start(f32[64,1024]{1,0:T(8,128)} %get-tuple-element.97), channel_id=1, source_target_pairs={{0,8},{8,0},{1,9},{9,1},{2,10},{10,2},{3,11},{11,3},{4,12},{12,4},... | collective-permute-start | bytes 786440 | tf_op jit(solution)/shard_map/ppermute | solution.py:77
  131.0 2.0 collective-permute-start.13
  132.2 1.7 collective-permute-start.14
  132.6 1.7 collective-permute-start.15
  133.0 7.8 %collective-permute-start.16 = (f32[64,1024]{1,0:T(8,128)}, f32[64,1024]{1,0:T(8,128)S(1)}, u32[]{:S(2)}, u32[]{:S(2)}) collective-permute-start(f32[64,1024]{1,0:T(8,128)} %get-tuple-element.101), channel_id=1, source_target_pairs={{0,8},{8,0},{1,9},{9,1},{2,10},{10,2},{3,11},{11,3},{4,12},{12,4},... | collective-permute-start | bytes 786440 | tf_op jit(solution)/shard_map/ppermute | solution.py:77
  134.0 6.8 %collective-permute-start.17 = (f32[64,1024]{1,0:T(8,128)}, f32[64,1024]{1,0:T(8,128)S(1)}, u32[]{:S(2)}, u32[]{:S(2)}) collective-permute-start(f32[64,1024]{1,0:T(8,128)} %get-tuple-element.102), channel_id=1, source_target_pairs={{0,8},{8,0},{1,9},{9,1},{2,10},{10,2},{3,11},{11,3},{4,12},{12,4},... | collective-permute-start | bytes 786440 | tf_op jit(solution)/shard_map/ppermute | solution.py:77
  134.3 6.5 %collective-permute-start.18 = (f32[64,1024]{1,0:T(8,128)}, f32[64,1024]{1,0:T(8,128)S(1)}, u32[]{:S(2)}, u32[]{:S(2)}) collective-permute-start(f32[64,1024]{1,0:T(8,128)} %get-tuple-element.103), channel_id=1, source_target_pairs={{0,8},{8,0},{1,9},{9,1},{2,10},{10,2},{3,11},{11,3},{4,12},{12,4},... | collective-permute-start | bytes 786440 | tf_op jit(solution)/shard_map/ppermute | solution.py:77
  144.1 15.8 %collective-permute-start.21 = (f32[256,512]{1,0:T(8,128)S(1)}, f32[256,512]{1,0:T(8,128)S(1)}, u32[]{:S(2)}, u32[]{:S(2)}) collective-permute-start(f32[256,512]{1,0:T(8,128)S(1)} %get-tuple-element.108), channel_id=1, source_target_pairs={{0,1},{1,0},{2,3},{3,2},{4,5},{5,4},{6,7},{7,6},{8,9},{9,8},{10,11... | collective-permute-start | bytes 1572872 | tf_op jit(solution)/shard_map/ppermute | solution.py:77
  144.4 15.3 %collective-permute-start.22 = (f32[128,512]{1,0:T(8,128)S(1)}, f32[128,512]{1,0:T(8,128)S(1)}, u32[]{:S(2)}, u32[]{:S(2)}) collective-permute-start(f32[128,512]{1,0:T(8,128)S(1)} %get-tuple-element.110), channel_id=1, source_target_pairs={{0,2},{2,4},{4,6},{6,0},{1,3},{3,5},{5,7},{7,1},{8,10},{10,12},{12... | collective-permute-start | bytes 786440 | tf_op jit(solution)/shard_map/ppermute | solution.py:361
  144.9 14.7 %collective-permute-start.23 = (f32[128,512]{1,0:T(8,128)S(1)}, f32[128,512]{1,0:T(8,128)S(1)}, u32[]{:S(2)}, u32[]{:S(2)}) collective-permute-start(f32[128,512]{1,0:T(8,128)S(1)} %get-tuple-element.111), channel_id=1, source_target_pairs={{0,6},{2,0},{4,2},{6,4},{1,7},{3,1},{5,3},{7,5},{8,14},{10,8},{12,... | collective-permute-start | bytes 786440 | tf_op jit(solution)/shard_map/ppermute | solution.py:361
  147.6 12.1 %collective-permute-start.24 = (f32[128,512]{1,0:T(8,128)S(1)}, f32[128,512]{1,0:T(8,128)S(1)}, u32[]{:S(2)}, u32[]{:S(2)}) collective-permute-start(f32[128,512]{1,0:T(8,128)S(1)} %get-tuple-element.112), channel_id=1, source_target_pairs={{0,4},{2,6},{4,0},{6,2},{1,5},{3,7},{5,1},{7,3},{8,12},{10,14},{12... | collective-permute-start | bytes 786440 | tf_op jit(solution)/shard_map/ppermute | solution.py:361
  160.5 7.6 %collective-permute-start.25 = (f32[64,512]{1,0:T(8,128)S(1)}, f32[64,512]{1,0:T(8,128)S(1)}, u32[]{:S(2)}, u32[]{:S(2)}) collective-permute-start(f32[64,512]{1,0:T(8,128)S(1)} %get-tuple-element.115), channel_id=1, source_target_pairs={{0,2},{2,4},{4,6},{6,0},{1,3},{3,5},{5,7},{7,1},{8,10},{10,12},{12... | collective-permute-start | bytes 393224 | tf_op jit(solution)/shard_map/ppermute | solution.py:361
  161.3 7.6 %collective-permute-start.26 = (f32[64,512]{1,0:T(8,128)S(1)}, f32[64,512]{1,0:T(8,128)S(1)}, u32[]{:S(2)}, u32[]{:S(2)}) collective-permute-start(f32[64,512]{1,0:T(8,128)S(1)} %get-tuple-element.116), channel_id=1, source_target_pairs={{0,6},{2,0},{4,2},{6,4},{1,7},{3,1},{5,3},{7,5},{8,14},{10,8},{12,... | collective-permute-start | bytes 393224 | tf_op jit(solution)/shard_map/ppermute | solution.py:361
  163.8 6.8 %collective-permute-start.27 = (f32[64,512]{1,0:T(8,128)S(1)}, f32[64,512]{1,0:T(8,128)S(1)}, u32[]{:S(2)}, u32[]{:S(2)}) collective-permute-start(f32[64,512]{1,0:T(8,128)S(1)} %get-tuple-element.117), channel_id=1, source_target_pairs={{0,4},{2,6},{4,0},{6,2},{1,5},{3,7},{5,1},{7,3},{8,12},{10,14},{12... | collective-permute-start | bytes 393224 | tf_op jit(solution)/shard_map/ppermute | solution.py:361
  164.9 8.3 %collective-permute-start.28 = (f32[128,512]{1,0:T(8,128)S(1)}, f32[128,512]{1,0:T(8,128)S(1)}, u32[]{:S(2)}, u32[]{:S(2)}) collective-permute-start(f32[128,512]{1,0:T(8,128)S(1)} %add_add_fusion), channel_id=1, source_target_pairs={{0,1},{1,0},{2,3},{3,2},{4,5},{5,4},{6,7},{7,6},{8,9},{9,8},{10,11... | collective-permute-start | bytes 786440 | tf_op jit(solution)/shard_map/ppermute | solution.py:77
  173.3 5.2 %collective-permute-start.34 = (f32[64,512]{1,0:T(8,128)S(1)}, f32[64,512]{1,0:T(8,128)S(1)}, u32[]{:S(2)}, u32[]{:S(2)}) collective-permute-start(f32[64,512]{1,0:T(8,128)S(1)} %add_add_fusion.1.refs_0_), channel_id=1, source_target_pairs={{0,6},{2,0},{4,2},{6,4},{1,7},{3,1},{5,3},{7,5},{8,14},{10,8},{12,... | collective-permute-start | bytes 393224 | tf_op jit(solution)/shard_map/ppermute | solution.py:364
  174.6 6.5 %collective-permute-start.33 = (f32[64,512]{1,0:T(8,128)S(1)}, f32[64,512]{1,0:T(8,128)S(1)}, u32[]{:S(2)}, u32[]{:S(2)}) collective-permute-start(f32[64,512]{1,0:T(8,128)S(1)} %add_add_fusion.1.refs_0_), channel_id=1, source_target_pairs={{0,4},{2,6},{4,0},{6,2},{1,5},{3,7},{5,1},{7,3},{8,12},{10,14},{12... | collective-permute-start | bytes 393224 | tf_op jit(solution)/shard_map/ppermute | solution.py:364
  176.5 6.2 %collective-permute-start.32 = (f32[64,512]{1,0:T(8,128)S(1)}, f32[64,512]{1,0:T(8,128)S(1)}, u32[]{:S(2)}, u32[]{:S(2)}) collective-permute-start(f32[64,512]{1,0:T(8,128)S(1)} %add_add_fusion.1.refs_0_), channel_id=1, source_target_pairs={{0,2},{2,4},{4,6},{6,0},{1,3},{3,5},{5,7},{7,1},{8,10},{10,12},{12... | collective-permute-start | bytes 393224 | tf_op jit(solution)/shard_map/ppermute | solution.py:364
  183.3 14.7 %collective-permute-start.35 = (f32[256,512]{1,0:T(8,128)S(1)}, f32[256,512]{1,0:T(8,128)S(1)}, u32[]{:S(2)}, u32[]{:S(2)}) collective-permute-start(f32[256,512]{1,0:T(8,128)S(1)} %gather.1.refs_4_), channel_id=1, source_target_pairs={{0,1},{1,0},{2,3},{3,2},{4,5},{5,4},{6,7},{7,6},{8,9},{9,8},{10,11... | collective-permute-start | bytes 1572872 | tf_op jit(solution)/shard_map/ppermute | solution.py:77
  186.4 6.7 %collective-permute-start.31 = (f32[128,512]{1,0:T(8,128)S(1)}, f32[128,512]{1,0:T(8,128)S(1)}, u32[]{:S(2)}, u32[]{:S(2)}) collective-permute-start(f32[128,512]{1,0:T(8,128)S(1)} %add.97.refs_0_), channel_id=1, source_target_pairs={{0,6},{2,0},{4,2},{6,4},{1,7},{3,1},{5,3},{7,5},{8,14},{10,8},{12,... | collective-permute-start | bytes 786440 | tf_op jit(solution)/shard_map/ppermute | solution.py:364
  186.6 8.7 %collective-permute-start.30 = (f32[128,512]{1,0:T(8,128)S(1)}, f32[128,512]{1,0:T(8,128)S(1)}, u32[]{:S(2)}, u32[]{:S(2)}) collective-permute-start(f32[128,512]{1,0:T(8,128)S(1)} %add.97.refs_0_), channel_id=1, source_target_pairs={{0,4},{2,6},{4,0},{6,2},{1,5},{3,7},{5,1},{7,3},{8,12},{10,14},{12... | collective-permute-start | bytes 786440 | tf_op jit(solution)/shard_map/ppermute | solution.py:364
  188.6 9.4 %collective-permute-start.29 = (f32[128,512]{1,0:T(8,128)S(1)}, f32[128,512]{1,0:T(8,128)S(1)}, u32[]{:S(2)}, u32[]{:S(2)}) collective-permute-start(f32[128,512]{1,0:T(8,128)S(1)} %add.97.refs_0_), channel_id=1, source_target_pairs={{0,2},{2,4},{4,6},{6,0},{1,3},{3,5},{5,7},{7,1},{8,10},{10,12},{12... | collective-permute-start | bytes 786440 | tf_op jit(solution)/shard_map/ppermute | solution.py:364
Sparse Core Ops, SparseCore 0:
  9.8 44.2 all-gather.1
  142.5 38.1 reduce-scatter.1

commit v4 on v3

--- a/solution.py
+++ b/solution.py
@@ -110,14 +110,18 @@
     return lax.dot_general(a, b, (dims, ((), ())), preferred_element_type=F32)
 
 
+def split_image_kernel(image_ref, near_ref, far_ref, h_ref, m_ref, l_ref):
+    i = pl.program_id(0)
+    a = jnp.where(i < 2, image_ref[...], jnp.where(i == 2, near_ref[...], far_ref[...]))
+    h_ref[...], m_ref[...], l_ref[...] = split3(a)
+
+
 def scores_kernel(first, place, *refs):
     i = pl.program_id(0)
-    if first:
-        image_ref, near_ref, far_ref, text_ref = refs[:4]
-        s_ref, th_ref, tm_ref, r_ref, c_ref, ih_ref, im_ref, il_ref = refs[4:12]
-    else:
-        ih_ref, im_ref, il_ref, r_in, c_in, text_ref = refs[:6]
-        s_ref, th_ref, tm_ref, r_ref, c_ref = refs[6:11]
+    ih_ref, im_ref, il_ref = refs[:3]
+    if not first:
+        r_in, c_in = refs[3:5]
+    text_ref, s_ref, th_ref, tm_ref, r_ref, c_ref = refs[-11:-5]
     h_t, m_t, l_t, top, total = refs[-5:]
 
     @pl.when(i == 0)
@@ -132,9 +136,6 @@
         else:
             c_ref[...] = c_in[...]
 
-    if first:
-        a = jnp.where(i < 2, image_ref[...], jnp.where(i == 2, near_ref[...], far_ref[...]))
-        ih_ref[...], im_ref[...], il_ref[...] = split3(a)
     ih, im, il = ih_ref[...], im_ref[...], il_ref[...]
     th, tm, tl = h_t[...], m_t[...], l_t[...]
     small = dot(ih, tl) + dot(il, th) + dot(im, tm)
@@ -271,39 +272,38 @@
 
     near, far = swap_x(image[:half], image[half:])
     line = lax.all_gather(text, "z", axis=0, tiled=True)
-    line, near, far = lax.optimization_barrier((line, near, far))
     columns = Z * part
     full = (columns, width)
+    ih, im, il = grid_call(
+        split_image_kernel,
+        "split_image",
+        2 * steps,
+        [pl.BlockSpec(tall, lambda i: (jnp.minimum(i, 1), 0)), whole(tall), whole(tall)],
+        [((2 * rows, width), BF16, rows_at(tall))] * 3,
+        free_in=(1, 2),
+    )(image, near, far)
+    line, ih, im, il = lax.optimization_barrier((line, ih, im, il))
 
     s, th, tm = [], [], []
     for b, texts in enumerate((line, flip(line, "core", 2, 1))):
-        outs = [
-            ((2 * rows, columns), F32, rows_at((STEP, columns))),
-            (full, BF16, whole(full)),
-            (full, BF16, whole(full)),
-        ] + table
-        if b == 0:
-            ins = [pl.BlockSpec(tall, lambda i: (jnp.minimum(i, 1), 0)), whole(tall), whole(tall)]
-            outs += [((2 * rows, width), BF16, rows_at(tall))] * 3
-            args = (image, near, far)
-        else:
-            ins = [rows_at(tall)] * 3 + [spec for _, _, spec in table]
-            args = (ih, im, il, r, c)
-        out = grid_call(
+        carried = () if b == 0 else (r, c)
+        a, h, m, r, c = grid_call(
             functools.partial(scores_kernel, b == 0),
             "scores",
             2 * steps,
-            [SMEM] + ins + [whole(full)],
-            outs,
+            [SMEM] + [rows_at(tall)] * 3 + [spec for _, _, spec in table][: len(carried)] + [whole(full)],
+            [
+                ((2 * rows, columns), F32, rows_at((STEP, columns))),
+                (full, BF16, whole(full)),
+                (full, BF16, whole(full)),
+            ]
+            + table,
             scratch=[pltpu.VMEM((width, columns), BF16)] * 3 + [pltpu.VMEM((1, columns), F32)] * 2,
-            free_in=(6,) if b else (2, 3),
-        )(place, *args, texts)
-        s.append(out[0])
-        th.append(out[1])
-        tm.append(out[2])
-        r, c = out[3:5]
-        if b == 0:
-            ih, im, il = out[5:]
+            free_in=(6,) if b else (),
+        )(place, ih, im, il, *carried, texts)
+        s.append(a)
+        th.append(h)
+        tm.append(m)
 
     c = c.reshape(2, Z, part)
     rounds = zip(

time: 207 us -> 205 us (level)
  Pallas kernels: 61.8 us -> 65.7 us
  waiting for transfers between devices: 80.9 us -> 77.4 us
  local copies, waits for them, and re-layouts: 5.43 us -> 3.2 us
    pallas_call x6 -> x7, Pallas kernels: 55.4 us -> 59.3 us  [apply(): run(*[a if k == 0 and ins[0] is SMEM or k in free_in else pltpu.with_memo...]
    all_gather x1, waiting for transfers between devices: 17.2 us -> 13.6 us  [local(): line = lax.all_gather(text, 'z', axis=0, tiled=True)]
    unnamed x4 -> x0, local copies, waits for them, and re-layouts: 2.2 us -> none
  transfers between devices with their start and end apart: 38 -> 38, of which waited for: 23 -> 23; matrix products, arithmetic and copies ran while one was open for 2% -> 2% of each run, Pallas kernels for 20% -> 22%
where the time goes in v4:
time: 205 us
  waiting for transfers between devices  77.4 us (38%)
  Pallas kernels  65.7 us (32%)
  starting transfers between devices  42.9 us (21%)
  between operations  14.2 us (7%)
  local copies, waits for them, and re-layouts  3.2 us (2%)
    pallas_call x7, Pallas kernels, apply(): run(*[a if k == 0 and ins[0] is SMEM or k in free_in else pltpu.with_memo...  59.3 us
    ppermute x22, starting transfers between devices, flip(): return lax.ppermute(a, axis, [(i, i ^ bit) for i in range(size)])  24.7 us
    ppermute x2, waiting for transfers between devices, swap_x(): return (flip(near, 'xl', 2, 1), lax.ppermute(far, ('xl', 'xh'), x_other()))  21.6 us
    ppermute x6, waiting for transfers between devices, over_y(): lax.ppermute(pieces[k], 'y', ring(Y, k))  14.5 us
    ppermute x6, waiting for transfers between devices, to_y(): return [own] + [lax.ppermute(own, 'y', ring(Y, k)) for k in (1, 2, 3)]  13.9 us
    all_gather x1, waiting for transfers between devices, local(): line = lax.all_gather(text, 'z', axis=0, tiled=True)  13.6 us
    ppermute x22, waiting for transfers between devices, flip(): return lax.ppermute(a, axis, [(i, i ^ bit) for i in range(size)])  13 us
    ppermute x6, starting transfers between devices, over_y(): lax.ppermute(pieces[k], 'y', ring(Y, k))  7.77 us
  transfers between devices with their start and end apart: 38, of which 23 were waited for; matrix products, arithmetic and copies ran while one was open for 2% of the time, Pallas kernels for 22%

profile of v4, /device:TPU:2, one launch (start us, length us, event | category | flops | bytes accessed | tf_op | source)
XLA Modules:
  0.0 204.9 jit_solution(2567478141346059235)
XLA Ops:
  7.2 0.7 all-gather.2.cloned.1.call-update
  7.9 1.7 fusion
  9.6 1.6 collective-permute-start.1
  11.2 1.8 collective-permute-start
  13.0 21.6 %collective-permute-done.1.far_ref = f32[256,1024]{1,0:T(8,128)S(1)} collective-permute-done((f32[256,1024]{1,0:T(8,128)S(1)}, f32[256,1024]{1,0:T(8,128)S(1)}, u32[]{:S(2)}, u32[]{:S(2)}) %collective-permute-start.1) | collective-permute-done | bytes 1048608 | tf_op jit(solution)/shard_map/ppermute | solution.py:89
  34.6 1.3 collective-permute-done.near_ref
  35.9 4.6 %split_image.1 = (bf16[1024,1024]{1,0:T(8,128)(2,1)}, bf16[1024,1024]{1,0:T(8,128)(2,1)}, bf16[1024,1024]{1,0:T(8,128)(2,1)}) custom-call(f32[512,1024]{1,0:T(8,128)} %image_ref.1, f32[256,1024]{1,0:T(8,128)S(1)} %collective-permute-done.near_ref, f32[256,1024]{1,0:T(8,128)S(1)} %collective-permute-done.1.far_ref), custom_call_target="tpu_custom_call" | custom-call | flops 1000 | bytes 1000 | tf_op jit(solution)/shard_map/split_image/pallas_call | solution.py:54
  40.5 13.6 %all-gather.2.cloned.1.call-done.refs_3_ = f32[512,1024]{1,0:T(8,128)} async-done(((f32[64,1024]{1,0:T(8,128)}), f32[512,1024]{1,0:T(8,128)}) %all-gather.2.cloned.1.call-update) | async-done | bytes 2097168 | tf_op jit(solution)/shard_map/all_gather | solution.py:274
  54.2 12.9 %scores.2 = (f32[1024,512]{1,0:T(8,128)}, bf16[512,1024]{1,0:T(8,128)(2,1)}, bf16[512,1024]{1,0:T(8,128)(2,1)}, f32[4,256]{1,0:T(4,128)}, f32[2,512]{1,0:T(2,128)}) custom-call(s32[6]{0:T(128)S(1)} %stack.27.place, bf16[1024,1024]{1,0:T(8,128)(2,1)} %get-tuple-element.66.refs_0_.ih, bf16[1024,1024]{1,0:T(8,128)(2,1)} %get-tuple-element.67.refs_1_.im, ...), custom_call_target="tpu_custom_call" | custom-call | flops 1000 | bytes 1000 | tf_op jit(solution)/shard_map/scores/pallas_call | solution.py:54
  67.1 12.2 %scores.3 = (f32[1024,512]{1,0:T(8,128)}, bf16[512,1024]{1,0:T(8,128)(2,1)}, bf16[512,1024]{1,0:T(8,128)(2,1)}, f32[4,256]{1,0:T(4,128)}, f32[2,512]{1,0:T(2,128)}) custom-call(s32[6]{0:T(128)S(1)} %stack.27.place, bf16[1024,1024]{1,0:T(8,128)(2,1)} %get-tuple-element.66.refs_0_.ih, bf16[1024,1024]{1,0:T(8,128)(2,1)} %get-tuple-element.67.refs_1_.im, ...), custom_call_target="tpu_custom_call" | custom-call | flops 1000 | bytes 1000 | tf_op jit(solution)/shard_map/scores/pallas_call | solution.py:54
  79.3 0.8 reshape.10
  80.1 0.5 collective-permute-start.7
  80.6 1.5 collective-permute-start.3
  82.1 1.1 collective-permute-start.8
  83.2 1.2 collective-permute-done.3
  84.4 0.7 log_add_fusion.7
  85.1 3.1 %collective-permute-start.4 = (f32[4,256]{1,0:T(4,128)S(1)}, f32[4,256]{1,0:T(4,128)S(1)}, u32[]{:S(2)}, u32[]{:S(2)}) collective-permute-start(f32[4,256]{1,0:T(4,128)S(1)} %log_add_fusion.7), channel_id=1, source_target_pairs={{0,4},{2,6},{4,0},{6,2},{1,5},{3,7},{5,1},{7,3},{8,12},{10,14},{12... | collective-permute-start | bytes 12296 | tf_op jit(solution)/shard_map/ppermute | solution.py:77
  88.2 1.1 collective-permute-start.9
  89.3 1.0 collective-permute-done.4
  90.3 0.6 collective-permute-start.5
  90.9 1.9 collective-permute-done.9
  92.8 2.8 %collective-permute-start.10 = (f32[2,8,64]{2,1,0:T(8,128)S(1)}, f32[2,8,64]{2,1,0:T(8,128)S(1)}, u32[]{:S(2)}, u32[]{:S(2)}) collective-permute-start(f32[2,8,64]{2,1,0:T(8,128)S(1)} %log_add_fusion.1), channel_id=1, source_target_pairs={{0,128},{32,160},{64,192},{96,224},{128,0},{160,32},{192,64},{224,... | collective-permute-start | bytes 12296 | tf_op jit(solution)/shard_map/ppermute | solution.py:77
  95.7 2.5 %collective-permute-start.6 = (f32[4,256]{1,0:T(4,128)S(1)}, f32[4,256]{1,0:T(4,128)S(1)}, u32[]{:S(2)}, u32[]{:S(2)}) collective-permute-start(f32[4,256]{1,0:T(4,128)S(1)} %log_add_fusion.5), channel_id=1, source_target_pairs={{0,1},{1,0},{2,3},{3,2},{4,5},{5,4},{6,7},{7,6},{8,9},{9,8},{10,11... | collective-permute-start | bytes 12296 | tf_op jit(solution)/shard_map/ppermute | solution.py:77
  98.2 2.3 %collective-permute-done.10 = f32[2,8,64]{2,1,0:T(8,128)S(1)} collective-permute-done((f32[2,8,64]{2,1,0:T(8,128)S(1)}, f32[2,8,64]{2,1,0:T(8,128)S(1)}, u32[]{:S(2)}, u32[]{:S(2)}) %collective-permute-start.10) | collective-permute-done | bytes 4128 | tf_op jit(solution)/shard_map/ppermute | solution.py:77
  100.5 0.7 reshape.11.c_ref
  101.2 0.6 log_add_fusion.4.r_ref
  101.8 8.6 %away.1 = (f32[256,1024]{1,0:T(8,128)}, f32[256,1024]{1,0:T(8,128)}, bf16[512,512]{1,0:T(8,128)(2,1)}, bf16[512,512]{1,0:T(8,128)(2,1)}, bf16[512,512]{1,0:T(8,128)(2,1)}, /*index=5*/bf16[512,512]{1,0:T(8,128)(2,1)}) custom-call(s32[6]{0:T(128)S(1)} %stack.27.place, f32[1024,512]{1,0:T(8,128)} %get-tuple-element.81.s1, f32[1024,512]{1,0:T(8,128)} %get-tuple-element.82.s2, ...), custom_call_target="tpu_custom_call" | custom-call | flops 1000 | bytes 1000 | tf_op jit(solution)/shard_map/away/pallas_call | solution.py:54
  110.4 1.6 collective-permute-start.20
  111.9 1.8 collective-permute-start.19
  113.8 6.9 %home.1 = (f32[512,1024]{1,0:T(8,128)S(1)}, bf16[512,512]{1,0:T(8,128)(2,1)}, bf16[512,512]{1,0:T(8,128)(2,1)}, bf16[512,512]{1,0:T(8,128)(2,1)}, bf16[512,512]{1,0:T(8,128)(2,1)}) custom-call(s32[6]{0:T(128)S(1)} %stack.27.place, f32[1024,512]{1,0:T(8,128)} %get-tuple-element.81.s1, f32[1024,512]{1,0:T(8,128)} %get-tuple-element.82.s2, ...), custom_call_target="tpu_custom_call" | custom-call | flops 1000 | bytes 1000 | tf_op jit(solution)/shard_map/home/pallas_call | solution.py:54
  120.7 7.8 %text_other.1 = (f32[64,1024]{1,0:T(8,128)}, f32[64,1024]{1,0:T(8,128)}, f32[64,1024]{1,0:T(8,128)}, f32[64,1024]{1,0:T(8,128)}, f32[64,1024]{1,0:T(8,128)}, /*i...) custom-call(bf16[512,512]{1,0:T(8,128)(2,1)} %get-tuple-element.94.home_h, ...), custom_call_target="tpu_custom_call" | custom-call | flops 1000 | bytes 1000 | tf_op jit(solution)/shard_map/text_other/pallas_call | solution.py:54
  128.5 0.5 collective-permute-start.12
  129.1 1.1 collective-permute-done.11.refs_0_
  131.1 0.9 collective-permute-done.14.refs_3_
  132.5 6.3 %text_own.1.own = f32[512,1024]{1,0:T(8,128)S(1)} custom-call(bf16[512,512]{1,0:T(8,128)(2,1)} %get-tuple-element.90.home_h, bf16[512,512]{1,0:T(8,128)(2,1)} %get-tuple-element.91.home_l, bf16[512,512]{1,0:T(8,128)(2,1)} %get-tuple-element.92.away_h, bf16[512,512]{1,0:T(8,128)(2,1)} %get-tuple-element.93.away_l, ...), custom_call_target="tpu_custom_call" | custom-call | flops 1000 | bytes 1000 | tf_op jit(solution)/shard_map/text_own/pallas_call | solution.py:54
  138.8 1.6 collect.1
  140.4 1.7 pick.1
  142.1 0.3 collective-permute-start.21
  142.3 0.6 collective-permute-start.22
  142.9 2.6 %collective-permute-start.23 = (f32[128,512]{1,0:T(8,128)S(1)}, f32[128,512]{1,0:T(8,128)S(1)}, u32[]{:S(2)}, u32[]{:S(2)}) collective-permute-start(f32[128,512]{1,0:T(8,128)S(1)} %get-tuple-element.113), channel_id=1, source_target_pairs={{0,6},{2,0},{4,2},{6,4},{1,7},{3,1},{5,3},{7,5},{8,14},{10,8},{12,... | collective-permute-start | bytes 786440 | tf_op jit(solution)/shard_map/ppermute | solution.py:361
  145.7 11.9 %collective-permute-done.22 = f32[128,512]{1,0:T(8,128)S(1)} collective-permute-done((f32[128,512]{1,0:T(8,128)S(1)}, f32[128,512]{1,0:T(8,128)S(1)}, u32[]{:S(2)}, u32[]{:S(2)}) %collective-permute-start.22) | collective-permute-done | bytes 262176 | tf_op jit(solution)/shard_map/ppermute | solution.py:361
  157.9 0.6 turn.1
  158.5 0.8 collective-permute-start.25
  159.3 2.5 %collective-permute-start.26 = (f32[64,512]{1,0:T(8,128)S(1)}, f32[64,512]{1,0:T(8,128)S(1)}, u32[]{:S(2)}, u32[]{:S(2)}) collective-permute-start(f32[64,512]{1,0:T(8,128)S(1)} %get-tuple-element.118), channel_id=1, source_target_pairs={{0,6},{2,0},{4,2},{6,4},{1,7},{3,1},{5,3},{7,5},{8,14},{10,8},{12,... | collective-permute-start | bytes 393224 | tf_op jit(solution)/shard_map/ppermute | solution.py:361
  161.8 1.1 collective-permute-start.27
  162.9 3.2 %collective-permute-start.28 = (f32[128,512]{1,0:T(8,128)S(1)}, f32[128,512]{1,0:T(8,128)S(1)}, u32[]{:S(2)}, u32[]{:S(2)}) collective-permute-start(f32[128,512]{1,0:T(8,128)S(1)} %add_add_fusion), channel_id=1, source_target_pairs={{0,1},{1,0},{2,3},{3,2},{4,5},{5,4},{6,7},{7,6},{8,9},{9,8},{10,11... | collective-permute-start | bytes 786440 | tf_op jit(solution)/shard_map/ppermute | solution.py:77
  166.0 0.9 collective-permute-done.26
  166.9 1.7 collective-permute-done.27
  168.7 2.6 %collective-permute-done.28 = f32[128,512]{1,0:T(8,128)S(1)} collective-permute-done((f32[128,512]{1,0:T(8,128)S(1)}, f32[128,512]{1,0:T(8,128)S(1)}, u32[]{:S(2)}, u32[]{:S(2)}) %collective-permute-start.28) | collective-permute-done | bytes 262176 | tf_op jit(solution)/shard_map/ppermute | solution.py:77
  171.3 1.3 collective-permute-start.34
  172.6 2.0 collective-permute-start.33
  174.6 0.8 collective-permute-start.32
  175.4 1.0 collective-permute-done.34.refs_3_
  176.4 2.7 %collective-permute-done.33.refs_2_ = f32[64,512]{1,0:T(8,128)S(1)} collective-permute-done((f32[64,512]{1,0:T(8,128)S(1)}, f32[64,512]{1,0:T(8,128)S(1)}, u32[]{:S(2)}, u32[]{:S(2)}) %collective-permute-start.33) | collective-permute-done | bytes 131104 | tf_op jit(solution)/shard_map/ppermute | solution.py:364
  179.0 1.7 collective-permute-done.32.refs_1_
  180.7 0.6 gather.1.refs_4_
  181.3 3.0 %collective-permute-start.35 = (f32[256,512]{1,0:T(8,128)S(1)}, f32[256,512]{1,0:T(8,128)S(1)}, u32[]{:S(2)}, u32[]{:S(2)}) collective-permute-start(f32[256,512]{1,0:T(8,128)S(1)} %gather.1.refs_4_), channel_id=1, source_target_pairs={{0,1},{1,0},{2,3},{3,2},{4,5},{5,4},{6,7},{7,6},{8,9},{9,8},{10,11... | collective-permute-start | bytes 1572872 | tf_op jit(solution)/shard_map/ppermute | solution.py:77
  184.4 0.2 collective-permute-start.31
  184.6 2.0 collective-permute-start.30
  186.6 0.9 collective-permute-start.29
  187.5 3.6 %collective-permute-done.31.refs_3_ = f32[128,512]{1,0:T(8,128)S(1)} collective-permute-done((f32[128,512]{1,0:T(8,128)S(1)}, f32[128,512]{1,0:T(8,128)S(1)}, u32[]{:S(2)}, u32[]{:S(2)}) %collective-permute-start.31) | collective-permute-done | bytes 262176 | tf_op jit(solution)/shard_map/ppermute | solution.py:364
  191.1 2.2 %collective-permute-done.30.refs_2_ = f32[128,512]{1,0:T(8,128)S(1)} collective-permute-done((f32[128,512]{1,0:T(8,128)S(1)}, f32[128,512]{1,0:T(8,128)S(1)}, u32[]{:S(2)}, u32[]{:S(2)}) %collective-permute-start.30) | collective-permute-done | bytes 262176 | tf_op jit(solution)/shard_map/ppermute | solution.py:364
  193.3 2.7 %collective-permute-done.29.refs_1_ = f32[128,512]{1,0:T(8,128)S(1)} collective-permute-done((f32[128,512]{1,0:T(8,128)S(1)}, f32[128,512]{1,0:T(8,128)S(1)}, u32[]{:S(2)}, u32[]{:S(2)}) %collective-permute-start.29) | collective-permute-done | bytes 262176 | tf_op jit(solution)/shard_map/ppermute | solution.py:364
  196.0 2.0 assemble.1
  (41 shorter events, 2.2 us)
Async XLA Ops:
  7.2 47.0 %all-gather.2.cloned.1.call-start = ((), (), s32[]{:S(2)}) async-start(), calls=%async_computation.1 | async-start | bytes 2359296 | tf_op jit(solution)/shard_map/all_gather | solution.py:274
  7.9 190.2 %reduce-scatter.2.cloned.1.call-start = ((), (), s32[]{:S(2)}) async-start(), calls=%async_computation.2 | async-start | bytes 2359296 | tf_op jit(solution)/shard_map/reduce_scatter | solution.py:358
  9.6 25.0 %collective-permute-start.1 = (f32[256,1024]{1,0:T(8,128)S(1)}, f32[256,1024]{1,0:T(8,128)S(1)}, u32[]{:S(2)}, u32[]{:S(2)}) collective-permute-start(f32[256,1024]{1,0:T(8,128)S(1)} %get-tuple-element.124), channel_id=1, source_target_pairs={{0,17},{16,1},{1,16},{17,0},{2,19},{18,3},{3,18},{19,2},{4,21},{20... | collective-permute-start | bytes 3145736 | tf_op jit(solution)/shard_map/ppermute | solution.py:89
  11.2 24.7 %collective-permute-start = (f32[256,1024]{1,0:T(8,128)S(1)}, f32[256,1024]{1,0:T(8,128)S(1)}, u32[]{:S(2)}, u32[]{:S(2)}) collective-permute-start(f32[256,1024]{1,0:T(8,128)S(1)} %get-tuple-element.125), channel_id=1, source_target_pairs={{0,16},{16,0},{1,17},{17,1},{2,18},{18,2},{3,19},{19,3},{4,20},{20... | collective-permute-start | bytes 3145736 | tf_op jit(solution)/shard_map/ppermute | solution.py:77
  54.1 13.0 %collective-permute-start.2 = (f32[512,1024]{1,0:T(8,128)}, f32[512,1024]{1,0:T(8,128)S(1)}, u32[]{:S(2)}, u32[]{:S(2)}) collective-permute-start(f32[512,1024]{1,0:T(8,128)} %all-gather.2.cloned.1.call-done.refs_3_), channel_id=1, source_target_pairs={{0,8},{8,0},{1,9},{9,1},{2,10},{10,2},{3,11},{11,3},{4,12},{12,4},... | collective-permute-start | bytes 6291464 | tf_op jit(solution)/shard_map/ppermute | solution.py:77
  80.1 2.0 collective-permute-start.7
  80.6 3.8 %collective-permute-start.3 = (f32[4,256]{1,0:T(4,128)}, f32[4,256]{1,0:T(4,128)S(1)}, u32[]{:S(2)}, u32[]{:S(2)}) collective-permute-start(f32[4,256]{1,0:T(4,128)} %get-tuple-element.74), channel_id=1, source_target_pairs={{0,2},{2,0},{4,6},{6,4},{1,3},{3,1},{5,7},{7,5},{8,10},{10,8},{12,... | collective-permute-start | bytes 12296 | tf_op jit(solution)/shard_map/ppermute | solution.py:77
  82.1 6.1 %collective-permute-start.8 = (f32[2,8,64]{2,1,0:T(8,128)S(1)}, f32[2,8,64]{2,1,0:T(8,128)S(1)}, u32[]{:S(2)}, u32[]{:S(2)}) collective-permute-start(f32[2,8,64]{2,1,0:T(8,128)S(1)} %log_add_fusion.3), channel_id=1, source_target_pairs={{0,32},{32,0},{64,96},{96,64},{128,160},{160,128},{192,224},{224,1... | collective-permute-start | bytes 12296 | tf_op jit(solution)/shard_map/ppermute | solution.py:77
  85.1 5.2 %collective-permute-start.4 = (f32[4,256]{1,0:T(4,128)S(1)}, f32[4,256]{1,0:T(4,128)S(1)}, u32[]{:S(2)}, u32[]{:S(2)}) collective-permute-start(f32[4,256]{1,0:T(4,128)S(1)} %log_add_fusion.7), channel_id=1, source_target_pairs={{0,4},{2,6},{4,0},{6,2},{1,5},{3,7},{5,1},{7,3},{8,12},{10,14},{12... | collective-permute-start | bytes 12296 | tf_op jit(solution)/shard_map/ppermute | solution.py:77
  88.2 4.6 %collective-permute-start.9 = (f32[2,8,64]{2,1,0:T(8,128)S(1)}, f32[2,8,64]{2,1,0:T(8,128)S(1)}, u32[]{:S(2)}, u32[]{:S(2)}) collective-permute-start(f32[2,8,64]{2,1,0:T(8,128)S(1)} %log_add_fusion.2), channel_id=1, source_target_pairs={{0,64},{32,96},{64,0},{96,32},{128,192},{160,224},{192,128},{224,1... | collective-permute-start | bytes 12296 | tf_op jit(solution)/shard_map/ppermute | solution.py:77
  90.3 5.4 %collective-permute-start.5 = (f32[4,256]{1,0:T(4,128)S(1)}, f32[4,256]{1,0:T(4,128)S(1)}, u32[]{:S(2)}, u32[]{:S(2)}) collective-permute-start(f32[4,256]{1,0:T(4,128)S(1)} %log_add_fusion.6), channel_id=1, source_target_pairs={{0,16},{16,0},{1,17},{17,1},{2,18},{18,2},{3,19},{19,3},{4,20},{20... | collective-permute-start | bytes 12296 | tf_op jit(solution)/shard_map/ppermute | solution.py:77
  92.8 7.6 %collective-permute-start.10 = (f32[2,8,64]{2,1,0:T(8,128)S(1)}, f32[2,8,64]{2,1,0:T(8,128)S(1)}, u32[]{:S(2)}, u32[]{:S(2)}) collective-permute-start(f32[2,8,64]{2,1,0:T(8,128)S(1)} %log_add_fusion.1), channel_id=1, source_target_pairs={{0,128},{32,160},{64,192},{96,224},{128,0},{160,32},{192,64},{224,... | collective-permute-start | bytes 12296 | tf_op jit(solution)/shard_map/ppermute | solution.py:77
  95.7 5.5 %collective-permute-start.6 = (f32[4,256]{1,0:T(4,128)S(1)}, f32[4,256]{1,0:T(4,128)S(1)}, u32[]{:S(2)}, u32[]{:S(2)}) collective-permute-start(f32[4,256]{1,0:T(4,128)S(1)} %log_add_fusion.5), channel_id=1, source_target_pairs={{0,1},{1,0},{2,3},{3,2},{4,5},{5,4},{6,7},{7,6},{8,9},{9,8},{10,11... | collective-permute-start | bytes 12296 | tf_op jit(solution)/shard_map/ppermute | solution.py:77
  110.4 30.0 %collective-permute-start.20 = (f32[256,1024]{1,0:T(8,128)}, f32[256,1024]{1,0:T(8,128)S(1)}, u32[]{:S(2)}, u32[]{:S(2)}) collective-permute-start(f32[256,1024]{1,0:T(8,128)} %get-tuple-element.106), channel_id=1, source_target_pairs={{0,17},{16,1},{1,16},{17,0},{2,19},{18,3},{3,18},{19,2},{4,21},{20... | collective-permute-start | bytes 3145736 | tf_op jit(solution)/shard_map/ppermute | solution.py:89
  111.9 28.4 %collective-permute-start.19 = (f32[256,1024]{1,0:T(8,128)}, f32[256,1024]{1,0:T(8,128)}, u32[]{:S(2)}, u32[]{:S(2)}) collective-permute-start(f32[256,1024]{1,0:T(8,128)} %get-tuple-element.80), channel_id=1, source_target_pairs={{0,16},{16,0},{1,17},{17,1},{2,18},{18,2},{3,19},{19,3},{4,20},{20... | collective-permute-start | bytes 3145736 | tf_op jit(solution)/shard_map/ppermute | solution.py:77
  128.5 1.7 collective-permute-start.11
  128.5 2.1 %collective-permute-start.12 = (f32[64,1024]{1,0:T(8,128)}, f32[64,1024]{1,0:T(8,128)S(1)}, u32[]{:S(2)}, u32[]{:S(2)}) collective-permute-start(f32[64,1024]{1,0:T(8,128)} %get-tuple-element.99), channel_id=1, source_target_pairs={{0,8},{8,0},{1,9},{9,1},{2,10},{10,2},{3,11},{11,3},{4,12},{12,4},... | collective-permute-start | bytes 786440 | tf_op jit(solution)/shard_map/ppermute | solution.py:77
  129.0 2.0 collective-permute-start.13
  130.2 1.7 collective-permute-start.14
  130.6 1.7 collective-permute-start.15
  131.0 7.8 %collective-permute-start.16 = (f32[64,1024]{1,0:T(8,128)}, f32[64,1024]{1,0:T(8,128)S(1)}, u32[]{:S(2)}, u32[]{:S(2)}) collective-permute-start(f32[64,1024]{1,0:T(8,128)} %get-tuple-element.103), channel_id=1, source_target_pairs={{0,8},{8,0},{1,9},{9,1},{2,10},{10,2},{3,11},{11,3},{4,12},{12,4},... | collective-permute-start | bytes 786440 | tf_op jit(solution)/shard_map/ppermute | solution.py:77
  131.9 6.8 %collective-permute-start.17 = (f32[64,1024]{1,0:T(8,128)}, f32[64,1024]{1,0:T(8,128)S(1)}, u32[]{:S(2)}, u32[]{:S(2)}) collective-permute-start(f32[64,1024]{1,0:T(8,128)} %get-tuple-element.104), channel_id=1, source_target_pairs={{0,8},{8,0},{1,9},{9,1},{2,10},{10,2},{3,11},{11,3},{4,12},{12,4},... | collective-permute-start | bytes 786440 | tf_op jit(solution)/shard_map/ppermute | solution.py:77
  132.3 6.5 %collective-permute-start.18 = (f32[64,1024]{1,0:T(8,128)}, f32[64,1024]{1,0:T(8,128)S(1)}, u32[]{:S(2)}, u32[]{:S(2)}) collective-permute-start(f32[64,1024]{1,0:T(8,128)} %get-tuple-element.105), channel_id=1, source_target_pairs={{0,8},{8,0},{1,9},{9,1},{2,10},{10,2},{3,11},{11,3},{4,12},{12,4},... | collective-permute-start | bytes 786440 | tf_op jit(solution)/shard_map/ppermute | solution.py:77
  142.1 15.8 %collective-permute-start.21 = (f32[256,512]{1,0:T(8,128)S(1)}, f32[256,512]{1,0:T(8,128)S(1)}, u32[]{:S(2)}, u32[]{:S(2)}) collective-permute-start(f32[256,512]{1,0:T(8,128)S(1)} %get-tuple-element.110), channel_id=1, source_target_pairs={{0,1},{1,0},{2,3},{3,2},{4,5},{5,4},{6,7},{7,6},{8,9},{9,8},{10,11... | collective-permute-start | bytes 1572872 | tf_op jit(solution)/shard_map/ppermute | solution.py:77
  142.3 15.3 %collective-permute-start.22 = (f32[128,512]{1,0:T(8,128)S(1)}, f32[128,512]{1,0:T(8,128)S(1)}, u32[]{:S(2)}, u32[]{:S(2)}) collective-permute-start(f32[128,512]{1,0:T(8,128)S(1)} %get-tuple-element.112), channel_id=1, source_target_pairs={{0,2},{2,4},{4,6},{6,0},{1,3},{3,5},{5,7},{7,1},{8,10},{10,12},{12... | collective-permute-start | bytes 786440 | tf_op jit(solution)/shard_map/ppermute | solution.py:361
  142.9 14.7 %collective-permute-start.23 = (f32[128,512]{1,0:T(8,128)S(1)}, f32[128,512]{1,0:T(8,128)S(1)}, u32[]{:S(2)}, u32[]{:S(2)}) collective-permute-start(f32[128,512]{1,0:T(8,128)S(1)} %get-tuple-element.113), channel_id=1, source_target_pairs={{0,6},{2,0},{4,2},{6,4},{1,7},{3,1},{5,3},{7,5},{8,14},{10,8},{12,... | collective-permute-start | bytes 786440 | tf_op jit(solution)/shard_map/ppermute | solution.py:361
  145.6 12.1 %collective-permute-start.24 = (f32[128,512]{1,0:T(8,128)S(1)}, f32[128,512]{1,0:T(8,128)S(1)}, u32[]{:S(2)}, u32[]{:S(2)}) collective-permute-start(f32[128,512]{1,0:T(8,128)S(1)} %get-tuple-element.114), channel_id=1, source_target_pairs={{0,4},{2,6},{4,0},{6,2},{1,5},{3,7},{5,1},{7,3},{8,12},{10,14},{12... | collective-permute-start | bytes 786440 | tf_op jit(solution)/shard_map/ppermute | solution.py:361
  158.5 7.6 %collective-permute-start.25 = (f32[64,512]{1,0:T(8,128)S(1)}, f32[64,512]{1,0:T(8,128)S(1)}, u32[]{:S(2)}, u32[]{:S(2)}) collective-permute-start(f32[64,512]{1,0:T(8,128)S(1)} %get-tuple-element.117), channel_id=1, source_target_pairs={{0,2},{2,4},{4,6},{6,0},{1,3},{3,5},{5,7},{7,1},{8,10},{10,12},{12... | collective-permute-start | bytes 393224 | tf_op jit(solution)/shard_map/ppermute | solution.py:361
  159.3 7.6 %collective-permute-start.26 = (f32[64,512]{1,0:T(8,128)S(1)}, f32[64,512]{1,0:T(8,128)S(1)}, u32[]{:S(2)}, u32[]{:S(2)}) collective-permute-start(f32[64,512]{1,0:T(8,128)S(1)} %get-tuple-element.118), channel_id=1, source_target_pairs={{0,6},{2,0},{4,2},{6,4},{1,7},{3,1},{5,3},{7,5},{8,14},{10,8},{12,... | collective-permute-start | bytes 393224 | tf_op jit(solution)/shard_map/ppermute | solution.py:361
  161.8 6.8 %collective-permute-start.27 = (f32[64,512]{1,0:T(8,128)S(1)}, f32[64,512]{1,0:T(8,128)S(1)}, u32[]{:S(2)}, u32[]{:S(2)}) collective-permute-start(f32[64,512]{1,0:T(8,128)S(1)} %get-tuple-element.119), channel_id=1, source_target_pairs={{0,4},{2,6},{4,0},{6,2},{1,5},{3,7},{5,1},{7,3},{8,12},{10,14},{12... | collective-permute-start | bytes 393224 | tf_op jit(solution)/shard_map/ppermute | solution.py:361
  162.9 8.4 %collective-permute-start.28 = (f32[128,512]{1,0:T(8,128)S(1)}, f32[128,512]{1,0:T(8,128)S(1)}, u32[]{:S(2)}, u32[]{:S(2)}) collective-permute-start(f32[128,512]{1,0:T(8,128)S(1)} %add_add_fusion), channel_id=1, source_target_pairs={{0,1},{1,0},{2,3},{3,2},{4,5},{5,4},{6,7},{7,6},{8,9},{9,8},{10,11... | collective-permute-start | bytes 786440 | tf_op jit(solution)/shard_map/ppermute | solution.py:77
  171.3 5.1 %collective-permute-start.34 = (f32[64,512]{1,0:T(8,128)S(1)}, f32[64,512]{1,0:T(8,128)S(1)}, u32[]{:S(2)}, u32[]{:S(2)}) collective-permute-start(f32[64,512]{1,0:T(8,128)S(1)} %add_add_fusion.1.refs_0_), channel_id=1, source_target_pairs={{0,6},{2,0},{4,2},{6,4},{1,7},{3,1},{5,3},{7,5},{8,14},{10,8},{12,... | collective-permute-start | bytes 393224 | tf_op jit(solution)/shard_map/ppermute | solution.py:364
  172.6 6.5 %collective-permute-start.33 = (f32[64,512]{1,0:T(8,128)S(1)}, f32[64,512]{1,0:T(8,128)S(1)}, u32[]{:S(2)}, u32[]{:S(2)}) collective-permute-start(f32[64,512]{1,0:T(8,128)S(1)} %add_add_fusion.1.refs_0_), channel_id=1, source_target_pairs={{0,4},{2,6},{4,0},{6,2},{1,5},{3,7},{5,1},{7,3},{8,12},{10,14},{12... | collective-permute-start | bytes 393224 | tf_op jit(solution)/shard_map/ppermute | solution.py:364
  174.6 6.2 %collective-permute-start.32 = (f32[64,512]{1,0:T(8,128)S(1)}, f32[64,512]{1,0:T(8,128)S(1)}, u32[]{:S(2)}, u32[]{:S(2)}) collective-permute-start(f32[64,512]{1,0:T(8,128)S(1)} %add_add_fusion.1.refs_0_), channel_id=1, source_target_pairs={{0,2},{2,4},{4,6},{6,0},{1,3},{3,5},{5,7},{7,1},{8,10},{10,12},{12... | collective-permute-start | bytes 393224 | tf_op jit(solution)/shard_map/ppermute | solution.py:364
  181.3 14.7 %collective-permute-start.35 = (f32[256,512]{1,0:T(8,128)S(1)}, f32[256,512]{1,0:T(8,128)S(1)}, u32[]{:S(2)}, u32[]{:S(2)}) collective-permute-start(f32[256,512]{1,0:T(8,128)S(1)} %gather.1.refs_4_), channel_id=1, source_target_pairs={{0,1},{1,0},{2,3},{3,2},{4,5},{5,4},{6,7},{7,6},{8,9},{9,8},{10,11... | collective-permute-start | bytes 1572872 | tf_op jit(solution)/shard_map/ppermute | solution.py:77
  184.4 6.7 %collective-permute-start.31 = (f32[128,512]{1,0:T(8,128)S(1)}, f32[128,512]{1,0:T(8,128)S(1)}, u32[]{:S(2)}, u32[]{:S(2)}) collective-permute-start(f32[128,512]{1,0:T(8,128)S(1)} %add.97.refs_0_), channel_id=1, source_target_pairs={{0,6},{2,0},{4,2},{6,4},{1,7},{3,1},{5,3},{7,5},{8,14},{10,8},{12,... | collective-permute-start | bytes 786440 | tf_op jit(solution)/shard_map/ppermute | solution.py:364
  184.6 8.7 %collective-permute-start.30 = (f32[128,512]{1,0:T(8,128)S(1)}, f32[128,512]{1,0:T(8,128)S(1)}, u32[]{:S(2)}, u32[]{:S(2)}) collective-permute-start(f32[128,512]{1,0:T(8,128)S(1)} %add.97.refs_0_), channel_id=1, source_target_pairs={{0,4},{2,6},{4,0},{6,2},{1,5},{3,7},{5,1},{7,3},{8,12},{10,14},{12... | collective-permute-start | bytes 786440 | tf_op jit(solution)/shard_map/ppermute | solution.py:364
  186.6 9.4 %collective-permute-start.29 = (f32[128,512]{1,0:T(8,128)S(1)}, f32[128,512]{1,0:T(8,128)S(1)}, u32[]{:S(2)}, u32[]{:S(2)}) collective-permute-start(f32[128,512]{1,0:T(8,128)S(1)} %add.97.refs_0_), channel_id=1, source_target_pairs={{0,2},{2,4},{4,6},{6,0},{1,3},{3,5},{5,7},{7,1},{8,10},{10,12},{12... | collective-permute-start | bytes 786440 | tf_op jit(solution)/shard_map/ppermute | solution.py:364
Sparse Core Ops, SparseCore 0:
  9.8 44.2 all-gather.1
  140.5 38.1 reduce-scatter.1

commit v5 on v4

--- a/solution.py
+++ b/solution.py
@@ -10,7 +10,7 @@
 Z, Y = 8, 4
 STEP = 256
 CUTS = 8
-WIDE = 512
+WIDE = 384
 PICK = 100_000_000
 F32, BF16 = jnp.float32, jnp.bfloat16
 VMEM = pl.BlockSpec(memory_space=pltpu.VMEM)

time: 205 us -> 210 us (1.024)
  waiting for transfers between devices: 77.4 us -> 88 us
  starting transfers between devices: 42.9 us -> 36.4 us
    ppermute x22, starting transfers between devices: 24.7 us -> 18.9 us  [flip(): return lax.ppermute(a, axis, [(i, i ^ bit) for i in range(size)])]
    ppermute x6, waiting for transfers between devices: 14.5 us -> 19.4 us  [over_y(): lax.ppermute(pieces[k], 'y', ring(Y, k))]
    ppermute x6, waiting for transfers between devices: 13.9 us -> 17.3 us  [to_y(): return [own] + [lax.ppermute(own, 'y', ring(Y, k)) for k in (1, 2, 3)]]
    ppermute x22, waiting for transfers between devices: 13 us -> 15.3 us  [flip(): return lax.ppermute(a, axis, [(i, i ^ bit) for i in range(size)])]
  transfers between devices with their start and end apart: 38 -> 38, of which waited for: 23 -> 23; matrix products, arithmetic and copies ran while one was open for 2% -> 2% of each run, Pallas kernels for 22% -> 21%
where the time goes in v5:
time: 210 us; the launch traced here: 209 us
  waiting for transfers between devices  88 us (42%)
  Pallas kernels  65.6 us (31%)
  starting transfers between devices  36.4 us (17%)
  between operations  14.2 us (7%)
  local copies, waits for them, and re-layouts  3.2 us (2%)
    pallas_call x7, Pallas kernels, apply(): run(*[a if k == 0 and ins[0] is SMEM or k in free_in else pltpu.with_memo...  59.3 us
    ppermute x2, waiting for transfers between devices, swap_x(): return (flip(near, 'xl', 2, 1), lax.ppermute(far, ('xl', 'xh'), x_other()))  21.6 us
    ppermute x6, waiting for transfers between devices, over_y(): lax.ppermute(pieces[k], 'y', ring(Y, k))  19.4 us
    ppermute x22, starting transfers between devices, flip(): return lax.ppermute(a, axis, [(i, i ^ bit) for i in range(size)])  18.9 us
    ppermute x6, waiting for transfers between devices, to_y(): return [own] + [lax.ppermute(own, 'y', ring(Y, k)) for k in (1, 2, 3)]  17.3 us
    ppermute x22, waiting for transfers between devices, flip(): return lax.ppermute(a, axis, [(i, i ^ bit) for i in range(size)])  15.3 us
    all_gather x1, waiting for transfers between devices, local(): line = lax.all_gather(text, 'z', axis=0, tiled=True)  13.6 us
    ppermute x6, starting transfers between devices, over_y(): lax.ppermute(pieces[k], 'y', ring(Y, k))  7.96 us
  transfers between devices with their start and end apart: 38, of which 23 were waited for; matrix products, arithmetic and copies ran while one was open for 2% of the time, Pallas kernels for 21%

profile of v5, /device:TPU:2, one launch (start us, length us, event | category | flops | bytes accessed | tf_op | source)
XLA Modules:
  0.0 208.9 jit_solution(4296863038591149594)
XLA Ops:
  7.2 0.7 all-gather.2.cloned.1.call-update
  7.9 1.7 fusion
  9.6 1.6 collective-permute-start.1
  11.2 1.8 collective-permute-start
  13.0 21.6 %collective-permute-done.1.far_ref = f32[256,1024]{1,0:T(8,128)S(1)} collective-permute-done((f32[256,1024]{1,0:T(8,128)S(1)}, f32[256,1024]{1,0:T(8,128)S(1)}, u32[]{:S(2)}, u32[]{:S(2)}) %collective-permute-start.1) | collective-permute-done | bytes 1048608 | tf_op jit(solution)/shard_map/ppermute | solution.py:89
  34.6 1.3 collective-permute-done.near_ref
  35.9 4.6 %split_image.1 = (bf16[1024,1024]{1,0:T(8,128)(2,1)}, bf16[1024,1024]{1,0:T(8,128)(2,1)}, bf16[1024,1024]{1,0:T(8,128)(2,1)}) custom-call(f32[512,1024]{1,0:T(8,128)} %image_ref.1, f32[256,1024]{1,0:T(8,128)S(1)} %collective-permute-done.near_ref, f32[256,1024]{1,0:T(8,128)S(1)} %collective-permute-done.1.far_ref), custom_call_target="tpu_custom_call" | custom-call | flops 1000 | bytes 1000 | tf_op jit(solution)/shard_map/split_image/pallas_call | solution.py:54
  40.5 13.6 %all-gather.2.cloned.1.call-done.refs_3_ = f32[512,1024]{1,0:T(8,128)} async-done(((f32[64,1024]{1,0:T(8,128)}), f32[512,1024]{1,0:T(8,128)}) %all-gather.2.cloned.1.call-update) | async-done | bytes 2097168 | tf_op jit(solution)/shard_map/all_gather | solution.py:274
  54.2 12.9 %scores.2 = (f32[1024,512]{1,0:T(8,128)}, bf16[512,1024]{1,0:T(8,128)(2,1)}, bf16[512,1024]{1,0:T(8,128)(2,1)}, f32[4,256]{1,0:T(4,128)}, f32[2,512]{1,0:T(2,128)}) custom-call(s32[6]{0:T(128)S(1)} %stack.27.place, bf16[1024,1024]{1,0:T(8,128)(2,1)} %get-tuple-element.66.refs_0_.ih, bf16[1024,1024]{1,0:T(8,128)(2,1)} %get-tuple-element.67.refs_1_.im, ...), custom_call_target="tpu_custom_call" | custom-call | flops 1000 | bytes 1000 | tf_op jit(solution)/shard_map/scores/pallas_call | solution.py:54
  67.1 12.2 %scores.3 = (f32[1024,512]{1,0:T(8,128)}, bf16[512,1024]{1,0:T(8,128)(2,1)}, bf16[512,1024]{1,0:T(8,128)(2,1)}, f32[4,256]{1,0:T(4,128)}, f32[2,512]{1,0:T(2,128)}) custom-call(s32[6]{0:T(128)S(1)} %stack.27.place, bf16[1024,1024]{1,0:T(8,128)(2,1)} %get-tuple-element.66.refs_0_.ih, bf16[1024,1024]{1,0:T(8,128)(2,1)} %get-tuple-element.67.refs_1_.im, ...), custom_call_target="tpu_custom_call" | custom-call | flops 1000 | bytes 1000 | tf_op jit(solution)/shard_map/scores/pallas_call | solution.py:54
  79.3 0.8 reshape.10
  80.1 0.5 collective-permute-start.7
  80.6 1.5 collective-permute-start.3
  82.1 1.1 collective-permute-start.8
  83.2 1.2 collective-permute-done.3
  84.4 0.7 log_add_fusion.7
  85.1 3.1 %collective-permute-start.4 = (f32[4,256]{1,0:T(4,128)S(1)}, f32[4,256]{1,0:T(4,128)S(1)}, u32[]{:S(2)}, u32[]{:S(2)}) collective-permute-start(f32[4,256]{1,0:T(4,128)S(1)} %log_add_fusion.7), channel_id=1, source_target_pairs={{0,4},{2,6},{4,0},{6,2},{1,5},{3,7},{5,1},{7,3},{8,12},{10,14},{12... | collective-permute-start | bytes 12296 | tf_op jit(solution)/shard_map/ppermute | solution.py:77
  88.2 1.1 collective-permute-start.9
  89.3 1.0 collective-permute-done.4
  90.3 0.6 collective-permute-start.5
  90.9 1.9 collective-permute-done.9
  92.8 2.8 %collective-permute-start.10 = (f32[2,8,64]{2,1,0:T(8,128)S(1)}, f32[2,8,64]{2,1,0:T(8,128)S(1)}, u32[]{:S(2)}, u32[]{:S(2)}) collective-permute-start(f32[2,8,64]{2,1,0:T(8,128)S(1)} %log_add_fusion.1), channel_id=1, source_target_pairs={{0,128},{32,160},{64,192},{96,224},{128,0},{160,32},{192,64},{224,... | collective-permute-start | bytes 12296 | tf_op jit(solution)/shard_map/ppermute | solution.py:77
  95.7 2.5 %collective-permute-start.6 = (f32[4,256]{1,0:T(4,128)S(1)}, f32[4,256]{1,0:T(4,128)S(1)}, u32[]{:S(2)}, u32[]{:S(2)}) collective-permute-start(f32[4,256]{1,0:T(4,128)S(1)} %log_add_fusion.5), channel_id=1, source_target_pairs={{0,1},{1,0},{2,3},{3,2},{4,5},{5,4},{6,7},{7,6},{8,9},{9,8},{10,11... | collective-permute-start | bytes 12296 | tf_op jit(solution)/shard_map/ppermute | solution.py:77
  98.2 2.3 %collective-permute-done.10 = f32[2,8,64]{2,1,0:T(8,128)S(1)} collective-permute-done((f32[2,8,64]{2,1,0:T(8,128)S(1)}, f32[2,8,64]{2,1,0:T(8,128)S(1)}, u32[]{:S(2)}, u32[]{:S(2)}) %collective-permute-start.10) | collective-permute-done | bytes 4128 | tf_op jit(solution)/shard_map/ppermute | solution.py:77
  100.5 0.7 reshape.11.c_ref
  101.2 0.6 log_add_fusion.4.r_ref
  101.8 8.6 %away.1 = (f32[256,1024]{1,0:T(8,128)}, f32[256,1024]{1,0:T(8,128)}, bf16[512,512]{1,0:T(8,128)(2,1)}, bf16[512,512]{1,0:T(8,128)(2,1)}, bf16[512,512]{1,0:T(8,128)(2,1)}, /*index=5*/bf16[512,512]{1,0:T(8,128)(2,1)}) custom-call(s32[6]{0:T(128)S(1)} %stack.27.place, f32[1024,512]{1,0:T(8,128)} %get-tuple-element.81.s1, f32[1024,512]{1,0:T(8,128)} %get-tuple-element.82.s2, ...), custom_call_target="tpu_custom_call" | custom-call | flops 1000 | bytes 1000 | tf_op jit(solution)/shard_map/away/pallas_call | solution.py:54
  110.4 1.6 collective-permute-start.20
  111.9 1.8 collective-permute-start.19
  113.8 6.9 %home.1 = (f32[512,1024]{1,0:T(8,128)S(1)}, bf16[512,512]{1,0:T(8,128)(2,1)}, bf16[512,512]{1,0:T(8,128)(2,1)}, bf16[512,512]{1,0:T(8,128)(2,1)}, bf16[512,512]{1,0:T(8,128)(2,1)}) custom-call(s32[6]{0:T(128)S(1)} %stack.27.place, f32[1024,512]{1,0:T(8,128)} %get-tuple-element.81.s1, f32[1024,512]{1,0:T(8,128)} %get-tuple-element.82.s2, ...), custom_call_target="tpu_custom_call" | custom-call | flops 1000 | bytes 1000 | tf_op jit(solution)/shard_map/home/pallas_call | solution.py:54
  120.7 7.8 %text_other.1 = (f32[64,1024]{1,0:T(8,128)}, f32[64,1024]{1,0:T(8,128)}, f32[64,1024]{1,0:T(8,128)}, f32[64,1024]{1,0:T(8,128)}, f32[64,1024]{1,0:T(8,128)}, /*i...) custom-call(bf16[512,512]{1,0:T(8,128)(2,1)} %get-tuple-element.94.home_h, ...), custom_call_target="tpu_custom_call" | custom-call | flops 1000 | bytes 1000 | tf_op jit(solution)/shard_map/text_other/pallas_call | solution.py:54
  128.5 0.5 collective-permute-start.12
  129.1 1.1 collective-permute-done.11.refs_0_
  130.3 0.2 collective-permute-done.12.refs_1_
  131.1 0.9 collective-permute-done.14.refs_3_
  132.5 6.3 %text_own.1.own = f32[512,1024]{1,0:T(8,128)S(1)} custom-call(bf16[512,512]{1,0:T(8,128)(2,1)} %get-tuple-element.90.home_h, bf16[512,512]{1,0:T(8,128)(2,1)} %get-tuple-element.91.home_l, bf16[512,512]{1,0:T(8,128)(2,1)} %get-tuple-element.92.away_h, bf16[512,512]{1,0:T(8,128)(2,1)} %get-tuple-element.93.away_l, ...), custom_call_target="tpu_custom_call" | custom-call | flops 1000 | bytes 1000 | tf_op jit(solution)/shard_map/text_own/pallas_call | solution.py:54
  138.8 1.6 collect.1
  140.4 1.6 pick.1
  142.0 0.7 collective-permute-start.22
  142.7 2.7 %collective-permute-start.23 = (f32[128,640]{1,0:T(8,128)S(1)}, f32[128,640]{1,0:T(8,128)S(1)}, u32[]{:S(2)}, u32[]{:S(2)}) collective-permute-start(f32[128,640]{1,0:T(8,128)S(1)} %get-tuple-element.113), channel_id=1, source_target_pairs={{0,6},{2,0},{4,2},{6,4},{1,7},{3,1},{5,3},{7,5},{8,14},{10,8},{12,... | collective-permute-start | bytes 983048 | tf_op jit(solution)/shard_map/ppermute | solution.py:361
  145.7 14.7 %collective-permute-done.22 = f32[128,640]{1,0:T(8,128)S(1)} collective-permute-done((f32[128,640]{1,0:T(8,128)S(1)}, f32[128,640]{1,0:T(8,128)S(1)}, u32[]{:S(2)}, u32[]{:S(2)}) %collective-permute-start.22) | collective-permute-done | bytes 327712 | tf_op jit(solution)/shard_map/ppermute | solution.py:361
  160.4 0.6 turn.1
  161.0 0.9 collective-permute-start.25
  161.9 2.4 %collective-permute-start.26 = (f32[64,384]{1,0:T(8,128)S(1)}, f32[64,384]{1,0:T(8,128)S(1)}, u32[]{:S(2)}, u32[]{:S(2)}) collective-permute-start(f32[64,384]{1,0:T(8,128)S(1)} %get-tuple-element.118), channel_id=1, source_target_pairs={{0,6},{2,0},{4,2},{6,4},{1,7},{3,1},{5,3},{7,5},{8,14},{10,8},{12,... | collective-permute-start | bytes 294920 | tf_op jit(solution)/shard_map/ppermute | solution.py:361
  164.3 1.2 collective-permute-start.27
  165.7 1.2 collective-permute-done.25
  166.9 0.5 collective-permute-done.26
  167.5 3.0 %collective-permute-done.27 = f32[64,384]{1,0:T(8,128)S(1)} collective-permute-done((f32[64,384]{1,0:T(8,128)S(1)}, f32[64,384]{1,0:T(8,128)S(1)}, u32[]{:S(2)}, u32[]{:S(2)}) %collective-permute-start.27) | collective-permute-done | bytes 98336 | tf_op jit(solution)/shard_map/ppermute | solution.py:361
  170.5 4.9 %collective-permute-done.28 = f32[128,640]{1,0:T(8,128)S(1)} collective-permute-done((f32[128,640]{1,0:T(8,128)S(1)}, f32[128,640]{1,0:T(8,128)S(1)}, u32[]{:S(2)}, u32[]{:S(2)}) %collective-permute-start.28) | collective-permute-done | bytes 327712 | tf_op jit(solution)/shard_map/ppermute | solution.py:77
  175.5 1.1 collective-permute-start.34
  176.6 2.1 %collective-permute-start.33 = (f32[64,384]{1,0:T(8,128)S(1)}, f32[64,384]{1,0:T(8,128)S(1)}, u32[]{:S(2)}, u32[]{:S(2)}) collective-permute-start(f32[64,384]{1,0:T(8,128)S(1)} %add_add_fusion.1.refs_0_), channel_id=1, source_target_pairs={{0,4},{2,6},{4,0},{6,2},{1,5},{3,7},{5,1},{7,3},{8,12},{10,14},{12... | collective-permute-start | bytes 294920 | tf_op jit(solution)/shard_map/ppermute | solution.py:364
  178.7 0.4 collective-permute-start.32
  179.1 1.0 collective-permute-done.34.refs_3_
  180.2 2.6 %collective-permute-done.33.refs_2_ = f32[64,384]{1,0:T(8,128)S(1)} collective-permute-done((f32[64,384]{1,0:T(8,128)S(1)}, f32[64,384]{1,0:T(8,128)S(1)}, u32[]{:S(2)}, u32[]{:S(2)}) %collective-permute-start.33) | collective-permute-done | bytes 98336 | tf_op jit(solution)/shard_map/ppermute | solution.py:364
  182.7 1.8 collective-permute-done.32.refs_1_
  184.6 0.6 gather.1.refs_4_
  185.2 0.4 collective-permute-start.35
  185.5 0.3 collective-permute-start.31
  185.8 1.7 collective-permute-start.30
  187.5 0.7 collective-permute-start.29
  188.2 6.2 %collective-permute-done.31.refs_3_ = f32[128,640]{1,0:T(8,128)S(1)} collective-permute-done((f32[128,640]{1,0:T(8,128)S(1)}, f32[128,640]{1,0:T(8,128)S(1)}, u32[]{:S(2)}, u32[]{:S(2)}) %collective-permute-start.31) | collective-permute-done | bytes 327712 | tf_op jit(solution)/shard_map/ppermute | solution.py:364
  194.4 2.3 %collective-permute-done.30.refs_2_ = f32[128,640]{1,0:T(8,128)S(1)} collective-permute-done((f32[128,640]{1,0:T(8,128)S(1)}, f32[128,640]{1,0:T(8,128)S(1)}, u32[]{:S(2)}, u32[]{:S(2)}) %collective-permute-start.30) | collective-permute-done | bytes 327712 | tf_op jit(solution)/shard_map/ppermute | solution.py:364
  196.7 3.4 %collective-permute-done.29.refs_1_ = f32[128,640]{1,0:T(8,128)S(1)} collective-permute-done((f32[128,640]{1,0:T(8,128)S(1)}, f32[128,640]{1,0:T(8,128)S(1)}, u32[]{:S(2)}, u32[]{:S(2)}) %collective-permute-start.29) | collective-permute-done | bytes 327712 | tf_op jit(solution)/shard_map/ppermute | solution.py:364
  200.1 2.0 assemble.1
  (41 shorter events, 2.2 us)
Async XLA Ops:
  7.2 47.0 %all-gather.2.cloned.1.call-start = ((), (), s32[]{:S(2)}) async-start(), calls=%async_computation.1 | async-start | bytes 2359296 | tf_op jit(solution)/shard_map/all_gather | solution.py:274
  7.9 194.2 %reduce-scatter.2.cloned.1.call-start = ((), (), s32[]{:S(2)}) async-start(), calls=%async_computation.2 | async-start | bytes 2359296 | tf_op jit(solution)/shard_map/reduce_scatter | solution.py:358
  9.6 25.0 %collective-permute-start.1 = (f32[256,1024]{1,0:T(8,128)S(1)}, f32[256,1024]{1,0:T(8,128)S(1)}, u32[]{:S(2)}, u32[]{:S(2)}) collective-permute-start(f32[256,1024]{1,0:T(8,128)S(1)} %get-tuple-element.124), channel_id=1, source_target_pairs={{0,17},{16,1},{1,16},{17,0},{2,19},{18,3},{3,18},{19,2},{4,21},{20... | collective-permute-start | bytes 3145736 | tf_op jit(solution)/shard_map/ppermute | solution.py:89
  11.2 24.7 %collective-permute-start = (f32[256,1024]{1,0:T(8,128)S(1)}, f32[256,1024]{1,0:T(8,128)S(1)}, u32[]{:S(2)}, u32[]{:S(2)}) collective-permute-start(f32[256,1024]{1,0:T(8,128)S(1)} %get-tuple-element.125), channel_id=1, source_target_pairs={{0,16},{16,0},{1,17},{17,1},{2,18},{18,2},{3,19},{19,3},{4,20},{20... | collective-permute-start | bytes 3145736 | tf_op jit(solution)/shard_map/ppermute | solution.py:77
  54.1 13.0 %collective-permute-start.2 = (f32[512,1024]{1,0:T(8,128)}, f32[512,1024]{1,0:T(8,128)S(1)}, u32[]{:S(2)}, u32[]{:S(2)}) collective-permute-start(f32[512,1024]{1,0:T(8,128)} %all-gather.2.cloned.1.call-done.refs_3_), channel_id=1, source_target_pairs={{0,8},{8,0},{1,9},{9,1},{2,10},{10,2},{3,11},{11,3},{4,12},{12,4},... | collective-permute-start | bytes 6291464 | tf_op jit(solution)/shard_map/ppermute | solution.py:77
  80.1 2.0 collective-permute-start.7
  80.6 3.8 %collective-permute-start.3 = (f32[4,256]{1,0:T(4,128)}, f32[4,256]{1,0:T(4,128)S(1)}, u32[]{:S(2)}, u32[]{:S(2)}) collective-permute-start(f32[4,256]{1,0:T(4,128)} %get-tuple-element.74), channel_id=1, source_target_pairs={{0,2},{2,0},{4,6},{6,4},{1,3},{3,1},{5,7},{7,5},{8,10},{10,8},{12,... | collective-permute-start | bytes 12296 | tf_op jit(solution)/shard_map/ppermute | solution.py:77
  82.1 6.1 %collective-permute-start.8 = (f32[2,8,64]{2,1,0:T(8,128)S(1)}, f32[2,8,64]{2,1,0:T(8,128)S(1)}, u32[]{:S(2)}, u32[]{:S(2)}) collective-permute-start(f32[2,8,64]{2,1,0:T(8,128)S(1)} %log_add_fusion.3), channel_id=1, source_target_pairs={{0,32},{32,0},{64,96},{96,64},{128,160},{160,128},{192,224},{224,1... | collective-permute-start | bytes 12296 | tf_op jit(solution)/shard_map/ppermute | solution.py:77
  85.1 5.2 %collective-permute-start.4 = (f32[4,256]{1,0:T(4,128)S(1)}, f32[4,256]{1,0:T(4,128)S(1)}, u32[]{:S(2)}, u32[]{:S(2)}) collective-permute-start(f32[4,256]{1,0:T(4,128)S(1)} %log_add_fusion.7), channel_id=1, source_target_pairs={{0,4},{2,6},{4,0},{6,2},{1,5},{3,7},{5,1},{7,3},{8,12},{10,14},{12... | collective-permute-start | bytes 12296 | tf_op jit(solution)/shard_map/ppermute | solution.py:77
  88.2 4.6 %collective-permute-start.9 = (f32[2,8,64]{2,1,0:T(8,128)S(1)}, f32[2,8,64]{2,1,0:T(8,128)S(1)}, u32[]{:S(2)}, u32[]{:S(2)}) collective-permute-start(f32[2,8,64]{2,1,0:T(8,128)S(1)} %log_add_fusion.2), channel_id=1, source_target_pairs={{0,64},{32,96},{64,0},{96,32},{128,192},{160,224},{192,128},{224,1... | collective-permute-start | bytes 12296 | tf_op jit(solution)/shard_map/ppermute | solution.py:77
  90.3 5.4 %collective-permute-start.5 = (f32[4,256]{1,0:T(4,128)S(1)}, f32[4,256]{1,0:T(4,128)S(1)}, u32[]{:S(2)}, u32[]{:S(2)}) collective-permute-start(f32[4,256]{1,0:T(4,128)S(1)} %log_add_fusion.6), channel_id=1, source_target_pairs={{0,16},{16,0},{1,17},{17,1},{2,18},{18,2},{3,19},{19,3},{4,20},{20... | collective-permute-start | bytes 12296 | tf_op jit(solution)/shard_map/ppermute | solution.py:77
  92.8 7.6 %collective-permute-start.10 = (f32[2,8,64]{2,1,0:T(8,128)S(1)}, f32[2,8,64]{2,1,0:T(8,128)S(1)}, u32[]{:S(2)}, u32[]{:S(2)}) collective-permute-start(f32[2,8,64]{2,1,0:T(8,128)S(1)} %log_add_fusion.1), channel_id=1, source_target_pairs={{0,128},{32,160},{64,192},{96,224},{128,0},{160,32},{192,64},{224,... | collective-permute-start | bytes 12296 | tf_op jit(solution)/shard_map/ppermute | solution.py:77
  95.7 5.5 %collective-permute-start.6 = (f32[4,256]{1,0:T(4,128)S(1)}, f32[4,256]{1,0:T(4,128)S(1)}, u32[]{:S(2)}, u32[]{:S(2)}) collective-permute-start(f32[4,256]{1,0:T(4,128)S(1)} %log_add_fusion.5), channel_id=1, source_target_pairs={{0,1},{1,0},{2,3},{3,2},{4,5},{5,4},{6,7},{7,6},{8,9},{9,8},{10,11... | collective-permute-start | bytes 12296 | tf_op jit(solution)/shard_map/ppermute | solution.py:77
  110.4 30.0 %collective-permute-start.20 = (f32[256,1024]{1,0:T(8,128)}, f32[256,1024]{1,0:T(8,128)S(1)}, u32[]{:S(2)}, u32[]{:S(2)}) collective-permute-start(f32[256,1024]{1,0:T(8,128)} %get-tuple-element.106), channel_id=1, source_target_pairs={{0,17},{16,1},{1,16},{17,0},{2,19},{18,3},{3,18},{19,2},{4,21},{20... | collective-permute-start | bytes 3145736 | tf_op jit(solution)/shard_map/ppermute | solution.py:89
  111.9 28.4 %collective-permute-start.19 = (f32[256,1024]{1,0:T(8,128)}, f32[256,1024]{1,0:T(8,128)}, u32[]{:S(2)}, u32[]{:S(2)}) collective-permute-start(f32[256,1024]{1,0:T(8,128)} %get-tuple-element.80), channel_id=1, source_target_pairs={{0,16},{16,0},{1,17},{17,1},{2,18},{18,2},{3,19},{19,3},{4,20},{20... | collective-permute-start | bytes 3145736 | tf_op jit(solution)/shard_map/ppermute | solution.py:77
  128.5 1.7 collective-permute-start.11
  128.5 2.1 %collective-permute-start.12 = (f32[64,1024]{1,0:T(8,128)}, f32[64,1024]{1,0:T(8,128)S(1)}, u32[]{:S(2)}, u32[]{:S(2)}) collective-permute-start(f32[64,1024]{1,0:T(8,128)} %get-tuple-element.99), channel_id=1, source_target_pairs={{0,8},{8,0},{1,9},{9,1},{2,10},{10,2},{3,11},{11,3},{4,12},{12,4},... | collective-permute-start | bytes 786440 | tf_op jit(solution)/shard_map/ppermute | solution.py:77
  129.0 2.0 collective-permute-start.13
  130.2 1.7 collective-permute-start.14
  130.6 1.7 collective-permute-start.15
  131.0 7.8 %collective-permute-start.16 = (f32[64,1024]{1,0:T(8,128)}, f32[64,1024]{1,0:T(8,128)S(1)}, u32[]{:S(2)}, u32[]{:S(2)}) collective-permute-start(f32[64,1024]{1,0:T(8,128)} %get-tuple-element.103), channel_id=1, source_target_pairs={{0,8},{8,0},{1,9},{9,1},{2,10},{10,2},{3,11},{11,3},{4,12},{12,4},... | collective-permute-start | bytes 786440 | tf_op jit(solution)/shard_map/ppermute | solution.py:77
  131.9 6.8 %collective-permute-start.17 = (f32[64,1024]{1,0:T(8,128)}, f32[64,1024]{1,0:T(8,128)S(1)}, u32[]{:S(2)}, u32[]{:S(2)}) collective-permute-start(f32[64,1024]{1,0:T(8,128)} %get-tuple-element.104), channel_id=1, source_target_pairs={{0,8},{8,0},{1,9},{9,1},{2,10},{10,2},{3,11},{11,3},{4,12},{12,4},... | collective-permute-start | bytes 786440 | tf_op jit(solution)/shard_map/ppermute | solution.py:77
  132.3 6.5 %collective-permute-start.18 = (f32[64,1024]{1,0:T(8,128)}, f32[64,1024]{1,0:T(8,128)S(1)}, u32[]{:S(2)}, u32[]{:S(2)}) collective-permute-start(f32[64,1024]{1,0:T(8,128)} %get-tuple-element.105), channel_id=1, source_target_pairs={{0,8},{8,0},{1,9},{9,1},{2,10},{10,2},{3,11},{11,3},{4,12},{12,4},... | collective-permute-start | bytes 786440 | tf_op jit(solution)/shard_map/ppermute | solution.py:77
  142.0 18.3 %collective-permute-start.22 = (f32[128,640]{1,0:T(8,128)S(1)}, f32[128,640]{1,0:T(8,128)S(1)}, u32[]{:S(2)}, u32[]{:S(2)}) collective-permute-start(f32[128,640]{1,0:T(8,128)S(1)} %get-tuple-element.112), channel_id=1, source_target_pairs={{0,2},{2,4},{4,6},{6,0},{1,3},{3,5},{5,7},{7,1},{8,10},{10,12},{12... | collective-permute-start | bytes 983048 | tf_op jit(solution)/shard_map/ppermute | solution.py:361
  142.7 17.6 %collective-permute-start.23 = (f32[128,640]{1,0:T(8,128)S(1)}, f32[128,640]{1,0:T(8,128)S(1)}, u32[]{:S(2)}, u32[]{:S(2)}) collective-permute-start(f32[128,640]{1,0:T(8,128)S(1)} %get-tuple-element.113), channel_id=1, source_target_pairs={{0,6},{2,0},{4,2},{6,4},{1,7},{3,1},{5,3},{7,5},{8,14},{10,8},{12,... | collective-permute-start | bytes 983048 | tf_op jit(solution)/shard_map/ppermute | solution.py:361
  145.4 15.0 %collective-permute-start.24 = (f32[128,640]{1,0:T(8,128)S(1)}, f32[128,640]{1,0:T(8,128)S(1)}, u32[]{:S(2)}, u32[]{:S(2)}) collective-permute-start(f32[128,640]{1,0:T(8,128)S(1)} %get-tuple-element.114), channel_id=1, source_target_pairs={{0,4},{2,6},{4,0},{6,2},{1,5},{3,7},{5,1},{7,3},{8,12},{10,14},{12... | collective-permute-start | bytes 983048 | tf_op jit(solution)/shard_map/ppermute | solution.py:361
  145.5 14.9 %collective-permute-start.21 = (f32[256,384]{1,0:T(8,128)S(1)}, f32[256,384]{1,0:T(8,128)S(1)}, u32[]{:S(2)}, u32[]{:S(2)}) collective-permute-start(f32[256,384]{1,0:T(8,128)S(1)} %get-tuple-element.110), channel_id=1, source_target_pairs={{0,1},{1,0},{2,3},{3,2},{4,5},{5,4},{6,7},{7,6},{8,9},{9,8},{10,11... | collective-permute-start | bytes 1179656 | tf_op jit(solution)/shard_map/ppermute | solution.py:77
  161.0 5.9 %collective-permute-start.25 = (f32[64,384]{1,0:T(8,128)S(1)}, f32[64,384]{1,0:T(8,128)S(1)}, u32[]{:S(2)}, u32[]{:S(2)}) collective-permute-start(f32[64,384]{1,0:T(8,128)S(1)} %get-tuple-element.117), channel_id=1, source_target_pairs={{0,2},{2,4},{4,6},{6,0},{1,3},{3,5},{5,7},{7,1},{8,10},{10,12},{12... | collective-permute-start | bytes 294920 | tf_op jit(solution)/shard_map/ppermute | solution.py:361
  161.9 5.5 %collective-permute-start.26 = (f32[64,384]{1,0:T(8,128)S(1)}, f32[64,384]{1,0:T(8,128)S(1)}, u32[]{:S(2)}, u32[]{:S(2)}) collective-permute-start(f32[64,384]{1,0:T(8,128)S(1)} %get-tuple-element.118), channel_id=1, source_target_pairs={{0,6},{2,0},{4,2},{6,4},{1,7},{3,1},{5,3},{7,5},{8,14},{10,8},{12,... | collective-permute-start | bytes 294920 | tf_op jit(solution)/shard_map/ppermute | solution.py:361
  164.3 6.1 %collective-permute-start.27 = (f32[64,384]{1,0:T(8,128)S(1)}, f32[64,384]{1,0:T(8,128)S(1)}, u32[]{:S(2)}, u32[]{:S(2)}) collective-permute-start(f32[64,384]{1,0:T(8,128)S(1)} %get-tuple-element.119), channel_id=1, source_target_pairs={{0,4},{2,6},{4,0},{6,2},{1,5},{3,7},{5,1},{7,3},{8,12},{10,14},{12... | collective-permute-start | bytes 294920 | tf_op jit(solution)/shard_map/ppermute | solution.py:361
  165.5 9.9 %collective-permute-start.28 = (f32[128,640]{1,0:T(8,128)S(1)}, f32[128,640]{1,0:T(8,128)S(1)}, u32[]{:S(2)}, u32[]{:S(2)}) collective-permute-start(f32[128,640]{1,0:T(8,128)S(1)} %add_add_fusion), channel_id=1, source_target_pairs={{0,1},{1,0},{2,3},{3,2},{4,5},{5,4},{6,7},{7,6},{8,9},{9,8},{10,11... | collective-permute-start | bytes 983048 | tf_op jit(solution)/shard_map/ppermute | solution.py:77
  175.5 4.7 %collective-permute-start.34 = (f32[64,384]{1,0:T(8,128)S(1)}, f32[64,384]{1,0:T(8,128)S(1)}, u32[]{:S(2)}, u32[]{:S(2)}) collective-permute-start(f32[64,384]{1,0:T(8,128)S(1)} %add_add_fusion.1.refs_0_), channel_id=1, source_target_pairs={{0,6},{2,0},{4,2},{6,4},{1,7},{3,1},{5,3},{7,5},{8,14},{10,8},{12,... | collective-permute-start | bytes 294920 | tf_op jit(solution)/shard_map/ppermute | solution.py:364
  176.6 6.1 %collective-permute-start.33 = (f32[64,384]{1,0:T(8,128)S(1)}, f32[64,384]{1,0:T(8,128)S(1)}, u32[]{:S(2)}, u32[]{:S(2)}) collective-permute-start(f32[64,384]{1,0:T(8,128)S(1)} %add_add_fusion.1.refs_0_), channel_id=1, source_target_pairs={{0,4},{2,6},{4,0},{6,2},{1,5},{3,7},{5,1},{7,3},{8,12},{10,14},{12... | collective-permute-start | bytes 294920 | tf_op jit(solution)/shard_map/ppermute | solution.py:364
  178.7 5.8 %collective-permute-start.32 = (f32[64,384]{1,0:T(8,128)S(1)}, f32[64,384]{1,0:T(8,128)S(1)}, u32[]{:S(2)}, u32[]{:S(2)}) collective-permute-start(f32[64,384]{1,0:T(8,128)S(1)} %add_add_fusion.1.refs_0_), channel_id=1, source_target_pairs={{0,2},{2,4},{4,6},{6,0},{1,3},{3,5},{5,7},{7,1},{8,10},{10,12},{12... | collective-permute-start | bytes 294920 | tf_op jit(solution)/shard_map/ppermute | solution.py:364
  185.2 14.9 %collective-permute-start.35 = (f32[256,384]{1,0:T(8,128)S(1)}, f32[256,384]{1,0:T(8,128)S(1)}, u32[]{:S(2)}, u32[]{:S(2)}) collective-permute-start(f32[256,384]{1,0:T(8,128)S(1)} %gather.1.refs_4_), channel_id=1, source_target_pairs={{0,1},{1,0},{2,3},{3,2},{4,5},{5,4},{6,7},{7,6},{8,9},{9,8},{10,11... | collective-permute-start | bytes 1179656 | tf_op jit(solution)/shard_map/ppermute | solution.py:77
  185.5 8.8 %collective-permute-start.31 = (f32[128,640]{1,0:T(8,128)S(1)}, f32[128,640]{1,0:T(8,128)S(1)}, u32[]{:S(2)}, u32[]{:S(2)}) collective-permute-start(f32[128,640]{1,0:T(8,128)S(1)} %add.97.refs_0_), channel_id=1, source_target_pairs={{0,6},{2,0},{4,2},{6,4},{1,7},{3,1},{5,3},{7,5},{8,14},{10,8},{12,... | collective-permute-start | bytes 983048 | tf_op jit(solution)/shard_map/ppermute | solution.py:364
  185.8 10.9 %collective-permute-start.30 = (f32[128,640]{1,0:T(8,128)S(1)}, f32[128,640]{1,0:T(8,128)S(1)}, u32[]{:S(2)}, u32[]{:S(2)}) collective-permute-start(f32[128,640]{1,0:T(8,128)S(1)} %add.97.refs_0_), channel_id=1, source_target_pairs={{0,4},{2,6},{4,0},{6,2},{1,5},{3,7},{5,1},{7,3},{8,12},{10,14},{12... | collective-permute-start | bytes 983048 | tf_op jit(solution)/shard_map/ppermute | solution.py:364
  187.5 12.6 %collective-permute-start.29 = (f32[128,640]{1,0:T(8,128)S(1)}, f32[128,640]{1,0:T(8,128)S(1)}, u32[]{:S(2)}, u32[]{:S(2)}) collective-permute-start(f32[128,640]{1,0:T(8,128)S(1)} %add.97.refs_0_), channel_id=1, source_target_pairs={{0,2},{2,4},{4,6},{6,0},{1,3},{3,5},{5,7},{7,1},{8,10},{10,12},{12... | collective-permute-start | bytes 983048 | tf_op jit(solution)/shard_map/ppermute | solution.py:364
Sparse Core Ops, SparseCore 0:
  9.8 44.2 all-gather.1
  140.5 38.0 reduce-scatter.1
